TPU v7x, 32 devices: a whole 2x2x4 slice. The times are simulated.
32 devices in a mesh: dp: 16 (over z, y, x), mp: 2 (over core).
Axes of the slice: x: 2, y: 2, z: 4, core: 2. Of those that a mesh axis runs over, the one named last changes fastest.
Arguments:
- tokens: bfloat16 [32000, 768], P('dp'), may hold values from -6 to 6
- cotangent: bfloat16 [32000, 768], P('dp'), may hold values from -6 to 6
- buckets: int32 [128, 250, 250], P('dp'), may hold values from 0 to 32, as said below
- inward_master: float32 [768, 3, 768], P('dp', None, 'mp'), may hold values from -0.09375 to 0.09375
- inward_first: float32 [768, 3, 768], P('dp', None, 'mp'), may hold values from -4096 to 4096
- inward_second: float32 [768, 3, 768], P('dp', None, 'mp'), may hold values from 512000 to 2048000
- outward_master: float32 [768, 768], P(('mp', 'dp')), may hold values from -2 to 2
- outward_first: float32 [768, 768], P(('mp', 'dp')), may hold values from -128 to 128
- outward_second: float32 [768, 768], P(('mp', 'dp')), may hold values from 544 to 2176
- expand_master: float32 [768, 3072], P('dp', 'mp'), may hold values from -0.21875 to 0.21875
- expand_first: float32 [768, 3072], P('dp', 'mp'), may hold values from -320 to 320
- expand_second: float32 [768, 3072], P('dp', 'mp'), may hold values from 3520 to 14080
- reduce_master: float32 [3072, 768], P(('mp', 'dp')), may hold values from -0.109375 to 0.109375
- reduce_first: float32 [3072, 768], P(('mp', 'dp')), may hold values from -640 to 640
- reduce_second: float32 [3072, 768], P(('mp', 'dp')), may hold values from 13440 to 54400
- gains_master: float32 [2, 768], replicated, may hold values from 0.5 to 1.5
- gains_first: float32 [2, 768], replicated, may hold values from -1536 to 1536
- gains_second: float32 [2, 768], replicated, may hold values from 72000 to 288000
- table_master: float32 [32, 12], P(None, 'mp'), may hold values from -4 to 4
- table_first: float32 [32, 12], P(None, 'mp'), may hold values from -512 to 512
- table_second: float32 [32, 12], P(None, 'mp'), may hold values from 8000 to 32000
Outputs:
- layer_out: bfloat16 [32000, 768], P('dp')
- input_grad: float32 [32000, 768], P('dp')
- inward_new: float32 [768, 3, 768], P('dp', None, 'mp')
- inward_first_new: float32 [768, 3, 768], P('dp', None, 'mp')
- inward_second_new: float32 [768, 3, 768], P('dp', None, 'mp')
- inward_copy: bfloat16 [768, 3, 768], P('dp', None, 'mp')
- outward_new: float32 [768, 768], P(('mp', 'dp'))
- outward_first_new: float32 [768, 768], P(('mp', 'dp'))
- outward_second_new: float32 [768, 768], P(('mp', 'dp'))
- outward_copy: bfloat16 [768, 768], P(('mp', 'dp'))
- expand_new: float32 [768, 3072], P('dp', 'mp')
- expand_first_new: float32 [768, 3072], P('dp', 'mp')
- expand_second_new: float32 [768, 3072], P('dp', 'mp')
- expand_copy: bfloat16 [768, 3072], P('dp', 'mp')
- reduce_new: float32 [3072, 768], P(('mp', 'dp'))
- reduce_first_new: float32 [3072, 768], P(('mp', 'dp'))
- reduce_second_new: float32 [3072, 768], P(('mp', 'dp'))
- reduce_copy: bfloat16 [3072, 768], P(('mp', 'dp'))
- gains_new: float32 [2, 768], replicated
- gains_first_new: float32 [2, 768], replicated
- gains_second_new: float32 [2, 768], replicated
- table_new: float32 [32, 12], P(None, 'mp')
- table_first_new: float32 [32, 12], P(None, 'mp')
- table_second_new: float32 [32, 12], P(None, 'mp')
Inputs may be any that keep to these rules, and one draw needn't show every extreme that they name: Entry [p, i, j] is the bidirectional T5 bucket of the distance from query i to key j of passage p (32 buckets, distances up to 128), or 32 where key j lies in passage p's padding; a passage's valid keys come first and number at least 125.
All inputs are finite; a program needn't handle non-finite values.
Results may differ from a plain program's by a relative error of at most 0.014.
The roundings to bfloat16 on the way count: a program that leaves them out, or rounds other values in their place, can miss the bound.
Values may be sent and summed in bfloat16 or wider, within the bound.
A program may use at most 192 MiB of HBM per device.

v0:
```python
from functools import partial
import math

import jax
import jax.numpy as jnp
from jax import lax
from jax.sharding import PartitionSpec as P

DH = 64
PLEN = 250
STEP = 5


norm_eps = 1e-06
masked_score = -1000000000.0
beta_first = 0.5
beta_second = 0.5
adam_eps = 1e-08
decay_rate = 0.01
rate_inward = 0.015
rate_outward = 0.3
rate_expand = 0.04
rate_reduce = 0.02
rate_gains = 0.5
rate_table = 0.5


def rms_apply(values, gain_row):
    inv_rms = lax.rsqrt(jnp.mean(values * values, axis=-1, keepdims=True) + norm_eps)
    return values * inv_rms * gain_row


def adamw(weight, first_moment, second, gradient, step_rate):
    new_first = beta_first * first_moment + (1.0 - beta_first) * gradient
    new_second = beta_second * second + (1.0 - beta_second) * gradient * gradient
    first_hat = new_first / (1.0 - beta_first**STEP)
    second_hat = new_second / (1.0 - beta_second**STEP)
    new_weight = weight - step_rate * (
        first_hat / (jnp.sqrt(second_hat) + adam_eps) + decay_rate * weight
    )
    return (new_weight, new_first, new_second)


def scores_of(queries, key_rows, bucket_rows, bias_table):
    onehot = (bucket_rows[..., None] == jnp.arange(bias_table.shape[0], dtype=jnp.int32)).astype(
        jnp.float32
    )
    bias_scores = jnp.einsum("pqkb,bh->phqk", onehot, bias_table, precision=lax.Precision.HIGHEST)
    raw_scores = (
        jnp.einsum("pqhd,pkhd->phqk", queries, key_rows, preferred_element_type=jnp.float32)
        + bias_scores
    )
    valid_keys = (bucket_rows < bias_table.shape[0])[:, None]
    return jnp.where(valid_keys, raw_scores, masked_score)


def attend_block(bias_table, block_items):
    queries, key_rows, value_rows, bucket_rows = block_items
    scores = scores_of(queries, key_rows, bucket_rows, bias_table)
    row_max = jnp.max(scores, axis=-1, keepdims=True)
    exponents = jnp.exp(scores - row_max)
    row_sum = jnp.sum(exponents, axis=-1, keepdims=True)
    attention = (exponents / row_sum).astype(jnp.bfloat16)
    context = jnp.einsum(
        "phqk,pkhd->pqhd", attention, value_rows, preferred_element_type=jnp.float32
    )
    return (context.astype(jnp.bfloat16), (row_max + jnp.log(row_sum))[..., 0])


def attend_back(bias_table, block_items):
    queries, key_rows, value_rows, bucket_rows, context_grad, log_sums = block_items
    scores = scores_of(queries, key_rows, bucket_rows, bias_table)
    probs_full = jnp.exp(scores - log_sums[..., None])
    attention = probs_full.astype(jnp.bfloat16)
    value_grad = jnp.einsum(
        "phqk,pqhd->pkhd", attention, context_grad, preferred_element_type=jnp.float32
    )
    prob_grad = jnp.einsum(
        "pqhd,pkhd->phqk", context_grad, value_rows, preferred_element_type=jnp.float32
    )
    centred = jnp.sum(probs_full * prob_grad, axis=-1, keepdims=True)
    score_grad = (probs_full * (prob_grad - centred)).astype(jnp.bfloat16)
    query_grad = jnp.einsum(
        "phqk,pkhd->pqhd", score_grad, key_rows, preferred_element_type=jnp.float32
    )
    key_grad = jnp.einsum(
        "phqk,pqhd->pkhd", score_grad, queries, preferred_element_type=jnp.float32
    )
    onehot = (bucket_rows[..., None] == jnp.arange(bias_table.shape[0], dtype=jnp.int32)).astype(
        jnp.bfloat16
    )
    table_grad = jnp.einsum("phqk,pqkb->bh", score_grad, onehot, preferred_element_type=jnp.float32)
    return (
        query_grad.astype(jnp.bfloat16),
        key_grad.astype(jnp.bfloat16),
        value_grad.astype(jnp.bfloat16),
        table_grad,
    )


def shards(
    tokens,
    cotangent,
    buckets,
    inward_master,
    inward_first,
    inward_second,
    outward_master,
    outward_first,
    outward_second,
    expand_master,
    expand_first,
    expand_second,
    reduce_master,
    reduce_first,
    reduce_second,
    gains_master,
    gains_first,
    gains_second,
    table_master,
    table_first,
    table_second,
):
    inward_weight, outward_weight, expand_weight, reduce_weight = (
        lax.all_gather(inward_master.astype(jnp.bfloat16), "dp", axis=0, tiled=True),
        lax.all_gather(outward_master.astype(jnp.bfloat16), "dp", axis=0, tiled=True),
        lax.all_gather(expand_master.astype(jnp.bfloat16), "dp", axis=0, tiled=True),
        lax.all_gather(reduce_master.astype(jnp.bfloat16), "dp", axis=0, tiled=True),
    )
    row_count = tokens.shape[0]
    passages = row_count // PLEN
    per_block = math.gcd(passages, 2)
    block_count = passages // per_block
    heads = inward_weight.shape[2] // DH
    inputs = tokens.astype(jnp.float32)
    normed = rms_apply(inputs, gains_master[0]).astype(jnp.bfloat16)
    projected = jnp.einsum(
        "td,dch->tch", normed, inward_weight, preferred_element_type=jnp.float32
    ).astype(jnp.bfloat16)
    stacked = projected.reshape(block_count, per_block, PLEN, 3, heads, DH)
    queries = stacked[:, :, :, 0]
    key_rows = stacked[:, :, :, 1]
    value_rows = stacked[:, :, :, 2]
    bucket_blocks = buckets.reshape(block_count, per_block, PLEN, PLEN)
    context, log_sums = lax.map(
        partial(attend_block, table_master), (queries, key_rows, value_rows, bucket_blocks)
    )
    context = context.reshape(row_count, heads * DH)
    attended_terms = jnp.dot(context, outward_weight, preferred_element_type=jnp.float32)
    attended = lax.psum(attended_terms, "mp")
    hidden = inputs + attended
    normed_two = rms_apply(hidden, gains_master[1]).astype(jnp.bfloat16)
    expanded = jnp.dot(normed_two, expand_weight, preferred_element_type=jnp.float32)
    activated = jax.nn.gelu(expanded).astype(jnp.bfloat16)
    reduced_terms = jnp.dot(activated, reduce_weight, preferred_element_type=jnp.float32)
    reduced = lax.psum(reduced_terms.astype(jnp.bfloat16), "mp").astype(jnp.float32)
    layer_out = (hidden + reduced).astype(jnp.bfloat16)
    cotangent_wide = cotangent.astype(jnp.float32)
    reduce_grad = jnp.einsum("tf,td->fd", activated, cotangent, preferred_element_type=jnp.float32)
    gelu_in = jnp.einsum("td,fd->tf", cotangent, reduce_weight, preferred_element_type=jnp.float32)
    _, gelu_back = jax.vjp(jax.nn.gelu, expanded)
    expanded_grad = gelu_back(gelu_in)[0].astype(jnp.bfloat16)
    expand_grad = jnp.einsum(
        "td,tf->df", normed_two, expanded_grad, preferred_element_type=jnp.float32
    )
    normed_two_terms = jnp.einsum(
        "tf,df->td", expanded_grad, expand_weight, preferred_element_type=jnp.float32
    )
    normed_two_grad = lax.psum(normed_two_terms, "mp")
    _, second_norm_back = jax.vjp(rms_apply, hidden, gains_master[1])
    hidden_part, gain_two_grad = second_norm_back(normed_two_grad)
    hidden_grad = cotangent_wide + hidden_part
    attended_grad = hidden_grad.astype(jnp.bfloat16)
    outward_grad = jnp.einsum(
        "th,td->hd", context, attended_grad, preferred_element_type=jnp.float32
    )
    context_grad = jnp.einsum(
        "td,hd->th", attended_grad, outward_weight, preferred_element_type=jnp.float32
    ).astype(jnp.bfloat16)
    context_grad = context_grad.reshape(block_count, per_block, PLEN, heads, DH)
    query_grad, key_grad, value_grad, table_parts = lax.map(
        partial(attend_back, table_master),
        (queries, key_rows, value_rows, bucket_blocks, context_grad, log_sums),
    )
    table_grad = jnp.sum(table_parts, axis=0)
    projected_grad = jnp.stack([query_grad, key_grad, value_grad], axis=3).reshape(
        row_count, 3, heads * DH
    )
    inward_grad = jnp.einsum(
        "td,tch->dch", normed, projected_grad, preferred_element_type=jnp.float32
    )
    inward_sum, outward_sum, expand_sum, reduce_sum = (
        lax.psum_scatter(inward_grad, "dp", scatter_dimension=0, tiled=True),
        lax.psum_scatter(outward_grad, "dp", scatter_dimension=0, tiled=True),
        lax.psum_scatter(expand_grad, "dp", scatter_dimension=0, tiled=True),
        lax.psum_scatter(reduce_grad, "dp", scatter_dimension=0, tiled=True),
    )
    normed_terms = jnp.einsum(
        "tch,dch->td", projected_grad, inward_weight, preferred_element_type=jnp.float32
    )
    normed_grad = lax.psum(normed_terms, "mp")
    _, first_norm_back = jax.vjp(rms_apply, inputs, gains_master[0])
    input_part, gain_one_grad = first_norm_back(normed_grad)
    input_grad = hidden_grad + input_part
    gains_sum, table_sum = lax.psum((jnp.stack([gain_one_grad, gain_two_grad]), table_grad), "dp")
    inward_new, inward_first_new, inward_second_new = adamw(
        inward_master, inward_first, inward_second, inward_sum, rate_inward
    )
    outward_new, outward_first_new, outward_second_new = adamw(
        outward_master, outward_first, outward_second, outward_sum, rate_outward
    )
    expand_new, expand_first_new, expand_second_new = adamw(
        expand_master, expand_first, expand_second, expand_sum, rate_expand
    )
    reduce_new, reduce_first_new, reduce_second_new = adamw(
        reduce_master, reduce_first, reduce_second, reduce_sum, rate_reduce
    )
    gains_new, gains_first_new, gains_second_new = adamw(
        gains_master, gains_first, gains_second, gains_sum, rate_gains
    )
    table_new, table_first_new, table_second_new = adamw(
        table_master, table_first, table_second, table_sum, rate_table
    )
    return (
        layer_out,
        input_grad,
        inward_new,
        inward_first_new,
        inward_second_new,
        inward_new.astype(jnp.bfloat16),
        outward_new,
        outward_first_new,
        outward_second_new,
        outward_new.astype(jnp.bfloat16),
        expand_new,
        expand_first_new,
        expand_second_new,
        expand_new.astype(jnp.bfloat16),
        reduce_new,
        reduce_first_new,
        reduce_second_new,
        reduce_new.astype(jnp.bfloat16),
        gains_new,
        gains_first_new,
        gains_second_new,
        table_new,
        table_first_new,
        table_second_new,
    )


def solution(mesh):
    return jax.shard_map(
        shards,
        mesh=mesh,
        in_specs=(
            P("dp", None),
            P("dp", None),
            P("dp", None, None),
            P("dp", None, "mp"),
            P("dp", None, "mp"),
            P("dp", None, "mp"),
            P(("mp", "dp"), None),
            P(("mp", "dp"), None),
            P(("mp", "dp"), None),
            P("dp", "mp"),
            P("dp", "mp"),
            P("dp", "mp"),
            P(("mp", "dp"), None),
            P(("mp", "dp"), None),
            P(("mp", "dp"), None),
            P(),
            P(),
            P(),
            P(None, "mp"),
            P(None, "mp"),
            P(None, "mp"),
        ),
        out_specs=(
            P("dp", None),
            P("dp", None),
            P("dp", None, "mp"),
            P("dp", None, "mp"),
            P("dp", None, "mp"),
            P("dp", None, "mp"),
            P(("mp", "dp"), None),
            P(("mp", "dp"), None),
            P(("mp", "dp"), None),
            P(("mp", "dp"), None),
            P("dp", "mp"),
            P("dp", "mp"),
            P("dp", "mp"),
            P("dp", "mp"),
            P(("mp", "dp"), None),
            P(("mp", "dp"), None),
            P(("mp", "dp"), None),
            P(("mp", "dp"), None),
            P(),
            P(),
            P(),
            P(None, "mp"),
            P(None, "mp"),
            P(None, "mp"),
        ),
        check_vma=False,
    )
```

profile of v0, /device:TPU:0, one launch (start us, length us, event | category | flops | bytes accessed | tf_op | source)
XLA Modules:
  0.0 1065.1 jit_solution(17359217566876784116)
XLA Ops:
  12.9 49.1 %all_gather.13 = bf16[384,768]{1,0:T(8,128)(2,1)} all-gather(bf16[24,768]{1,0:T(8,128)(2,1)S(1)} %convert_element_type.100), channel_id=1, replica_groups=mesh['dp'=16,'mp'=2] {'dp'}, dimensions={0}, use_global_device_ids=true | all-gather | bytes 626688 | tf_op jit(solution)/shard_map/all_gather | solution.py:126
  61.9 12.5 %all-gather.4.cloned.1.call-done = bf16[768,3,384]{2,0,1:T(8,128)(2,1)} async-done(((bf16[48,3,384]{2,0,1:T(8,128)(2,1)}), bf16[768,3,384]{2,0,1:T(8,128)(2,1)}) %all-gather.4.cloned.1.call-update) | async-done | bytes 1769488 | tf_op jit(solution)/shard_map/all_gather | solution.py:125
  74.4 7.7 convolution_convert_fusion.2
  82.1 6.6 copy.73
  88.7 11.6 %reshape.149 = bf16[4,2,250,3,6,64]{2,1,0,5,4,3:T(2,128)(2,1)} reshape(bf16[2000,3,384]{0,2,1:T(8,128)(2,1)} %copy.73) | data formatting | bytes 9216000 | tf_op jit(solution)/shard_map/reshape | solution.py:140
  111.7 65.8 %while.28 = (s32[]{:T(128)}, bf16[4,2,250,6,64]{2,1,0,4,3:T(2,128)(2,1)}, f32[4,2,6,250]{3,2,1,0:T(8,128)S(1)}, bf16[4,2,250,6,64]{2,4,3,1,0:T(8,128)(2,1)}, s32...) while((s32[]{:T(128)}, ...), condition=%wide.region_4.5_spmd, body=%wide.region_1.4_spmd.sunk | while | flops 490313984 | bytes 26202932 | solution.py:145
  113.0 6.4 fusion.144
  129.5 6.4 fusion.144
  145.9 6.4 fusion.144
  162.4 6.4 fusion.144
  187.2 29.0 %all-reduce.6.cloned.1.call-done = f32[2000,768]{1,0:T(8,128)} async-done(((f32[2000,768]{1,0:T(8,128)}), f32[2000,768]{1,0:T(8,128)}) %all-reduce.6.cloned.1.call-update) | async-done | bytes 6144016 | tf_op jit(solution)/shard_map/psum | solution.py:150
  216.2 6.2 multiply_reduce_fusion.3
  222.4 61.1 %all-gather.6.cloned.1.call-done = bf16[768,1536]{1,0:T(8,128)(2,1)} async-done(((bf16[48,1536]{1,0:T(8,128)(2,1)}), bf16[768,1536]{1,0:T(8,128)(2,1)}) %all-gather.6.cloned.1.call-update) | async-done | bytes 2359312 | tf_op jit(solution)/shard_map/all_gather | solution.py:127
  283.5 12.4 %multiply_convert_fusion.1 = (bf16[2000,1536]{1,0:T(8,128)(2,1)S(1)}, f32[2000,1536]{1,0:T(8,128)}) fusion(bf16[768,1536]{1,0:T(8,128)(2,1)} %all-gather.6.cloned.1.call-done, f32[2000,768]{1,0:T(8,128)} %get-tuple-element.245, f32[768]{0:T(1024)S(1)} %get-tuple-element.174, f32[2000]{0:T(1024)S(1)} %fusion.82), kind=kOutput, calls=%fused_computation.78 | convolution fusion | flops 4750848000 | bytes 26946368 | tf_op jit(solution)/shard_map/dot_general | solution.py:153
  298.5 6.9 fusion.102
  305.4 136.5 %reduce-scatter.11.cloned.1.call-done = f32[96,768]{1,0:T(8,128)} async-done(((f32[1536,768]{1,0:T(8,128)}), f32[96,768]{1,0:T(8,128)}) %reduce-scatter.11.cloned.1.call-update) | async-done | bytes 294928 | tf_op jit(solution)/shard_map/reduce_scatter | solution.py:196
  444.3 62.2 %all-gather.8.cloned.1.call-done = bf16[1536,768]{1,0:T(8,128)(2,1)} async-done(((bf16[96,768]{1,0:T(8,128)(2,1)}), bf16[1536,768]{1,0:T(8,128)(2,1)}) %all-gather.8.cloned.1.call-update) | async-done | bytes 2359312 | tf_op jit(solution)/shard_map/all_gather | solution.py:128
  506.5 25.5 %fusion.61 = bf16[2000,1536]{1,0:T(8,128)(2,1)S(1)} fusion(f32[2000,1536]{1,0:T(8,128)} %get-tuple-element.259, bf16[2000,768]{1,0:T(8,128)(2,1)S(1)} %copy-done.12, bf16[1536,768]{1,0:T(8,128)(2,1)} %all-gather.8.cloned.1.call-done), kind=kOutput, calls=%fused_computation.77 | convolution fusion | flops 4780032000 | bytes 23863296 | tf_op jit(solution)/shard_map/td,fd->tf/dot_general | solution.py:160
  534.6 6.9 fusion.101
  543.1 9.0 convolution_convert_fusion.3
  552.2 20.0 %all-reduce.10.cloned.1.call-done = f32[2000,768]{1,0:T(8,128)} async-done(((f32[2000,768]{1,0:T(8,128)}), f32[2000,768]{1,0:T(8,128)}) %all-reduce.10.cloned.1.call-update) | async-done | bytes 6144016 | tf_op jit(solution)/shard_map/psum | solution.py:169
  577.6 21.9 %all-reduce.8.cloned.1.call-done = bf16[2000,768]{1,0:T(8,128)(2,1)} async-done(((bf16[2000,768]{1,0:T(8,128)(2,1)}), bf16[2000,768]{1,0:T(8,128)(2,1)}) %all-reduce.8.cloned.1.call-update) | async-done | bytes 3072016 | tf_op jit(solution)/shard_map/psum | solution.py:156
  599.6 9.0 fusion.66
  613.8 10.8 %fusion.87 = f32[768,1536]{1,0:T(8,128)} fusion(bf16[2000,1536]{1,0:T(8,128)(2,1)} %copy-done.36, f32[2000,768]{1,0:T(8,128)} %get-tuple-element.245, f32[768]{0:T(1024)S(1)} %get-tuple-element.174, f32[2000]{0:T(1024)S(1)} %fusion.82), kind=kOutput, calls=%fused_computation.147 | convolution fusion | flops 4723200000 | bytes 17017664 | tf_op jit(solution)/shard_map/td,tf->df/dot_general | solution.py:163
  641.3 79.3 %while.29 = (s32[]{:T(128)}, bf16[4,2,250,6,64]{2,1,0,4,3:T(2,128)(2,1)}, bf16[4,2,250,6,64]{2,1,0,4,3:T(2,128)(2,1)}, bf16[4,2,250,6,64]{2,1,0,4,3:T(2,128)(2,1...) while((s32[]{:T(128)}, ...), condition=%wide.region_12.13_spmd, body=%wide.region_10.12_spmd.sunk | while | flops 831448000 | bytes 41786076 | solution.py:181
  735.8 9.3 convolution_bitcast_fusion
  747.0 8.5 fusion.71
  758.1 123.7 %reduce-scatter.9.cloned.1.call-done = f32[48,1536]{1,0:T(8,128)} async-done(((f32[768,1536]{1,0:T(8,128)}), f32[48,1536]{1,0:T(8,128)}) %reduce-scatter.9.cloned.1.call-update) | async-done | bytes 294928 | tf_op jit(solution)/shard_map/reduce_scatter | solution.py:195
  884.0 31.6 %all-reduce.12.cloned.1.call-done = f32[2000,768]{1,0:T(8,128)} async-done(((f32[2000,768]{1,0:T(8,128)}), f32[2000,768]{1,0:T(8,128)}) %all-reduce.12.cloned.1.call-update) | async-done | bytes 6144016 | tf_op jit(solution)/shard_map/psum | solution.py:201
  919.9 77.5 %all-reduce = (f32[2,768]{1,0:T(2,128)S(1)}, f32[32,6]{0,1:T(8,128)S(1)}) all-reduce(f32[2,768]{1,0:T(2,128)S(1)} %pad_maximum_fusion.3, f32[32,6]{0,1:T(8,128)S(1)} %reduce_sum.92), channel_id=1, replica_groups=mesh['dp'=16,'mp'=2] {'dp'}, use_global_device_ids=true, to_apply=%region_21.22 | all-reduce | flops 1728 | bytes 13824 | tf_op jit(solution)/shard_map/psum | solution.py:205
  998.8 7.2 fusion.67
  1005.9 50.4 %reduce-scatter.5.cloned.1.call-done = f32[48,3,384]{2,0,1:T(8,128)} async-done(((f32[768,3,384]{2,0,1:T(8,128)}), f32[48,3,384]{2,0,1:T(8,128)}) %reduce-scatter.5.cloned.1.call-update) | async-done | bytes 221200 | tf_op jit(solution)/shard_map/reduce_scatter | solution.py:193
  (231 shorter events, 210.8 us)
Async XLA Ops:
  7.2 67.2 %all-gather.4.cloned.1.call-start = ((), (), s32[]{:S(2)}) async-start(), calls=%async_computation.4 | async-start | bytes 1880064 | tf_op jit(solution)/shard_map/all_gather | solution.py:125
  9.0 207.2 %all-reduce.6.cloned.1.call-start = ((), (), s32[]{:S(2)}) async-start(), calls=%async_computation.5 | async-start | bytes 12288000 | tf_op jit(solution)/shard_map/psum | solution.py:150
  12.1 70.0 %copy-start.26 = (f32[768]{0:T(1024)}, f32[768]{0:T(1024)S(1)}, u32[]{:S(2)}) copy-start(f32[768]{0:T(1024)S(1)} %get-tuple-element.175) | copy-start | bytes 9220
  12.8 69.3 %copy-start.24 = (f32[2000]{0:T(1024)}, f32[2000]{0:T(1024)S(1)}, u32[]{:S(2)}) copy-start(f32[2000]{0:T(1024)S(1)} %fusion.68) | copy-start | bytes 24004
  12.9 69.3 %copy-start.22 = (f32[2000]{0:T(1024)}, f32[2000]{0:T(1024)S(1)}, u32[]{:S(2)}) copy-start(f32[2000]{0:T(1024)S(1)} %fusion.81) | copy-start | bytes 24004
  185.5 30.7 %copy-start.2 = (bf16[2000,768]{1,0:T(8,128)(2,1)S(1)}, bf16[2000,768]{1,0:T(8,128)(2,1)}, u32[]{:S(2)}) copy-start(bf16[2000,768]{1,0:T(8,128)(2,1)} %param.25) | copy-start | bytes 9216004
  185.5 98.0 %all-gather.6.cloned.1.call-start = ((), (), s32[]{:S(2)}) async-start(), calls=%async_computation.6 | async-start | bytes 2506752 | tf_op jit(solution)/shard_map/all_gather | solution.py:127
  187.2 254.7 %reduce-scatter.11.cloned.1.call-start = ((), (), s32[]{:S(2)}) async-start(), calls=%async_computation.14 | async-start | bytes 5013504 | tf_op jit(solution)/shard_map/reduce_scatter | solution.py:196
  283.5 15.0 %copy-start.12 = (bf16[2000,768]{1,0:T(8,128)(2,1)S(1)}, bf16[2000,768]{1,0:T(8,128)(2,1)}, u32[]{:S(2)}) copy-start(bf16[2000,768]{1,0:T(8,128)(2,1)} %param.26) | copy-start | bytes 9216004
  305.3 136.6 %copy-start.17 = (f32[96,768]{1,0:T(8,128)S(1)}, f32[96,768]{1,0:T(8,128)}, u32[]{:S(2)}) copy-start(f32[96,768]{1,0:T(8,128)} %param.37) | copy-start | bytes 884740
  305.3 201.1 %all-gather.8.cloned.1.call-start = ((), (), s32[]{:S(2)}) async-start(), calls=%async_computation.7 | async-start | bytes 2506752 | tf_op jit(solution)/shard_map/all_gather | solution.py:128
  444.2 128.0 %all-reduce.10.cloned.1.call-start = ((), (), s32[]{:S(2)}) async-start(), calls=%async_computation.9 | async-start | bytes 12288000 | tf_op jit(solution)/shard_map/psum | solution.py:169
  506.5 28.1 %copy-start.34 = (bf16[768,1536]{1,0:T(8,128)(2,1)S(1)}, bf16[768,1536]{1,0:T(8,128)(2,1)}, u32[]{:S(2)}) copy-start(bf16[768,1536]{1,0:T(8,128)(2,1)} %all-gather.6.cloned.1.call-done) | copy-start | bytes 7077892
  541.5 58.1 %all-reduce.8.cloned.1.call-start = ((), (), s32[]{:S(2)}) async-start(), calls=%async_computation.8 | async-start | bytes 6144000 | tf_op jit(solution)/shard_map/psum | solution.py:156
  552.2 203.4 %reduce-scatter.7.cloned.1.call-start = ((), (), s32[]{:S(2)}) async-start(), calls=%async_computation.12 | async-start | bytes 1253376 | tf_op jit(solution)/shard_map/reduce_scatter | solution.py:194
  577.6 33.6 %copy-start.7 = (bf16[2000,384]{0,1:T(8,128)(2,1)S(1)}, bf16[2000,384]{0,1:T(8,128)(2,1)}, u32[]{:S(2)}) copy-start(bf16[2000,384]{0,1:T(8,128)(2,1)} %copy-done.6) | copy-start | bytes 4608004
  613.7 268.0 %reduce-scatter.9.cloned.1.call-start = ((), (), s32[]{:S(2)}) async-start(), calls=%async_computation.13 | async-start | bytes 5013504 | tf_op jit(solution)/shard_map/reduce_scatter | solution.py:195
  624.6 291.1 %all-reduce.12.cloned.1.call-start = ((), (), s32[]{:S(2)}) async-start(), calls=%async_computation.10 | async-start | bytes 12288000 | tf_op jit(solution)/shard_map/psum | solution.py:201
  635.4 6.0 copy-start.4
  635.4 6.0 copy-start.5
  720.6 5.0 copy-start.8
  725.6 5.5 copy-start.9
  745.1 311.2 %reduce-scatter.5.cloned.1.call-start = ((), (), s32[]{:S(2)}) async-start(), calls=%async_computation.11 | async-start | bytes 3760128 | tf_op jit(solution)/shard_map/reduce_scatter | solution.py:193
  755.5 126.2 %copy-start.15 = (f32[48,1536]{1,0:T(8,128)S(1)}, f32[48,1536]{1,0:T(8,128)}, u32[]{:S(2)}) copy-start(f32[48,1536]{1,0:T(8,128)} %param.34) | copy-start | bytes 884740
  884.0 113.5 %copy-start.25 = (f32[2000]{0:T(1024)S(1)}, f32[2000]{0:T(1024)}, u32[]{:S(2)}) copy-start(f32[2000]{0:T(1024)} %copy-done.24) | copy-start | bytes 24004
  884.0 113.5 %copy-start.32 = (f32[32,6]{0,1:T(8,128)S(1)}, f32[32,6]{0,1:T(8,128)}, u32[]{:S(2)}) copy-start(f32[32,6]{0,1:T(8,128)} %param.44) | copy-start | bytes 2308
  884.0 113.5 %copy-start.33 = (f32[32,6]{0,1:T(8,128)S(1)}, f32[32,6]{0,1:T(8,128)}, u32[]{:S(2)}) copy-start(f32[32,6]{0,1:T(8,128)} %param.45) | copy-start | bytes 2308
  884.0 114.2 %copy-start.29 = (f32[2,768]{1,0:T(2,128)S(1)}, f32[2,768]{1,0:T(2,128)}, u32[]{:S(2)}) copy-start(f32[2,768]{1,0:T(2,128)} %param.40) | copy-start | bytes 18436
  884.0 114.1 %copy-start.30 = (f32[2,768]{1,0:T(2,128)S(1)}, f32[2,768]{1,0:T(2,128)}, u32[]{:S(2)}) copy-start(f32[2,768]{1,0:T(2,128)} %param.41) | copy-start | bytes 18436
  884.0 114.1 %copy-start.31 = (f32[2,768]{1,0:T(2,128)S(1)}, f32[2,768]{1,0:T(2,128)}, u32[]{:S(2)}) copy-start(f32[2,768]{1,0:T(2,128)} %param.42) | copy-start | bytes 18436
  998.7 57.6 %copy-start.16 = (f32[48,3,384]{2,0,1:T(8,128)S(1)}, f32[48,3,384]{2,0,1:T(8,128)}, u32[]{:S(2)}) copy-start(f32[48,3,384]{2,0,1:T(8,128)} %param.28) | copy-start | bytes 663556
  998.8 57.6 %copy-start.20 = (f32[48,3,384]{2,0,1:T(8,128)S(1)}, f32[48,3,384]{2,0,1:T(8,128)}, u32[]{:S(2)}) copy-start(f32[48,3,384]{2,0,1:T(8,128)} %param.29) | copy-start | bytes 663556
  (17 other events, 45.4 us)
Sparse Core Ops, SparseCore 0:
  11.3 63.0 all-gather.3
  185.7 30.5 all-reduce.5
  220.0 63.4 all-gather.5
  305.5 136.3 reduce-scatter.10
  445.1 61.3 all-gather.7
  541.6 30.5 all-reduce.9
  575.3 24.2 all-reduce.7
  613.8 125.6 reduce-scatter.6
  744.7 136.9 reduce-scatter.8
  884.8 30.7 all-reduce.11
  920.7 135.5 reduce-scatter.4
where the time goes:
time: 1070 us
  waiting for transfers between devices  549 us (51%)
  matrix products  201 us (19%)
  blocking collectives  127 us (12%)
  local copies, waits for them, and re-layouts  114 us (11%)
  other arithmetic  58.4 us (5%)
  between operations  14.5 us (1%)
    reduce_scatter x1, waiting for transfers between devices, shards(): lax.psum_scatter(reduce_grad, 'dp', scatter_dimension=0, tiled=True)  136 us
    reduce_scatter x1, waiting for transfers between devices, shards(): lax.psum_scatter(expand_grad, 'dp', scatter_dimension=0, tiled=True)  124 us
    psum x1, blocking collectives, shards(): lax.psum((jnp.stack([gain_one_grad, gain_two_grad]), table_grad), 'dp')  77.5 us
    all_gather x1, waiting for transfers between devices, shards(): lax.all_gather(reduce_master.astype(jnp.bfloat16), 'dp', axis=0, tiled=True)  62.2 us
    all_gather x1, waiting for transfers between devices, shards(): lax.all_gather(expand_master.astype(jnp.bfloat16), 'dp', axis=0, tiled=True)  61.1 us
    reduce_scatter x1, waiting for transfers between devices, shards(): lax.psum_scatter(inward_grad, 'dp', scatter_dimension=0, tiled=True)  50.4 us
    all_gather x1, blocking collectives, shards(): lax.all_gather(outward_master.astype(jnp.bfloat16), 'dp', axis=0, tiled=T...  49.1 us
    dot_general x8, matrix products, scores_of(): jnp.einsum('pqkb,bh->phqk', onehot, bias_table, precision=lax.Precision.H...  45.6 us
  transfers between devices with their start and end apart: 11, of which 10 were waited for; matrix products, arithmetic and copies ran while one was open for 17% of the time, Pallas kernels for 0%

commit v1 on v0

v1 whole, which is shorter than its diff:
```python
from functools import partial
import math

import jax
import jax.numpy as jnp
import numpy as np
from jax import lax
from jax.experimental import pallas as pl
from jax.experimental.pallas import tpu as pltpu
from jax.sharding import PartitionSpec as P

DH = 64
PLEN = 250
STEP = 5
ROWS = 256
BUCKETS = 32
SPAN = 128

MESH = pl.DeviceIdType.MESH
BF = jnp.bfloat16
F32 = jnp.float32
MIB = 2**20

norm_eps = 1e-06
masked_score = -1000000000.0
beta_first = 0.5
beta_second = 0.5
adam_eps = 1e-08
decay_rate = 0.01
rate_inward = 0.015
rate_outward = 0.3
rate_expand = 0.04
rate_reduce = 0.02
rate_gains = 0.5
rate_table = 0.5


def adamw(weight, first_moment, second, gradient, step_rate):
    new_first = beta_first * first_moment + (1.0 - beta_first) * gradient
    new_second = beta_second * second + (1.0 - beta_second) * gradient * gradient
    first_hat = new_first / (1.0 - beta_first**STEP)
    second_hat = new_second / (1.0 - beta_second**STEP)
    new_weight = weight - step_rate * (
        first_hat / (jnp.sqrt(second_hat) + adam_eps) + decay_rate * weight
    )
    return (new_weight, new_first, new_second)


def distance_onehot():
    span = 2 * ROWS
    relative = np.arange(span)
    relative = np.where(relative < ROWS, relative, relative - span)
    half = BUCKETS // 2
    exact = half // 2
    distance = np.abs(relative)
    far = np.full_like(distance, exact)
    for level in range(1, half - exact):
        far += distance >= math.ceil(exact * (SPAN / exact) ** (level / (half - exact)))
    bucket = np.where(relative > 0, half, 0) + np.where(distance < exact, distance, far)
    return (bucket[:, None] == np.arange(BUCKETS)[None]).astype(np.float32)


def dot(a, b, ca=1, cb=0):
    return lax.dot_general(a, b, (((ca,), (cb,)), ((), ())), preferred_element_type=F32)


def vmem():
    return pl.BlockSpec(memory_space=pltpu.VMEM)


def links(n):
    me = lax.axis_index("dp")
    nz = n // 4
    x, y, z = lax.rem(me, 2), lax.rem(me // 2, 2), me // 4
    column = lax.rem(me, 4)
    x_peer, y_peer = me + 1 - 2 * x, me + 2 - 4 * y
    far_peer = x_peer + 2 - 4 * y
    return me, nz, z, column, x_peer, y_peer, far_peer


def greet(peers):
    barrier = pltpu.get_barrier_semaphore()
    for peer in peers:
        pl.semaphore_signal(barrier, inc=1, device_id=peer, device_id_type=MESH)
    pl.semaphore_wait(barrier, len(peers))


def dp_peers(n):
    me, nz, z, column, x_peer, y_peer, _ = links(n)
    out = [{"dp": x_peer}, {"dp": y_peer}]
    for k in range(1, nz):
        out.append({"dp": lax.rem(z + k, nz) * 4 + column})
    return out


def gather_kernel(n, *refs):
    own = refs[:4]
    outs = refs[4:8]
    odd, wide, ss, rs = refs[8:12]
    full = (outs[0], odd, outs[2], outs[3])
    me, nz, z, column, x_peer, y_peer, far_peer = links(n)

    def block(k, base):
        return lax.rem(z + k, nz) * 4 + lax.rem(base, 4)

    def copy(a, role, k, blk, peer):
        return pltpu.make_async_remote_copy(
            src_ref=full[a].at[blk],
            dst_ref=full[a].at[blk],
            send_sem=ss.at[a, role, k],
            recv_sem=rs.at[a, role, k],
            device_id={"dp": peer},
            device_id_type=MESH,
        )

    greet(dp_peers(n))
    for a in range(4):
        full[a][me] = own[a][...]
    for a in range(4):
        for k in range(1, nz):
            copy(a, 0, k, me, lax.rem(z - k + nz, nz) * 4 + column).start()
        copy(a, 1, 0, me, x_peer).start()
        copy(a, 2, 0, me, y_peer).start()
    for a in range(4):
        for k in range(nz):
            if k > 0:
                blk = block(k, me)
                copy(a, 0, k, blk, x_peer).wait_recv()
                copy(a, 1, k, blk, x_peer).start()
                copy(a, 2, k, blk, y_peer).start()
        for k in range(nz):
            blk = block(k, x_peer)
            copy(a, 1, k, blk, x_peer).wait_recv()
            if k % 2 == 0:
                copy(a, 3, k, blk, y_peer).start()
            blk = block(k, y_peer)
            copy(a, 2, k, blk, y_peer).wait_recv()
            if k % 2 == 1:
                copy(a, 3, k, blk, x_peer).start()
    for a in range(4):
        for k in range(nz):
            copy(a, 3, k, block(k, far_peer), x_peer).wait_recv()
            if k > 0:
                copy(a, 0, k, me, x_peer).wait_send()
            for role in (1, 2, 3):
                copy(a, role, k, me, x_peer).wait_send()
    rows = wide.shape[0] // n
    for d in range(n):
        wide[d * rows : (d + 1) * rows] = odd[d].astype(F32)[:rows]
    outs[1][...] = wide[...].astype(BF)


def gather_weights(n, inward, outward, expand, reduce_):
    rows_o = outward.shape[0]
    padded = jnp.pad(outward, ((0, -rows_o % 16), (0, 0)))
    shards = [inward, padded, expand, reduce_]
    shapes = [(n,) + s.shape for s in shards]
    d = outward.shape[1]
    nz = n // 4
    out_shapes = [jax.ShapeDtypeStruct(s, BF) for s in shapes]
    out_shapes[1] = jax.ShapeDtypeStruct((n * rows_o, d), BF)
    outs = pl.pallas_call(
        partial(gather_kernel, n),
        out_shape=out_shapes,
        in_specs=[vmem()] * 4,
        out_specs=[vmem()] * 4,
        scratch_shapes=[
            pltpu.VMEM(shapes[1], BF),
            pltpu.VMEM((n * rows_o, d), F32),
            pltpu.SemaphoreType.DMA((4, 4, nz)),
            pltpu.SemaphoreType.DMA((4, 4, nz)),
        ],
        compiler_params=pltpu.CompilerParams(
            collective_id=1, has_side_effects=True, vmem_limit_bytes=32 * MIB
        ),
        name="gather_weights",
    )(*shards)
    return [o.reshape(-1, o.shape[-1]) for o in outs]


def scatter_kernel(n, *refs):
    grads = refs[:4]
    small = refs[4]
    outs = refs[5:9]
    small_out = refs[9]
    bufs = refs[10:14]
    small_z, small_xy, ss, rs, ssm, rsm = refs[14:20]
    me, nz, z, column, x_peer, y_peer, far_peer = links(n)

    def block(k, base):
        return lax.rem(z + k, nz) * 4 + lax.rem(base, 4)

    def copy(a, role, k, src, slot, peer):
        return pltpu.make_async_remote_copy(
            src_ref=src,
            dst_ref=bufs[a].at[slot, k],
            send_sem=ss.at[a, role, k],
            recv_sem=rs.at[a, role, k],
            device_id={"dp": peer},
            device_id_type=MESH,
        )

    def small_copy(role, src, dst, peer):
        return pltpu.make_async_remote_copy(
            src_ref=src,
            dst_ref=dst,
            send_sem=ssm.at[role],
            recv_sem=rsm.at[role],
            device_id={"dp": peer},
            device_id_type=MESH,
        )

    def z_peer(k):
        return lax.rem(z + k, nz) * 4 + column

    greet(dp_peers(n))
    small_z[z] = small[...]
    for k in range(1, nz):
        small_copy(k, small, small_z.at[z], z_peer(k)).start()
    for a in range(4):
        for k in range(nz):
            far = grads[a].at[block(k, far_peer)]
            copy(a, 0, k, far, 0, y_peer if k % 2 == 0 else x_peer).start()
        for k in range(nz):
            if k % 2 == 1:
                copy(a, 1, k, grads[a].at[block(k, x_peer)], 2, x_peer).start()
            else:
                copy(a, 2, k, grads[a].at[block(k, y_peer)], 4, y_peer).start()
    for k in range(1, nz):
        small_copy(k, small, small_z.at[lax.rem(z - k + nz, nz)], x_peer).wait()
    total = small_z[0]
    for k in range(1, nz):
        total += small_z[k]
    small_xy[0] = total
    small_copy(0, small_xy.at[0], small_xy.at[1], x_peer).start()
    for a in range(4):
        for k in range(nz):
            copy(a, 0, k, grads[a].at[0], 0, x_peer).wait_recv()
            role, peer, slot = (1, x_peer, 1) if k % 2 == 0 else (2, y_peer, 3)
            mine = grads[a][block(k, peer)].astype(F32) + bufs[a][0, k].astype(F32)
            bufs[a][slot, k] = mine.astype(BF)
            copy(a, role, k, bufs[a].at[slot, k], slot + 1, peer).start()
        if a == 0:
            small_copy(0, small_xy.at[0], small_xy.at[1], x_peer).wait()
            small_xy[2] = small_xy[0] + small_xy[1]
            small_copy(nz, small_xy.at[2], small_xy.at[3], y_peer).start()
    for a in range(4):
        for k in list(range(1, nz)) + [0]:
            copy(a, 1, k, grads[a].at[0], 2, x_peer).wait_recv()
            copy(a, 2, k, grads[a].at[0], 4, y_peer).wait_recv()
            mine = (
                grads[a][block(k, me)].astype(F32)
                + bufs[a][2, k].astype(F32)
                + bufs[a][4, k].astype(F32)
            )
            if k == 0:
                outs[a][...] = mine
            else:
                bufs[a][5, k] = mine.astype(BF)
                copy(a, 3, k, bufs[a].at[5, k], 6, z_peer(k)).start()
    small_copy(nz, small_xy.at[2], small_xy.at[3], y_peer).wait()
    small_out[...] = small_xy[2] + small_xy[3]
    for a in range(4):
        total = outs[a][...]
        for k in range(1, nz):
            copy(a, 3, k, grads[a].at[0], 6, x_peer).wait_recv()
            total += bufs[a][6, k].astype(F32)
        outs[a][...] = total
        for k in range(nz):
            for role in (0, 1, 2):
                copy(a, role, k, grads[a].at[0], 0, x_peer).wait_send()
            if k > 0:
                copy(a, 3, k, grads[a].at[0], 0, x_peer).wait_send()


def scatter_grads(n, grads, small):
    shapes = [g.shape[1:] for g in grads]
    nz = n // 4
    return pl.pallas_call(
        partial(scatter_kernel, n),
        out_shape=[jax.ShapeDtypeStruct(s, F32) for s in shapes]
        + [jax.ShapeDtypeStruct(small.shape, F32)],
        in_specs=[vmem()] * 5,
        out_specs=[vmem()] * 5,
        scratch_shapes=[pltpu.VMEM((7, nz) + s, BF) for s in shapes]
        + [
            pltpu.VMEM((nz,) + small.shape, F32),
            pltpu.VMEM((4,) + small.shape, F32),
            pltpu.SemaphoreType.DMA((4, 4, nz)),
            pltpu.SemaphoreType.DMA((4, 4, nz)),
            pltpu.SemaphoreType.DMA((nz + 1,)),
            pltpu.SemaphoreType.DMA((nz + 1,)),
        ],
        compiler_params=pltpu.CompilerParams(
            collective_id=2, has_side_effects=True, vmem_limit_bytes=48 * MIB
        ),
        name="scatter_grads",
    )(*grads, small)


def partner():
    return {"mp": 1 - lax.axis_index("mp")}


def swap(mine, theirs, ss, rs, p):
    return pltpu.make_async_remote_copy(
        src_ref=mine.at[p],
        dst_ref=theirs.at[p],
        send_sem=ss.at[p],
        recv_sem=rs.at[p],
        device_id=partner(),
        device_id_type=MESH,
    )


def inverse_rms(v):
    return lax.rsqrt(jnp.mean(v * v, axis=-1, keepdims=True) + norm_eps)


def attend_kernel(
    passages, heads, tok, tok_prev, mask, gains, line, wi, wo,
    proj, probs, ctx, hidden, bias, mine, theirs, ss, rs,
):
    p = pl.program_id(0)

    @pl.when(p == 0)
    def _():
        greet([partner()])
        for h in range(heads):
            rows = jnp.broadcast_to(line[h : h + 1, :], (ROWS, 2 * ROWS))
            bias[h] = pltpu.roll(rows, 0, 1, stride=1, stride_axis=0)[:, :ROWS]

    @pl.when(p < passages)
    def _():
        x = tok[0].astype(F32)
        normed = (x * inverse_rms(x) * gains[0:1, :]).astype(BF)
        proj[0] = dot(normed, wi[...]).astype(BF)
        width = heads * DH
        masked = mask[pl.ds(p, 1), :]
        for h in range(heads):
            q = proj[0, :, h * DH : (h + 1) * DH]
            k = proj[0, :, width + h * DH : width + (h + 1) * DH]
            v = proj[0, :, 2 * width + h * DH : 2 * width + (h + 1) * DH]
            s = dot(q, k, 1, 1) + bias[h] + masked
            e = jnp.exp(s - jnp.max(s, axis=-1, keepdims=True))
            a = (e * (1.0 / jnp.sum(e, axis=-1, keepdims=True))).astype(BF)
            probs[0, h] = a
            ctx[0, :, h * DH : (h + 1) * DH] = dot(a, v).astype(BF)
        mine[p] = dot(ctx[0], wo[...]).astype(BF)
        swap(mine, theirs, ss, rs, p).start()

    @pl.when(p > 0)
    def _():
        last = p - 1
        swap(mine, theirs, ss, rs, last).wait()
        hidden[0] = tok_prev[0].astype(F32) + (
            mine[last].astype(F32) + theirs[last].astype(F32)
        )


def this(passages, rank=3):
    return lambda p: (jnp.minimum(p, passages - 1),) + (0,) * (rank - 1)


def prev(rank=3):
    return lambda p: (jnp.maximum(p - 1, 0),) + (0,) * (rank - 1)


def whole(a):
    return pl.BlockSpec(a.shape, lambda p: (0,) * len(a.shape), pipeline_mode=pl.Buffered(1))


def attend(passages, heads, tok, mask, gains, line, wi, wo):
    d = tok.shape[-1]
    width = heads * DH
    now, lag = this(passages), prev()
    return pl.pallas_call(
        partial(attend_kernel, passages, heads),
        grid=(passages + 1,),
        in_specs=[
            pl.BlockSpec((1, ROWS, d), now),
            pl.BlockSpec((1, ROWS, d), lag),
            whole(mask), whole(gains), whole(line), whole(wi), whole(wo),
        ],
        out_specs=[
            pl.BlockSpec((1, ROWS, 3 * width), now),
            pl.BlockSpec((1, heads, ROWS, ROWS), this(passages, 4)),
            pl.BlockSpec((1, ROWS, width), now),
            pl.BlockSpec((1, ROWS, d), lag),
        ],
        out_shape=[
            jax.ShapeDtypeStruct((passages, ROWS, 3 * width), BF),
            jax.ShapeDtypeStruct((passages, heads, ROWS, ROWS), BF),
            jax.ShapeDtypeStruct((passages, ROWS, width), BF),
            jax.ShapeDtypeStruct((passages, ROWS, d), F32),
        ],
        scratch_shapes=[
            pltpu.VMEM((heads, ROWS, ROWS), F32),
            pltpu.VMEM((passages, ROWS, d), BF),
            pltpu.VMEM((passages, ROWS, d), BF),
            pltpu.SemaphoreType.DMA((passages,)),
            pltpu.SemaphoreType.DMA((passages,)),
        ],
        compiler_params=pltpu.CompilerParams(
            collective_id=3, has_side_effects=True, vmem_limit_bytes=48 * MIB
        ),
        name="attend",
    )(tok, tok, mask, gains, line, wi, wo)


gelu_root = math.sqrt(2.0 / math.pi)
gelu_cube = 0.044715


def feed_kernel(
    passages, parts, hid, hid_prev, cot, cot_prev, gains, we, wr,
    layer, hidden_grad, reduce_grad, expand_grad, gain_grad,
    acc_r, acc_e, out_m, out_t, in_m, in_t, ss, rs, ss2, rs2,
):
    p = pl.program_id(0)

    @pl.when(p == 0)
    def _():
        greet([partner()])
        acc_r[...] = jnp.zeros_like(acc_r)
        acc_e[...] = jnp.zeros_like(acc_e)
        gain_grad[...] = jnp.zeros_like(gain_grad)

    @pl.when(p < passages)
    def _():
        h = hid[0]
        normed = (h * inverse_rms(h) * gains[1:2, :]).astype(BF)
        c = cot[0]
        hidden_units = we.shape[1]
        step = hidden_units // parts
        reduced = None
        for i in range(parts):
            cut = slice(i * step, (i + 1) * step)
            u = dot(normed, we[:, cut])
            square = u * u
            t = jnp.tanh(u * (gelu_root + (gelu_root * gelu_cube) * square))
            half = 0.5 * (1.0 + t)
            act = (u * half).astype(BF)
            slope = half + (0.5 * u) * (1.0 - t * t) * (
                gelu_root + (3.0 * gelu_root * gelu_cube) * square
            )
            back = (dot(c, wr[cut, :], 1, 1) * slope).astype(BF)
            acc_r[cut, :] += dot(act, c, 0, 0)
            acc_e[:, cut] += dot(normed, back, 0, 0)
            r_part = dot(act, wr[cut, :])
            n_part = dot(back, we[:, cut], 1, 1)
            reduced = (r_part, n_part) if reduced is None else (reduced[0] + r_part, reduced[1] + n_part)
        out_m[p] = reduced[0].astype(BF)
        swap(out_m, out_t, ss, rs, p).start()
        in_m[p] = reduced[1].astype(BF)
        swap(in_m, in_t, ss2, rs2, p).start()

    @pl.when(p > 0)
    def _():
        last = p - 1
        h = hid_prev[0]
        swap(out_m, out_t, ss, rs, last).wait()
        layer[0] = (h + (out_m[last].astype(F32) + out_t[last].astype(F32))).astype(BF)
        swap(in_m, in_t, ss2, rs2, last).wait()
        grad = in_m[last].astype(F32) + in_t[last].astype(F32)
        r = inverse_rms(h)
        zed = gains[1:2, :] * grad
        hr = h * r
        gain_grad[0:1, :] += jnp.sum(grad * hr, axis=0, keepdims=True)
        inner = jnp.mean(zed * hr, axis=-1, keepdims=True)
        hidden_grad[0] = cot_prev[0].astype(F32) + r * (zed - hr * inner)

    @pl.when(p == passages)
    def _():
        reduce_grad[...] = acc_r[...].astype(BF)
        expand_grad[...] = acc_e[...].astype(BF)


def feed(passages, hid, cot, gains, we, wr):
    d = hid.shape[-1]
    units = we.shape[1]
    now, lag = this(passages), prev()
    row = (1, ROWS, d)
    fixed = lambda p: (0, 0)
    return pl.pallas_call(
        partial(feed_kernel, passages, 3),
        grid=(passages + 1,),
        in_specs=[
            pl.BlockSpec(row, now), pl.BlockSpec(row, lag), pl.BlockSpec(row, now), pl.BlockSpec(row, lag),
            whole(gains), whole(we), whole(wr),
        ],
        out_specs=[
            pl.BlockSpec(row, lag),
            pl.BlockSpec(row, lag),
            pl.BlockSpec((units, d), fixed),
            pl.BlockSpec((d, units), fixed),
            pl.BlockSpec((8, d), fixed),
        ],
        out_shape=[
            jax.ShapeDtypeStruct((passages, ROWS, d), BF),
            jax.ShapeDtypeStruct((passages, ROWS, d), F32),
            jax.ShapeDtypeStruct((units, d), BF),
            jax.ShapeDtypeStruct((d, units), BF),
            jax.ShapeDtypeStruct((8, d), F32),
        ],
        scratch_shapes=[pltpu.VMEM((units, d), F32), pltpu.VMEM((d, units), F32)]
        + [pltpu.VMEM((passages, ROWS, d), BF)] * 4
        + [pltpu.SemaphoreType.DMA((passages,))] * 4,
        compiler_params=pltpu.CompilerParams(
            collective_id=4, has_side_effects=True, vmem_limit_bytes=60 * MIB
        ),
        name="feed",
    )(hid, hid, cot, cot, gains, we, wr)


def attend_back_kernel(
    passages, heads, blocks, hgrad, hgrad_prev, tok, tok_prev, proj, probs, ctx, gains, wi, wo,
    input_grad, inward_grad, outward_grad, gain_grad, lines,
    acc_i, acc_o, acc_s, dproj, in_m, in_t, ss, rs,
):
    p = pl.program_id(0)

    @pl.when(p == 0)
    def _():
        greet([partner()])
        acc_i[...] = jnp.zeros_like(acc_i)
        acc_o[...] = jnp.zeros_like(acc_o)
        acc_s[...] = jnp.zeros_like(acc_s)
        gain_grad[...] = jnp.zeros_like(gain_grad)

    @pl.when(p < passages)
    def _():
        width = heads * DH
        above = hgrad[0].astype(BF)
        acc_o[...] += dot(ctx[0], above, 0, 0)
        dctx = dot(above, wo[...], 1, 1).astype(BF)
        for h in range(heads):
            at = [slice(c * width + h * DH, c * width + (h + 1) * DH) for c in range(3)]
            q, k, v = (proj[0, :, s] for s in at)
            dc = dctx[:, h * DH : (h + 1) * DH]
            a = probs[0, h]
            dproj[:, at[2]] = dot(a, dc, 0, 0).astype(BF)
            dp = dot(dc, v, 1, 1)
            a = a.astype(F32)
            centre = jnp.sum(a * dp, axis=-1, keepdims=True)
            ds = (a * (dp - centre)).astype(BF)
            acc_s[h] += ds.astype(F32)
            dproj[:, at[0]] = dot(ds, k).astype(BF)
            dproj[:, at[1]] = dot(ds, q, 0, 0).astype(BF)
        x = tok[0].astype(F32)
        normed = (x * inverse_rms(x) * gains[0:1, :]).astype(BF)
        acc_i[...] += dot(normed, dproj[...], 0, 0)
        in_m[p] = dot(dproj[...], wi[...], 1, 1).astype(BF)
        swap(in_m, in_t, ss, rs, p).start()

    @pl.when(p > 0)
    def _():
        last = p - 1
        x = tok_prev[0].astype(F32)
        swap(in_m, in_t, ss, rs, last).wait()
        grad = in_m[last].astype(F32) + in_t[last].astype(F32)
        r = inverse_rms(x)
        zed = gains[0:1, :] * grad
        xr = x * r
        gain_grad[0:1, :] += jnp.sum(grad * xr, axis=0, keepdims=True)
        inner = jnp.mean(zed * xr, axis=-1, keepdims=True)
        input_grad[0] = hgrad_prev[0] + r * (zed - xr * inner)

    @pl.when(p == passages)
    def _():
        inward_grad[...] = acc_i[...].astype(BF)
        rows = acc_o.shape[0] // blocks
        pad = outward_grad.shape[1] - rows
        for b in range(blocks):
            part = acc_o[b * rows : (b + 1) * rows, :]
            if pad:
                part = jnp.concatenate([part, jnp.zeros((pad, part.shape[1]), F32)], axis=0)
            outward_grad[b] = part.astype(BF)
        lines[...] = jnp.zeros_like(lines)
        for h in range(heads):
            rows = jnp.concatenate([acc_s[h], jnp.zeros((ROWS, ROWS), F32)], axis=1)
            while rows.shape[0] > 1:
                half = rows.shape[0] // 2
                rows = rows[:half] + pltpu.roll(rows[half:], 2 * ROWS - half, 1)
            lines[h : h + 1, :] = rows


def attend_back(passages, heads, blocks, hgrad, tok, proj, probs, ctx, gains, wi, wo):
    d = hgrad.shape[-1]
    width = heads * DH
    now, lag = this(passages), prev()
    row = (1, ROWS, d)
    fixed = lambda p: (0, 0)
    rows = width // blocks
    rows += -rows % 16
    return pl.pallas_call(
        partial(attend_back_kernel, passages, heads, blocks),
        grid=(passages + 1,),
        in_specs=[
            pl.BlockSpec(row, now), pl.BlockSpec(row, lag), pl.BlockSpec(row, now), pl.BlockSpec(row, lag),
            pl.BlockSpec((1, ROWS, 3 * width), now),
            pl.BlockSpec((1, heads, ROWS, ROWS), this(passages, 4)),
            pl.BlockSpec((1, ROWS, width), now),
            whole(gains), whole(wi), whole(wo),
        ],
        out_specs=[
            pl.BlockSpec(row, lag),
            pl.BlockSpec((d, 3 * width), fixed),
            pl.BlockSpec((blocks, rows, d), lambda p: (0, 0, 0)),
            pl.BlockSpec((8, d), fixed),
            pl.BlockSpec((8, 2 * ROWS), fixed),
        ],
        out_shape=[
            jax.ShapeDtypeStruct((passages, ROWS, d), F32),
            jax.ShapeDtypeStruct((d, 3 * width), BF),
            jax.ShapeDtypeStruct((blocks, rows, d), BF),
            jax.ShapeDtypeStruct((8, d), F32),
            jax.ShapeDtypeStruct((8, 2 * ROWS), F32),
        ],
        scratch_shapes=[
            pltpu.VMEM((d, 3 * width), F32),
            pltpu.VMEM((width, d), F32),
            pltpu.VMEM((heads, ROWS, ROWS), F32),
            pltpu.VMEM((ROWS, 3 * width), BF),
            pltpu.VMEM((passages, ROWS, d), BF),
            pltpu.VMEM((passages, ROWS, d), BF),
            pltpu.SemaphoreType.DMA((passages,)),
            pltpu.SemaphoreType.DMA((passages,)),
        ],
        compiler_params=pltpu.CompilerParams(
            collective_id=5, has_side_effects=True, vmem_limit_bytes=60 * MIB
        ),
        name="attend_back",
    )(hgrad, hgrad, tok, tok, proj, probs, ctx, gains, wi, wo)


def shards(
    n,
    tokens,
    cotangent,
    buckets,
    inward_master,
    inward_first,
    inward_second,
    outward_master,
    outward_first,
    outward_second,
    expand_master,
    expand_first,
    expand_second,
    reduce_master,
    reduce_first,
    reduce_second,
    gains_master,
    gains_first,
    gains_second,
    table_master,
    table_first,
    table_second,
):
    d = tokens.shape[1]
    passages = tokens.shape[0] // PLEN
    heads = inward_master.shape[2] // DH
    width = heads * DH
    inward_rows = inward_master.shape[0]
    inward_flat = inward_master.reshape(inward_rows, 3 * width)
    masters = (inward_flat, outward_master, expand_master, reduce_master)
    direct = (
        n % 4 == 0
        and inward_rows % 16 == 0
        and reduce_master.shape[0] % 16 == 0
        and outward_master.shape[0] % 8 == 0
    )
    if direct:
        wi, wo, we, wr = gather_weights(n, *(w.astype(BF) for w in masters))
    else:
        wi, wo, we, wr = (
            lax.all_gather(w.astype(BF), "dp", axis=0, tiled=True) for w in masters
        )

    def passage_rows(a):
        return jnp.pad(a.reshape(passages, PLEN, d), ((0, 0), (0, ROWS - PLEN), (0, 0)))

    tok, cot = passage_rows(tokens), passage_rows(cotangent)
    mask = jnp.where(buckets[:, 0, :] < BUCKETS, 0.0, masked_score)
    mask = jnp.pad(mask, ((0, -passages % 8), (0, ROWS - PLEN)), constant_values=masked_score)
    onehot = jnp.asarray(distance_onehot())
    line = lax.dot_general(
        table_master, onehot, (((0,), (1,)), ((), ())), precision=lax.Precision.HIGHEST
    )
    line = jnp.pad(line, ((0, -heads % 8), (0, 0)))
    proj, probs, ctx, hidden = attend(passages, heads, tok, mask, gains_master, line, wi, wo)
    layer, hidden_grad, reduce_grad, expand_grad, gain_two = feed(
        passages, hidden, cot, gains_master, we, wr
    )
    blocks = n if direct else 1
    input_grad, inward_grad, outward_grad, gain_one, lines = attend_back(
        passages, heads, blocks, hidden_grad, tok, proj, probs, ctx, gains_master, wi, wo
    )
    table_grad = lax.dot_general(
        lines[:heads], onehot, (((1,), (0,)), ((), ())), precision=lax.Precision.HIGHEST
    )
    if direct:
        flat = jnp.pad(table_grad.reshape(1, -1), ((0, 0), (0, d - table_grad.size)))
        small = jnp.concatenate([gain_one[:1], gain_two[:1], flat, jnp.zeros((5, d), F32)], axis=0)
        cut = [
            g.reshape((n, g.shape[0] // n, g.shape[1]))
            for g in (inward_grad, expand_grad, reduce_grad)
        ]
        sums = scatter_grads(n, [cut[0], outward_grad, cut[1], cut[2]], small)
        inward_sum, outward_sum, expand_sum, reduce_sum, small = sums
        outward_sum = outward_sum[: outward_master.shape[0]]
        gains_sum = small[:2]
        table_sum = small[2, : table_grad.size].reshape(table_grad.shape).T
    else:
        inward_sum, outward_sum, expand_sum, reduce_sum = (
            lax.psum_scatter(g.astype(F32), "dp", scatter_dimension=0, tiled=True)
            for g in (inward_grad, outward_grad[0], expand_grad, reduce_grad)
        )
        gains_sum, table_sum = lax.psum(
            (jnp.concatenate([gain_one[:1], gain_two[:1]]), table_grad.T), "dp"
        )
    inward_sum = inward_sum.reshape(inward_master.shape)

    layer_out = layer[:, :PLEN].reshape(tokens.shape)
    input_grad = input_grad[:, :PLEN].reshape(tokens.shape)
    inward_new, inward_first_new, inward_second_new = adamw(
        inward_master, inward_first, inward_second, inward_sum, rate_inward
    )
    outward_new, outward_first_new, outward_second_new = adamw(
        outward_master, outward_first, outward_second, outward_sum, rate_outward
    )
    expand_new, expand_first_new, expand_second_new = adamw(
        expand_master, expand_first, expand_second, expand_sum, rate_expand
    )
    reduce_new, reduce_first_new, reduce_second_new = adamw(
        reduce_master, reduce_first, reduce_second, reduce_sum, rate_reduce
    )
    gains_new, gains_first_new, gains_second_new = adamw(
        gains_master, gains_first, gains_second, gains_sum, rate_gains
    )
    table_new, table_first_new, table_second_new = adamw(
        table_master, table_first, table_second, table_sum, rate_table
    )
    return (
        layer_out,
        input_grad,
        inward_new,
        inward_first_new,
        inward_second_new,
        inward_new.astype(jnp.bfloat16),
        outward_new,
        outward_first_new,
        outward_second_new,
        outward_new.astype(jnp.bfloat16),
        expand_new,
        expand_first_new,
        expand_second_new,
        expand_new.astype(jnp.bfloat16),
        reduce_new,
        reduce_first_new,
        reduce_second_new,
        reduce_new.astype(jnp.bfloat16),
        gains_new,
        gains_first_new,
        gains_second_new,
        table_new,
        table_first_new,
        table_second_new,
    )


def solution(mesh):
    rows = P("dp", None)
    inward = P("dp", None, "mp")
    tall = P(("mp", "dp"), None)
    wide = P("dp", "mp")
    table = P(None, "mp")
    return jax.shard_map(
        partial(shards, mesh.shape["dp"]),
        mesh=mesh,
        in_specs=(rows, rows, P("dp", None, None))
        + (inward,) * 3
        + (tall,) * 3
        + (wide,) * 3
        + (tall,) * 3
        + (P(),) * 3
        + (table,) * 3,
        out_specs=(rows, rows)
        + (inward,) * 4
        + (tall,) * 4
        + (wide,) * 4
        + (tall,) * 4
        + (P(),) * 3
        + (table,) * 3,
        check_vma=False,
    )
```

time: 1070 us -> 321 us (0.30)
  waiting for transfers between devices: 549 us -> 0 us
  Pallas kernels: 0 us -> 280 us
  matrix products: 201 us -> 1.27 us
  blocking collectives: 127 us -> 0 us
  local copies, waits for them, and re-layouts: 114 us -> 28 us
  other arithmetic: 58.4 us -> 9.75 us
  between operations: 14.5 us -> 0.95 us
    reduce_scatter x4 -> x0, waiting for transfers between devices: 311 us -> none  [the longest x1 136 us: shards(): lax.psum_scatter(reduce_grad, 'dp', scatter_dimension=0, tiled=True)]
    pallas_call x0 -> x5, Pallas kernels: none -> 280 us  [the longest x1 86.7 us: scatter_grads(): pl.pallas_call(partial(scatter_kernel, n), out_shape=[jax.ShapeDtypeStruc...]
    dot_general x52 -> x2, matrix products: 201 us -> 1.27 us  [the longest x1 0.94 us: shards(): lax.dot_general(lines[:heads], onehot, (((1,), (0,)), ((), ())), precisio...]
    all_gather x3 -> x0, waiting for transfers between devices: 136 us -> none  [the longest x1 62.2 us: shards(): lax.all_gather(reduce_master.astype(jnp.bfloat16), 'dp', axis=0, tiled=True)]
    psum x4 -> x0, waiting for transfers between devices: 103 us -> none  [the longest x1 31.6 us: shards(): normed_grad = lax.psum(normed_terms, 'mp')]
    psum x1 -> x0, blocking collectives: 77.5 us -> none  [shards(): lax.psum((jnp.stack([gain_one_grad, gain_two_grad]), table_grad), 'dp')]
    all_gather x1 -> x0, blocking collectives: 49.1 us -> none  [shards(): lax.all_gather(outward_master.astype(jnp.bfloat16), 'dp', axis=0, tiled=T...]
    another operation x10 -> x1, local copies, waits for them, and re-layouts: 21.8 us -> 0.08 us  [shards(): table_sum = small[2, :table_grad.size].reshape(table_grad.shape).T]
  transfers between devices with their start and end apart: 11 -> 0, of which waited for: 10 -> 0; matrix products, arithmetic and copies ran while one was open for 17% -> 0% of each run, Pallas kernels for 0% -> 0%
where the time goes in v1:
time: 321 us; the launch traced here: 320 us
  Pallas kernels  280 us (87%)
  local copies, waits for them, and re-layouts  28 us (9%)
  other arithmetic  9.75 us (3%)
    pallas_call x1, Pallas kernels, scatter_grads(): pl.pallas_call(partial(scatter_kernel, n), out_shape=[jax.ShapeDtypeStruc...  86.7 us
    pallas_call x1, Pallas kernels, gather_weights(): pl.pallas_call(partial(gather_kernel, n), out_shape=out_shapes, in_specs=...  70.9 us
    pallas_call x1, Pallas kernels, attend_back(): pl.pallas_call(partial(attend_back_kernel, passages, heads, blocks), grid...  49.4 us
    pallas_call x1, Pallas kernels, feed(): pl.pallas_call(partial(feed_kernel, passages, 3), grid=(passages + 1,), i...  46.5 us
    pallas_call x1, Pallas kernels, attend(): pl.pallas_call(partial(attend_kernel, passages, heads), grid=(passages +...  26.4 us
    unnamed x58, local copies, waits for them, and re-layouts  6.66 us
    reshape x2, local copies, waits for them, and re-layouts, passage_rows(): a.reshape(passages, PLEN, d)  6.58 us

profile of v1, /device:TPU:0, one launch (start us, length us, event | category | flops | bytes accessed | tf_op | source)
XLA Modules:
  0.0 319.8 jit_solution(1293212415641277873)
XLA Ops:
  0.7 1.0 convert_bitcast_fusion
  1.6 1.0 convert_element_type.38.refs_2_
  2.6 1.0 convert_element_type.39.refs_3_
  3.6 0.9 convert_element_type.37
  4.5 70.9 %gather_weights.1 = (bf16[16,48,1152]{2,1,0:T(8,128)(2,1)S(1)}, bf16[384,768]{1,0:T(8,128)(2,1)S(1)}, bf16[16,48,1536]{2,1,0:T(8,128)(2,1)S(1)}, bf16[16,96,768]{2,1,0:T(8,128)(2,1)S(1)}) custom-call(bf16[48,1152]{1,0:T(8,128)(2,1)S(1)} %bitcast.35, bf16[32,768]{1,0:T(8,128)(2,1)S(1)} %pad.26.refs_1_, bf16[48,1536]{1,0:T(8,128)(2,1)S(1)} %convert_element_type.38.refs_2_, ...), custom_call_target="tpu_custom_call" | custom-call | tf_op jit(solution)/shard_map/gather_weights/pallas_call | solution.py:162
  75.5 1.4 copy-done.1
  76.9 1.4 copy-done.2
  78.2 4.3 %reshape.91 = bf16[8,250,768]{2,1,0:T(8,128)(2,1)} reshape(bf16[2000,768]{1,0:T(8,128)(2,1)} %param.22) | data formatting | bytes 6144000 | tf_op jit(solution)/shard_map/reshape | solution.py:682
  82.6 3.9 %pad.23.tok.tok_prev = bf16[8,256,768]{2,1,0:T(8,128)(2,1)} pad(bf16[8,250,768]{2,1,0:T(8,128)(2,1)} %reshape.91, bf16[]{:T(256)} %constant.15.clone.1), padding=0_0x0_6x0_0 | pad | bytes 6217730 | tf_op jit(solution)/shard_map/jit(_pad)/pad | solution.py:682
  86.5 0.3 convolution_bitcast_fusion
  86.8 0.7 select_bitcast_fusion
  87.6 26.4 %attend.1 = (bf16[8,256,1152]{2,1,0:T(8,128)(2,1)}, bf16[8,6,256,256]{3,2,1,0:T(8,128)(2,1)}, bf16[8,256,384]{2,1,0:T(8,128)(2,1)S(1)}, f32[8,256,768]{2,1,0:T(8,128)}) custom-call(bf16[8,256,768]{2,1,0:T(8,128)(2,1)} %pad.23.tok.tok_prev, bf16[8,256,768]{2,1,0:T(8,128)(2,1)} %pad.23.tok.tok_prev, f32[8,256]{1,0:T(8,128)S(1)} %pad.24.mask, ...), custom_call_target="tpu_custom_call" | custom-call | tf_op jit(solution)/shard_map/attend/pallas_call | solution.py:377
  114.0 1.2 copy-done.6
  115.1 2.3 reshape.93
  117.4 1.9 pad.27.cot.cot_prev
  119.3 46.5 %feed.1 = (bf16[8,256,768]{2,1,0:T(8,128)(2,1)}, f32[8,256,768]{2,1,0:T(8,128)}, bf16[1536,768]{1,0:T(8,128)(2,1)}, bf16[768,1536]{1,0:T(8,128)(2,1)}, f32[8,768]{1,0:T(8,128)}) custom-call(f32[8,256,768]{2,1,0:T(8,128)} %get-tuple-element.49.hid.hid_prev, f32[8,256,768]{2,1,0:T(8,128)} %get-tuple-element.49.hid.hid_prev, ...), custom_call_target="tpu_custom_call" | custom-call | tf_op jit(solution)/shard_map/feed/pallas_call | solution.py:485
  165.8 49.4 %attend_back.1 = (f32[8,256,768]{2,1,0:T(8,128)}, bf16[768,1152]{1,0:T(8,128)(2,1)}, bf16[16,32,768]{2,1,0:T(8,128)(2,1)}, f32[8,768]{1,0:T(8,128)}, f32[8,512]{1,0:T(8,128)}) custom-call(f32[8,256,768]{2,1,0:T(8,128)} %get-tuple-element.53.hgrad.hgrad_prev, f32[8,256,768]{2,1,0:T(8,128)} %get-tuple-element.53.hgrad.hgrad_prev, ...), custom_call_target="tpu_custom_call" | custom-call | tf_op jit(solution)/shard_map/attend_back/pallas_call | solution.py:596
  215.1 0.9 fusion.6
  216.2 0.8 slice.30
  216.9 0.7 slice.31
  217.8 1.5 copy-done.5
  219.3 1.1 copy-done.7
  220.5 86.7 %scatter_grads.1 = (f32[48,1152]{1,0:T(8,128)S(1)}, f32[32,768]{1,0:T(8,128)S(1)}, f32[48,1536]{1,0:T(8,128)S(1)}, f32[96,768]{1,0:T(8,128)S(1)}, f32[8,768]{1,0:T(8,128)S(1)}) custom-call(bf16[16,48,1152]{2,1,0:T(8,128)(2,1)S(1)} %bitcast.34, bf16[16,32,768]{2,1,0:T(8,128)(2,1)S(1)} %copy-done.7, bf16[16,48,1536]{2,1,0:T(8,128)(2,1)S(1)} %bitcast.33, ...), custom_call_target="tpu_custom_call" | custom-call | tf_op jit(solution)/shard_map/scatter_grads/pallas_call | solution.py:279
  307.3 1.1 fusion.12
  308.5 1.1 fusion.14
  309.6 1.0 fusion.18
  310.6 0.7 fusion.16
  311.3 0.6 multiply_subtract_fusion.4
  312.0 0.1 reshape_squeeze.3
  312.0 0.6 multiply_subtract_fusion.5
  312.7 5.0 %reshape.97 = f32[2000,768]{1,0:T(8,128)} reshape(f32[8,250,768]{2,1,0:T(8,128)} %bitcast.37) | data formatting | bytes 12288000 | tf_op jit(solution)/shard_map/reshape | solution.py:726
  317.7 2.0 reshape.96
  (62 shorter events, 0.4 us)
Async XLA Ops:
  75.4 1.4 copy-start.1
  76.9 1.4 copy-start.2
  78.2 9.3 %copy-start = (bf16[16,48,1152]{2,1,0:T(8,128)(2,1)}, bf16[16,48,1152]{2,1,0:T(8,128)(2,1)S(1)}, u32[]{:S(2)}) copy-start(bf16[16,48,1152]{2,1,0:T(8,128)(2,1)S(1)} %get-tuple-element.47) | copy-start | bytes 5308420
  78.2 9.3 %copy-start.4 = (bf16[384,768]{1,0:T(8,128)(2,1)}, bf16[384,768]{1,0:T(8,128)(2,1)S(1)}, u32[]{:S(2)}) copy-start(bf16[384,768]{1,0:T(8,128)(2,1)S(1)} %get-tuple-element.48.wo) | copy-start | bytes 1769476
  82.5 3.9 %copy-start.13 = (f32[512,32]{1,0:T(8,128)S(1)}, f32[512,32]{1,0:T(8,128)}, u32[]{:S(2)}) copy-start(f32[512,32]{1,0:T(8,128)} %constant.27.clone) | copy-start | bytes 196612
  82.5 3.9 %copy-start.24 = (f32[32,6]{0,1:T(8,128)S(1)}, f32[32,6]{0,1:T(8,128)}, u32[]{:S(2)}) copy-start(f32[32,6]{0,1:T(8,128)} %param.40) | copy-start | bytes 2308
  82.5 5.0 %copy-start.8 = (f32[2,768]{1,0:T(2,128)S(1)}, f32[2,768]{1,0:T(2,128)}, u32[]{:S(2)}) copy-start(f32[2,768]{1,0:T(2,128)} %gains.5) | copy-start | bytes 18436
  114.0 1.2 copy-start.6
  165.8 52.1 %copy-start.3 = (bf16[768,1536]{1,0:T(8,128)(2,1)S(1)}, bf16[768,1536]{1,0:T(8,128)(2,1)}, u32[]{:S(2)}) copy-start(bf16[768,1536]{1,0:T(8,128)(2,1)} %get-tuple-element.60) | copy-start | bytes 7077892
  217.8 1.5 copy-start.5
  219.3 1.1 copy-start.7
  220.4 86.8 %copy-start.11 = (f32[96,768]{1,0:T(8,128)S(1)}, f32[96,768]{1,0:T(8,128)}, u32[]{:S(2)}) copy-start(f32[96,768]{1,0:T(8,128)} %param.34) | copy-start | bytes 884740
  220.4 86.8 %copy-start.15 = (f32[96,768]{1,0:T(8,128)S(1)}, f32[96,768]{1,0:T(8,128)}, u32[]{:S(2)}) copy-start(f32[96,768]{1,0:T(8,128)} %param.35) | copy-start | bytes 884740
  220.4 86.8 %copy-start.16 = (f32[96,768]{1,0:T(8,128)S(1)}, f32[96,768]{1,0:T(8,128)}, u32[]{:S(2)}) copy-start(f32[96,768]{1,0:T(8,128)} %param.36) | copy-start | bytes 884740
  220.4 88.0 %copy-start.12 = (f32[48,1536]{1,0:T(8,128)S(1)}, f32[48,1536]{1,0:T(8,128)}, u32[]{:S(2)}) copy-start(f32[48,1536]{1,0:T(8,128)} %param.31) | copy-start | bytes 884740
  220.4 88.0 %copy-start.17 = (f32[48,1536]{1,0:T(8,128)S(1)}, f32[48,1536]{1,0:T(8,128)}, u32[]{:S(2)}) copy-start(f32[48,1536]{1,0:T(8,128)} %param.32) | copy-start | bytes 884740
  220.5 88.0 %copy-start.18 = (f32[48,1536]{1,0:T(8,128)S(1)}, f32[48,1536]{1,0:T(8,128)}, u32[]{:S(2)}) copy-start(f32[48,1536]{1,0:T(8,128)} %param.33) | copy-start | bytes 884740
  307.2 2.4 copy-start.14
  307.2 2.4 copy-start.20
  307.2 2.4 copy-start.21
  307.2 3.4 %copy-start.19 = (f32[24,768]{1,0:T(8,128)S(1)}, f32[24,768]{1,0:T(8,128)}, u32[]{:S(2)}) copy-start(f32[24,768]{1,0:T(8,128)} %param.28) | copy-start | bytes 221188
  307.2 3.3 %copy-start.22 = (f32[24,768]{1,0:T(8,128)S(1)}, f32[24,768]{1,0:T(8,128)}, u32[]{:S(2)}) copy-start(f32[24,768]{1,0:T(8,128)} %param.29) | copy-start | bytes 221188
  307.2 3.3 %copy-start.23 = (f32[24,768]{1,0:T(8,128)S(1)}, f32[24,768]{1,0:T(8,128)}, u32[]{:S(2)}) copy-start(f32[24,768]{1,0:T(8,128)} %param.30) | copy-start | bytes 221188
  307.3 4.0 %copy-start.9 = (f32[2,768]{1,0:T(2,128)S(1)}, f32[2,768]{1,0:T(2,128)}, u32[]{:S(2)}) copy-start(f32[2,768]{1,0:T(2,128)} %gains.5) | copy-start | bytes 18436
  307.3 4.0 %copy-start.25 = (f32[2,768]{1,0:T(2,128)S(1)}, f32[2,768]{1,0:T(2,128)}, u32[]{:S(2)}) copy-start(f32[2,768]{1,0:T(2,128)} %param.38) | copy-start | bytes 18436
  307.3 4.0 %copy-start.26 = (f32[2,768]{1,0:T(2,128)S(1)}, f32[2,768]{1,0:T(2,128)}, u32[]{:S(2)}) copy-start(f32[2,768]{1,0:T(2,128)} %param.39) | copy-start | bytes 18436
  307.3 4.7 %copy-start.27 = (f32[32,6]{0,1:T(8,128)S(1)}, f32[32,6]{0,1:T(8,128)}, u32[]{:S(2)}) copy-start(f32[32,6]{0,1:T(8,128)} %param.41) | copy-start | bytes 2308
  307.3 4.7 %copy-start.28 = (f32[32,6]{0,1:T(8,128)S(1)}, f32[32,6]{0,1:T(8,128)}, u32[]{:S(2)}) copy-start(f32[32,6]{0,1:T(8,128)} %param.42) | copy-start | bytes 2308
  312.7 5.0 %copy-start.10 = (bf16[8,256,768]{2,1,0:T(8,128)(2,1)S(1)}, bf16[8,256,768]{2,1,0:T(8,128)(2,1)}, u32[]{:S(2)}) copy-start(bf16[8,256,768]{2,1,0:T(8,128)(2,1)} %get-tuple-element.52) | copy-start | bytes 9437188

commit v2 on v0

v2 whole, which is shorter than its diff:
```python
from functools import partial
import math

import jax
import jax.numpy as jnp
import numpy as np
from jax import lax
from jax.experimental import pallas as pl
from jax.experimental.pallas import tpu as pltpu
from jax.sharding import PartitionSpec as P

DH = 64
PLEN = 250
STEP = 5
ROWS = 256
BUCKETS = 32
SPAN = 128

MESH = pl.DeviceIdType.MESH
BF = jnp.bfloat16
F32 = jnp.float32
MIB = 2**20

norm_eps = 1e-06
masked_score = -1000000000.0
beta_first = 0.5
beta_second = 0.5
adam_eps = 1e-08
decay_rate = 0.01
rate_inward = 0.015
rate_outward = 0.3
rate_expand = 0.04
rate_reduce = 0.02
rate_gains = 0.5
rate_table = 0.5


def adamw(weight, first_moment, second, gradient, step_rate):
    new_first = beta_first * first_moment + (1.0 - beta_first) * gradient
    new_second = beta_second * second + (1.0 - beta_second) * gradient * gradient
    first_hat = new_first / (1.0 - beta_first**STEP)
    second_hat = new_second / (1.0 - beta_second**STEP)
    new_weight = weight - step_rate * (
        first_hat / (jnp.sqrt(second_hat) + adam_eps) + decay_rate * weight
    )
    return (new_weight, new_first, new_second)


def distance_onehot():
    span = 2 * ROWS
    relative = np.arange(span)
    relative = np.where(relative < ROWS, relative, relative - span)
    half = BUCKETS // 2
    exact = half // 2
    distance = np.abs(relative)
    far = np.full_like(distance, exact)
    for level in range(1, half - exact):
        far += distance >= math.ceil(exact * (SPAN / exact) ** (level / (half - exact)))
    bucket = np.where(relative > 0, half, 0) + np.where(distance < exact, distance, far)
    return (bucket[:, None] == np.arange(BUCKETS)[None]).astype(np.float32)


def dot(a, b, ca=1, cb=0):
    return lax.dot_general(a, b, (((ca,), (cb,)), ((), ())), preferred_element_type=F32)


class Refs:
    pass


def run(kernel, grid, ins, outs, scratch, collective, limit, name):
    names = [i[0] for i in ins] + [o[0] for o in outs] + [s[0] for s in scratch]

    def body(*refs):
        space = Refs()
        for key, ref in zip(names, refs, strict=True):
            setattr(space, key, ref)
        kernel(space)

    results = pl.pallas_call(
        body,
        grid=grid,
        in_specs=[i[2] for i in ins],
        out_specs=[o[3] for o in outs],
        out_shape=[jax.ShapeDtypeStruct(o[1], o[2]) for o in outs],
        scratch_shapes=[s[1] for s in scratch],
        compiler_params=pltpu.CompilerParams(
            collective_id=collective, has_side_effects=True, vmem_limit_bytes=limit * MIB
        ),
        name=name,
    )(*[i[1] for i in ins])
    return dict(zip([o[0] for o in outs], results))


def whole(shape):
    return pl.BlockSpec(shape, lambda p: (0,) * len(shape), pipeline_mode=pl.Buffered(1))


def steps(first, count, shape):
    rest = (0,) * (len(shape) - 1)
    return pl.BlockSpec(shape, lambda p: (jnp.clip(p - first, 0, count - 1),) + rest)


ANY = pl.BlockSpec(memory_space=pl.ANY)


class Links:
    def __init__(self, n):
        me = lax.axis_index("dp")
        self.n, self.nz, self.me = n, n // 4, me
        x, y = lax.rem(me, 2), lax.rem(me // 2, 2)
        self.z, self.column = me // 4, lax.rem(me, 4)
        self.x_peer, self.y_peer = me + 1 - 2 * x, me + 2 - 4 * y
        self.far_peer = self.x_peer + 2 - 4 * y
        self.z_pair = self.z + 1 - 2 * lax.rem(self.z, 2)
        self.pair_peer = self.z_pair * 4 + self.column

    def z_peer(self, k):
        return lax.rem(self.z + k + self.nz, self.nz) * 4 + self.column

    def block(self, k, column_of, z=None):
        return lax.rem((self.z if z is None else z) + k, self.nz) * 4 + lax.rem(column_of, 4)

    def peers(self):
        ids = [self.x_peer, self.y_peer] + [self.z_peer(k) for k in range(1, self.nz)]
        return [{"dp": i} for i in ids]


def greet(peers):
    barrier = pltpu.get_barrier_semaphore()
    for peer in peers:
        pl.semaphore_signal(barrier, inc=1, device_id=peer, device_id_type=MESH)
    pl.semaphore_wait(barrier, len(peers))


def partner():
    return {"mp": 1 - lax.axis_index("mp")}


def cut(ref, blk, rows):
    return ref.at[pl.ds(pl.multiple_of(blk * rows, 16), rows)]


def remote(src, dst, send, recv, peer):
    return pltpu.make_async_remote_copy(
        src_ref=src,
        dst_ref=dst,
        send_sem=send,
        recv_sem=recv,
        device_id=peer,
        device_id_type=MESH,
    )


class Gather:
    def __init__(self, links, full, ss, rs):
        self.l, self.full, self.ss, self.rs = links, full, ss, rs

    def copy(self, a, role, k, blk, peer):
        ref, rows = self.full[a]
        at = cut(ref, blk, rows)
        return remote(at, at, self.ss.at[a, role, k], self.rs.at[a, role, k], {"dp": peer})

    def put(self, a, value, lanes=None):
        ref, rows = self.full[a]
        at = pl.ds(pl.multiple_of(self.l.me * rows, 16), rows)
        if lanes is None:
            ref[at] = value
        else:
            ref[at, lanes] = value

    def own(self, a):
        l = self.l
        for k in range(1, l.nz):
            self.copy(a, 0, k, l.me, l.z_peer(-k)).start()
        self.copy(a, 1, 0, l.me, l.x_peer).start()
        self.copy(a, 2, 0, l.me, l.y_peer).start()

    def along(self, a):
        l = self.l
        for k in range(1, l.nz):
            blk = l.block(k, l.me)
            self.copy(a, 0, k, blk, l.x_peer).wait_recv()
            self.copy(a, 1, k, blk, l.x_peer).start()
            self.copy(a, 2, k, blk, l.y_peer).start()

    def across(self, a):
        l = self.l
        for k in range(0, l.nz, 2):
            role, source, target = (1, l.x_peer, l.y_peer) if k % 4 == 0 else (2, l.y_peer, l.x_peer)
            blk = l.block(k, source)
            self.copy(a, role, k, blk, source).wait_recv()
            self.copy(a, 3, k, blk, target).start()

    def share(self, a):
        l = self.l
        for k in range(0, l.nz, 2):
            blk = l.block(k, l.far_peer)
            self.copy(a, 3, k, blk, l.x_peer).wait_recv()
            self.copy(a, 4, k, blk, l.pair_peer).start()

    def arrived(self, a):
        l = self.l
        for k in range(l.nz):
            if k % 4 != 0:
                self.copy(a, 1, k, l.block(k, l.x_peer), l.x_peer).wait_recv()
            if k % 4 != 2:
                self.copy(a, 2, k, l.block(k, l.y_peer), l.y_peer).wait_recv()
            if k % 2 == 0:
                self.copy(a, 4, k, l.block(k, l.far_peer, l.z_pair), l.pair_peer).wait_recv()

    def sent(self, a):
        l = self.l
        for k in range(l.nz):
            roles = (0,) * (k > 0) + (1, 2) + (3, 4) * (k % 2 == 0)
            for role in roles:
                self.copy(a, role, k, l.me, l.x_peer).wait_send()


class Scatter:
    def __init__(self, links, grads, bufs, ss, rs):
        self.l, self.grads, self.bufs, self.ss, self.rs = links, grads, bufs, ss, rs

    def part(self, a, blk):
        ref, rows = self.grads[a]
        return cut(ref, blk, rows)

    def read(self, a, blk):
        ref, rows = self.grads[a]
        return ref[pl.ds(pl.multiple_of(blk * rows, 16), rows), :].astype(F32)

    def copy(self, a, role, k, src, slot, peer):
        dst = self.bufs[a].at[slot, k]
        return remote(src, dst, self.ss.at[a, role, k], self.rs.at[a, role, k], {"dp": peer})

    def arrive(self, a, role, k, slot):
        self.copy(a, role, k, self.part(a, 0), slot, self.l.x_peer).wait_recv()

    def far(self, a):
        l = self.l
        for k in range(l.nz):
            peer = l.y_peer if k % 2 == 0 else l.x_peer
            self.copy(a, 0, k, self.part(a, l.block(k, l.far_peer)), 0, peer).start()

    def plain(self, a):
        l = self.l
        for k in range(l.nz):
            if k % 2 == 1:
                self.copy(a, 1, k, self.part(a, l.block(k, l.x_peer)), 2, l.x_peer).start()
            else:
                self.copy(a, 2, k, self.part(a, l.block(k, l.y_peer)), 4, l.y_peer).start()

    def near(self, a):
        l = self.l
        for k in range(l.nz):
            self.arrive(a, 0, k, 0)
            role, peer, slot = (1, l.x_peer, 1) if k % 2 == 0 else (2, l.y_peer, 3)
            mine = self.read(a, l.block(k, peer)) + self.bufs[a][0, k].astype(F32)
            self.bufs[a][slot, k] = mine.astype(BF)
            self.copy(a, role, k, self.bufs[a].at[slot, k], slot + 1, peer).start()

    def along(self, a, kept):
        l = self.l
        for k in list(range(1, l.nz)) + [0]:
            self.arrive(a, 1, k, 2)
            self.arrive(a, 2, k, 4)
            mine = (
                self.read(a, l.block(k, l.me))
                + self.bufs[a][2, k].astype(F32)
                + self.bufs[a][4, k].astype(F32)
            )
            if k == 0:
                kept[...] = mine
            else:
                self.bufs[a][5, k] = mine.astype(BF)
                self.copy(a, 3, k, self.bufs[a].at[5, k], 6, l.z_peer(k)).start()

    def total(self, a, kept):
        total = kept[...]
        for k in range(1, self.l.nz):
            self.arrive(a, 3, k, 6)
            total += self.bufs[a][6, k].astype(F32)
        return total

    def sent(self, a):
        for k in range(self.l.nz):
            for role in (0, 1, 2) + (3,) * (k > 0):
                self.copy(a, role, k, self.part(a, 0), 0, self.l.x_peer).wait_send()


class Swap:
    def __init__(self, mine, theirs, ss, rs):
        self.mine, self.theirs, self.ss, self.rs = mine, theirs, ss, rs

    def copy(self, slot):
        return remote(
            self.mine.at[slot], self.theirs.at[slot], self.ss.at[slot], self.rs.at[slot], partner()
        )

    def put(self, p, value):
        self.mine[lax.rem(p, 2)] = value.astype(BF)

    def send(self, p):
        self.copy(lax.rem(p, 2)).start()

    def take(self, p):
        slot = lax.rem(p, 2)
        self.copy(slot).wait()
        return self.mine[slot].astype(F32) + self.theirs[slot].astype(F32)


def swap_scratch(name, d):
    return [
        (name + "_mine", pltpu.VMEM((2, ROWS, d), BF)),
        (name + "_theirs", pltpu.VMEM((2, ROWS, d), BF)),
        (name + "_ss", pltpu.SemaphoreType.DMA((2,))),
        (name + "_rs", pltpu.SemaphoreType.DMA((2,))),
    ]


def swap_of(r, name):
    return Swap(*(getattr(r, name + part) for part in ("_mine", "_theirs", "_ss", "_rs")))


gelu_root = math.sqrt(2.0 / math.pi)
gelu_cube = 0.044715
WINDOW = 272


def inverse_rms(v):
    return lax.rsqrt(jnp.mean(v * v, axis=-1, keepdims=True) + norm_eps)


def window_start(p, total):
    return min(p * PLEN // 16 * 16, total - WINDOW)


def align(source, target, windows, sems, passages):
    total = source.shape[0]

    def fetch(p):
        return pltpu.make_async_copy(
            source.at[pl.ds(window_start(p, total), WINDOW)], windows.at[p % 2], sems.at[p % 2]
        )

    def start():
        fetch(0).start()
        fetch(1).start()

    def move(first, last):
        for p in range(first, last):
            fetch(p).wait()
            off = p * PLEN - window_start(p, total)
            rows = windows[p % 2].astype(F32)[off : off + PLEN]
            pad = jnp.zeros((ROWS - PLEN, rows.shape[1]), F32)
            target[p] = jnp.concatenate([rows, pad], axis=0).astype(BF)
            if p + 2 < passages:
                fetch(p + 2).start()

    return start, move


def forward_kernel(n, passages, heads, direct, parts, r):
    s = pl.program_id(0)
    width = heads * DH
    count = passages
    att, out, back_in = (swap_of(r, name) for name in ("att", "out", "in"))
    if direct:
        links = Links(n)
        full = [
            (r.wi, r.wi.shape[0] // n), (r.wo_wide, r.wo_wide.shape[0] // n),
            (r.we, r.we.shape[0] // n), (r.wr, r.wr.shape[0] // n),
        ]
        gather = Gather(links, full, r.g_ss, r.g_rs)
    tok_start, tok_move = align(r.tokens, r.tok, r.tok_window, r.tok_sem, passages)
    cot_start, cot_move = align(r.cotangent, r.cot, r.cot_window, r.cot_sem, passages)

    def local(src, dst, i):
        return pltpu.make_async_copy(src, dst, r.out_sem.at[i])

    @pl.when(s == 0)
    def _():
        tok_start()
        cot_start()
        if direct:
            for c in range(3):
                gather.put(0, r.own_i[c].astype(BF), slice(c * width, (c + 1) * width))
            rows_o = r.own_o.shape[0]
            pad = jnp.zeros((full[1][1] - rows_o, r.own_o.shape[1]), F32)
            gather.put(1, jnp.concatenate([r.own_o[...], pad], axis=0).astype(BF))
            gather.put(2, r.own_e[...].astype(BF))
            gather.put(3, r.own_r[...].astype(BF))
            greet(links.peers() + [partner()])
            gather.own(0)
            gather.own(1)
        else:
            greet([partner()])
        r.acc_r[...] = jnp.zeros_like(r.acc_r)
        r.acc_e[...] = jnp.zeros_like(r.acc_e)
        r.acc_o[...] = jnp.zeros_like(r.acc_o)
        r.gain_grad[...] = jnp.zeros_like(r.gain_grad)
        tok_move(0, passages // 2)
        if direct:
            gather.along(0)
            gather.own(2)
        tok_move(passages // 2, passages)
        local(r.tok, r.tok_out, 0).start()
        if direct:
            gather.across(0)
        cot_move(0, passages // 2)
        if direct:
            gather.along(1)
            gather.own(3)
            gather.share(0)
        cot_move(passages // 2, passages)
        for h in range(heads):
            rows = jnp.broadcast_to(r.line[h : h + 1, :], (ROWS, 2 * ROWS))
            r.bias[h] = pltpu.roll(rows, 0, 1, stride=1, stride_axis=0)[:, :ROWS]
        if direct:
            gather.across(1)
            gather.arrived(0)

    @pl.when(s < count)
    def _():
        x = r.tok[s].astype(F32)
        normed = (x * inverse_rms(x) * r.gains[0:1, :]).astype(BF)
        r.normed[0] = normed
        r.proj[0] = dot(normed, r.wi[...]).astype(BF)
        masked = r.mask[pl.ds(s, 1), :]
        for h in range(heads):
            q = r.proj[0, :, h * DH : (h + 1) * DH]
            k = r.proj[0, :, width + h * DH : width + (h + 1) * DH]
            v = r.proj[0, :, 2 * width + h * DH : 2 * width + (h + 1) * DH]
            sc = dot(q, k, 1, 1) + r.bias[h] + masked
            e = jnp.exp(sc - jnp.max(sc, axis=-1, keepdims=True))
            a = (e * (1.0 / jnp.sum(e, axis=-1, keepdims=True))).astype(BF)
            r.probs[0, h] = a
            r.ctx[s, :, h * DH : (h + 1) * DH] = dot(a, v).astype(BF)

    if direct:

        @pl.when(s == 0)
        def _():
            gather.share(1)
            gather.arrived(1)
            rows = r.own_o.shape[0]
            padded = full[1][1]
            for d in range(n):
                block = r.wo_wide[d * padded : (d + 1) * padded, :].astype(F32)
                r.wo_f32[d * rows : (d + 1) * rows, :] = block[:rows]
            r.wo[...] = r.wo_f32[...].astype(BF)

        for at, what, a in (
            (1, gather.along, 2), (2, gather.across, 2), (3, gather.share, 2),
            (4, gather.along, 3), (5, gather.across, 3), (6, gather.share, 3),
        ):
            pl.when(s == at)(partial(what, a))

        @pl.when(s == count - 1)
        def _():
            local(r.wi, r.wi_out, 1).start()
            local(r.wo, r.wo_out, 2).start()

    def settle(p):
        r.hidden[p] = r.tok[p].astype(F32) + att.take(p)

    @pl.when(s < count)
    def _():
        att.put(s, dot(r.ctx[s], r.wo[...]))

    @pl.when((s > 0) & (s < count))
    def _():
        settle(s - 1)

    @pl.when(s < count)
    def _():
        att.send(s)

    p = s - count

    @pl.when(s == count)
    def _():
        if direct:
            gather.arrived(2)
            gather.arrived(3)

    @pl.when((s >= count) & (s < 2 * count))
    def _():
        h = r.hidden[p]
        normed = (h * inverse_rms(h) * r.gains[1:2, :]).astype(BF)
        c = r.cot[p]
        step = r.we.shape[1] // parts
        reduced = None
        for i in range(parts):
            at = slice(i * step, (i + 1) * step)
            u = dot(normed, r.we[:, at])
            square = u * u
            t = jnp.tanh(u * (gelu_root + (gelu_root * gelu_cube) * square))
            half = 0.5 * (1.0 + t)
            act = (u * half).astype(BF)
            slope = half + (0.5 * u) * (1.0 - t * t) * (
                gelu_root + (3.0 * gelu_root * gelu_cube) * square
            )
            back = (dot(c, r.wr[at, :], 1, 1) * slope).astype(BF)
            r.acc_r[at, :] += dot(act, c, 0, 0)
            r.acc_e[:, at] += dot(normed, back, 0, 0)
            r_part = dot(act, r.wr[at, :])
            n_part = dot(back, r.we[:, at], 1, 1)
            if reduced is not None:
                r_part, n_part = reduced[0] + r_part, reduced[1] + n_part
            reduced = (r_part, n_part)
        out.put(p, reduced[0])
        back_in.put(p, reduced[1])

    @pl.when(s == count)
    def _():
        settle(count - 1)

    @pl.when(s == 2 * count - 1)
    def _():
        r.reduce_grad[...] = r.acc_r[...].astype(BF)
        r.expand_grad[...] = r.acc_e[...].astype(BF)

    @pl.when(s > count)
    def _():
        last = p - 1
        h = r.hidden[last]
        r.layer[0] = (h + out.take(last)).astype(BF)
        grad = back_in.take(last)
        inv = inverse_rms(h)
        zed = r.gains[1:2, :] * grad
        hr = h * inv
        r.gain_grad[0:1, :] += jnp.sum(grad * hr, axis=0, keepdims=True)
        inner = jnp.mean(zed * hr, axis=-1, keepdims=True)
        hidden_grad = r.cot[last].astype(F32) + inv * (zed - hr * inner)
        r.hidden_grad[0] = hidden_grad
        r.acc_o[...] += dot(r.ctx[last], hidden_grad.astype(BF), 0, 0)

    @pl.when((s >= count) & (s < 2 * count))
    def _():
        out.send(p)
        back_in.send(p)

    @pl.when(s == 2 * count)
    def _():
        rows = r.acc_o.shape[0] // (n if direct else 1)
        padded = rows + -rows % 16
        for b in range(n if direct else 1):
            part = r.acc_o[b * rows : (b + 1) * rows, :]
            if padded > rows:
                part = jnp.concatenate([part, jnp.zeros((padded - rows, part.shape[1]), F32)], axis=0)
            r.outward_grad[b * padded : (b + 1) * padded, :] = part.astype(BF)
        local(r.tok, r.tok_out, 0).wait()
        if direct:
            local(r.wi, r.wi_out, 1).wait()
            local(r.wo, r.wo_out, 2).wait()
            for a in range(4):
                gather.sent(a)


def forward(n, passages, heads, direct, tokens, cotangent, mask, gains, line, weights):
    d = tokens.shape[1]
    width = heads * DH
    one = (1, ROWS, d)
    fixed = lambda p: (0, 0)
    wide = lambda shape: pl.BlockSpec(shape, fixed, pipeline_mode=pl.Buffered(1))
    late, first = passages + 1, 0
    ins = [("tokens", tokens, ANY), ("cotangent", cotangent, ANY)]
    ins += [(k, v, whole(v.shape)) for k, v in (("mask", mask), ("gains", gains), ("line", line))]
    ins += [(k, v, whole(v.shape)) for k, v in weights.items()]
    if direct:
        units = weights["own_r"].shape[0] * n
        padded = weights["own_o"].shape[0]
        padded += -padded % 16
    else:
        units = weights["wr"].shape[0]
    outs = [
        ("proj", (passages, ROWS, 3 * width), BF, steps(first, passages, (1, ROWS, 3 * width))),
        ("probs", (passages, heads, ROWS, ROWS), BF, steps(first, passages, (1, heads, ROWS, ROWS))),
        ("normed", (passages, ROWS, d), BF, steps(first, passages, one)),
        ("tok_out", (passages, ROWS, d), BF, ANY),
        ("layer", (passages, ROWS, d), BF, steps(late, passages, one)),
        ("hidden_grad", (passages, ROWS, d), F32, steps(late, passages, one)),
        ("reduce_grad", (units, d), BF, wide((units, d))),
        ("expand_grad", (d, units), BF, wide((d, units))),
        ("gain_grad", (8, d), F32, wide((8, d))),
    ]
    rows_o = padded * n if direct else width
    outs.append(("outward_grad", (rows_o, d), BF, wide((rows_o, d))))
    scratch = [
        ("tok", pltpu.VMEM((passages, ROWS, d), BF)),
        ("cot", pltpu.VMEM((passages, ROWS, d), BF)),
        ("tok_window", pltpu.VMEM((2, WINDOW, d), BF)),
        ("cot_window", pltpu.VMEM((2, WINDOW, d), BF)),
        ("tok_sem", pltpu.SemaphoreType.DMA((2,))),
        ("cot_sem", pltpu.SemaphoreType.DMA((2,))),
        ("out_sem", pltpu.SemaphoreType.DMA((3,))),
        ("bias", pltpu.VMEM((heads, ROWS, ROWS), F32)),
        ("ctx", pltpu.VMEM((passages, ROWS, width), BF)),
        ("hidden", pltpu.VMEM((passages, ROWS, d), F32)),
        ("acc_r", pltpu.VMEM((units, d), F32)),
        ("acc_e", pltpu.VMEM((d, units), F32)),
        ("acc_o", pltpu.VMEM((width, d), F32)),
    ]
    for name in ("att", "out", "in"):
        scratch += swap_scratch(name, d)
    if direct:
        outs += [("wi_out", (d, 3 * width), BF, ANY), ("wo_out", (width, d), BF, ANY)]
        scratch += [
            ("wi", pltpu.VMEM((d, 3 * width), BF)),
            ("wo", pltpu.VMEM((width, d), BF)),
            ("wo_f32", pltpu.VMEM((width, d), F32)),
            ("wo_wide", pltpu.VMEM((n * padded, d), BF)),
            ("we", pltpu.VMEM((d, units), BF)),
            ("wr", pltpu.VMEM((units, d), BF)),
            ("g_ss", pltpu.SemaphoreType.DMA((4, 5, n // 4))),
            ("g_rs", pltpu.SemaphoreType.DMA((4, 5, n // 4))),
        ]
    kernel = partial(forward_kernel, n, passages, heads, direct, 3)
    return run(kernel, (2 * passages + 1,), ins, outs, scratch, 1, 62, "forward")


def backward_kernel(n, passages, heads, direct, r):
    s = pl.program_id(0)
    width = heads * DH
    swap = swap_of(r, "in")
    if direct:
        links = Links(n)
        names = ("r", "e", "o", "i")
        grads = [(g, g.shape[0] // n) for g in (r.reduce_grad, r.expand_grad, r.outward_grad, r.inward_grad)]
        bufs = [getattr(r, "buf_" + k) for k in names]
        kept = [getattr(r, "kept_" + k) for k in names]
        sums = Scatter(links, grads, bufs, r.s_ss, r.s_rs)

    @pl.when(s == 0)
    def _():
        if direct:
            greet(links.peers() + [partner()])
            for a in range(3):
                sums.far(a)
            for a in range(3):
                sums.plain(a)
        else:
            greet([partner()])
        r.acc_i[...] = jnp.zeros_like(r.acc_i)
        r.acc_s[...] = jnp.zeros_like(r.acc_s)
        r.gain_one[...] = jnp.zeros_like(r.gain_one)

    if direct:
        for at, what, arrays in ((2, "near", (0,)), (3, "near", (1, 2)), (5, "along", (0,)), (6, "along", (1, 2))):

            @pl.when(s == at)
            def _():
                for a in arrays:
                    if what == "near":
                        sums.near(a)
                    else:
                        sums.along(a, kept[a])

    @pl.when(s < passages)
    def _():
        above = r.hgrad[0].astype(BF)
        dctx = dot(above, r.wo[...], 1, 1).astype(BF)
        for h in range(heads):
            at = [slice(c * width + h * DH, c * width + (h + 1) * DH) for c in range(3)]
            q, k, v = (r.proj[0, :, c] for c in at)
            dc = dctx[:, h * DH : (h + 1) * DH]
            a = r.probs[0, h]
            r.dproj[:, at[2]] = dot(a, dc, 0, 0).astype(BF)
            dp = dot(dc, v, 1, 1)
            a = a.astype(F32)
            centre = jnp.sum(a * dp, axis=-1, keepdims=True)
            ds = (a * (dp - centre)).astype(BF)
            r.acc_s[h] += ds.astype(F32)
            r.dproj[:, at[0]] = dot(ds, k).astype(BF)
            r.dproj[:, at[1]] = dot(ds, q, 0, 0).astype(BF)
        r.acc_i[...] += dot(r.normed[0], r.dproj[...], 0, 0)
        swap.put(s, dot(r.dproj[...], r.wi[...], 1, 1))

    @pl.when(s == passages - 1)
    def _():
        r.inward_grad[...] = r.acc_i[...].astype(BF)
        if direct:
            sums.far(3)
            sums.plain(3)

    @pl.when(s > 0)
    def _():
        last = s - 1
        x = r.tok_prev[0].astype(F32)
        grad = swap.take(last)
        inv = inverse_rms(x)
        zed = r.gains[0:1, :] * grad
        xr = x * inv
        r.gain_one[0:1, :] += jnp.sum(grad * xr, axis=0, keepdims=True)
        inner = jnp.mean(zed * xr, axis=-1, keepdims=True)
        r.input_grad[0] = r.hgrad_prev[0] + inv * (zed - xr * inner)

    @pl.when(s < passages)
    def _():
        swap.send(s)

    @pl.when(s == passages)
    def _():
        small = r.small
        small[...] = jnp.zeros_like(small)
        small[0:1, :] = r.gain_one[0:1, :]
        small[1:2, :] = r.gain_two[0:1, :]
        for h in range(heads):
            rows = jnp.concatenate([r.acc_s[h], jnp.zeros((ROWS, ROWS), F32)], axis=1)
            while rows.shape[0] > 1:
                half = rows.shape[0] // 2
                rows = rows[:half] + pltpu.roll(rows[half:], 2 * ROWS - half, 1)
            small[8 + h : 9 + h, : 2 * ROWS] = rows
        if not direct:
            r.small_out[...] = small[...]
            return
        finish(n, heads, links, sums, kept, r)


def finish(n, heads, links, sums, kept, r):
    nz = links.nz
    width = heads * DH
    small, small_z, small_xy = r.small, r.small_z, r.small_xy

    def small_copy(role, src, dst, peer):
        return remote(src, dst, r.m_ss.at[role], r.m_rs.at[role], {"dp": peer})

    def update(key, gradient, rate, index=None):
        pick = (lambda ref: ref[...]) if index is None else (lambda ref: ref[index])
        refs = [getattr(r, key + part) for part in ("_w", "_m", "_v")]
        new = adamw(*(pick(ref) for ref in refs), gradient, rate)
        targets = [getattr(r, key + part) for part in ("_nw", "_nm", "_nv")]
        if hasattr(r, key + "_nc"):
            targets.append(getattr(r, key + "_nc"))
            new = new + (new[0].astype(BF),)
        for target, value in zip(targets, new, strict=True):
            if index is None:
                target[...] = value
            else:
                target[index] = value

    small_z[links.z] = small[...]
    for k in range(1, nz):
        small_copy(k, small, small_z.at[links.z], links.z_peer(k)).start()
    update("r", sums.total(0, kept[0]), rate_reduce)
    sums.near(3)
    for k in range(1, nz):
        small_copy(k, small, small_z.at[lax.rem(links.z - k + nz, nz)], links.x_peer).wait()
    total = small_z[0]
    for k in range(1, nz):
        total += small_z[k]
    small_xy[0] = total
    small_copy(0, small_xy.at[0], small_xy.at[1], links.x_peer).start()
    update("e", sums.total(1, kept[1]), rate_expand)
    update("o", sums.total(2, kept[2])[: r.o_w.shape[0]], rate_outward)
    small_copy(0, small_xy.at[0], small_xy.at[1], links.x_peer).wait()
    small_xy[2] = small_xy[0] + small_xy[1]
    small_copy(nz, small_xy.at[2], small_xy.at[3], links.y_peer).start()
    sums.along(3, kept[3])
    small_copy(nz, small_xy.at[2], small_xy.at[3], links.y_peer).wait()
    total = small_xy[2] + small_xy[3]
    update("g", total[:2], rate_gains)
    table_grad = lax.dot_general(
        r.onehot[...], total[8:, : 2 * ROWS], (((0,), (1,)), ((), ())),
        precision=lax.Precision.HIGHEST, preferred_element_type=F32,
    )
    update("t", table_grad[:, :heads], rate_table)
    inward = sums.total(3, kept[3])
    for c in range(3):
        update("i", inward[:, c * width : (c + 1) * width], rate_inward, c)
    for a in range(4):
        sums.sent(a)


def backward(n, passages, heads, direct, f, gains, wi, wo, onehot, states):
    d = f["normed"].shape[-1]
    width = heads * DH
    one = (1, ROWS, d)
    now = lambda shape: steps(0, passages, shape)
    lag = lambda shape: steps(1, passages, shape)
    hgrad, tok = f["hidden_grad"], f["tok_out"]
    ins = [
        ("hgrad", hgrad, now(one)),
        ("hgrad_prev", hgrad, lag(one)),
        ("tok_prev", tok, lag(one)),
        ("normed", f["normed"], now(one)),
        ("proj", f["proj"], now((1, ROWS, 3 * width))),
        ("probs", f["probs"], now((1, heads, ROWS, ROWS))),
    ]
    fixed = [("gains", gains), ("wi", wi), ("wo", wo), ("gain_two", f["gain_grad"])]
    outs = [("input_grad", (passages, ROWS, d), F32, lag(one))]
    scratch = [
        ("acc_i", pltpu.VMEM((d, 3 * width), F32)),
        ("acc_s", pltpu.VMEM((heads, ROWS, ROWS), F32)),
        ("dproj", pltpu.VMEM((ROWS, 3 * width), BF)),
        ("gain_one", pltpu.VMEM((8, d), F32)),
        ("small", pltpu.VMEM((16, d), F32)),
    ] + swap_scratch("in", d)
    if direct:
        nz = n // 4
        fixed += [("onehot", onehot)]
        fixed += [(k, f[k]) for k in ("reduce_grad", "expand_grad", "outward_grad")]
        for key, (w, m, v) in states.items():
            fixed += [(key + "_w", w), (key + "_m", m), (key + "_v", v)]
            for part in ("_nw", "_nm", "_nv"):
                outs.append((key + part, w.shape, F32, whole(w.shape)))
            if key not in "gt":
                outs.append((key + "_nc", w.shape, BF, whole(w.shape)))
        blocks = {
            "r": (f["reduce_grad"].shape[0] // n, d),
            "e": (d // n, f["expand_grad"].shape[1]),
            "o": (f["outward_grad"].shape[0] // n, d),
            "i": (d // n, 3 * width),
        }
        scratch.append(("inward_grad", pltpu.VMEM((d, 3 * width), BF)))
        for key, shape in blocks.items():
            scratch.append(("buf_" + key, pltpu.VMEM((7, nz) + shape, BF)))
            scratch.append(("kept_" + key, pltpu.VMEM(shape, F32)))
        scratch += [
            ("small_z", pltpu.VMEM((nz, 16, d), F32)),
            ("small_xy", pltpu.VMEM((4, 16, d), F32)),
            ("s_ss", pltpu.SemaphoreType.DMA((4, 4, nz))),
            ("s_rs", pltpu.SemaphoreType.DMA((4, 4, nz))),
            ("m_ss", pltpu.SemaphoreType.DMA((nz + 1,))),
            ("m_rs", pltpu.SemaphoreType.DMA((nz + 1,))),
        ]
    else:
        outs.append(("inward_grad", (d, 3 * width), BF, whole((d, 3 * width))))
        outs.append(("small_out", (16, d), F32, whole((16, d))))
    ins += [(k, v, whole(v.shape)) for k, v in fixed]
    kernel = partial(backward_kernel, n, passages, heads, direct)
    return run(kernel, (passages + 1,), ins, outs, scratch, 2, 62, "backward")


def shards(
    n,
    tokens,
    cotangent,
    buckets,
    inward_master,
    inward_first,
    inward_second,
    outward_master,
    outward_first,
    outward_second,
    expand_master,
    expand_first,
    expand_second,
    reduce_master,
    reduce_first,
    reduce_second,
    gains_master,
    gains_first,
    gains_second,
    table_master,
    table_first,
    table_second,
):
    passages = tokens.shape[0] // PLEN
    heads = inward_master.shape[2] // DH
    width = heads * DH
    states = {
        "i": tuple(a.transpose(1, 0, 2) for a in (inward_master, inward_first, inward_second)),
        "o": (outward_master, outward_first, outward_second),
        "e": (expand_master, expand_first, expand_second),
        "r": (reduce_master, reduce_first, reduce_second),
        "g": (gains_master, gains_first, gains_second),
        "t": (table_master, table_first, table_second),
    }
    direct = (
        n % 8 == 0
        and inward_master.shape[0] % 16 == 0
        and reduce_master.shape[0] % 16 == 0
        and outward_master.shape[0] % 8 == 0
    )
    if direct:
        weights = {"own_" + key: states[key][0] for key in "ioer"}
    else:
        masters = {
            "wi": inward_master.reshape(-1, 3 * width),
            "wo": outward_master,
            "we": expand_master,
            "wr": reduce_master,
        }
        weights = {
            key: lax.all_gather(w.astype(BF), "dp", axis=0, tiled=True)
            for key, w in masters.items()
        }
    mask = jnp.where(buckets[:, 0, :] < BUCKETS, 0.0, masked_score)
    mask = jnp.pad(mask, ((0, -passages % 8), (0, ROWS - PLEN)), constant_values=masked_score)
    onehot = jnp.asarray(distance_onehot())
    line = lax.dot_general(
        table_master, onehot, (((0,), (1,)), ((), ())), precision=lax.Precision.HIGHEST
    )
    line = jnp.pad(line, ((0, -heads % 8), (0, 0)))
    f = forward(n, passages, heads, direct, tokens, cotangent, mask, gains_master, line, weights)
    wi, wo = (f["wi_out"], f["wo_out"]) if direct else (weights["wi"], weights["wo"])
    b = backward(n, passages, heads, direct, f, gains_master, wi, wo, onehot, states)
    layer_out = f["layer"][:, :PLEN].reshape(tokens.shape)
    input_grad = b["input_grad"][:, :PLEN].reshape(tokens.shape)
    new = {}
    if direct:
        for key in "ioergt":
            parts = ("_nw", "_nm", "_nv") + ("_nc",) * (key not in "gt")
            new[key] = [b[key + part] for part in parts]
        new["i"] = [a.transpose(1, 0, 2) for a in new["i"]]
    else:
        grads = {
            "i": b["inward_grad"], "o": f["outward_grad"], "e": f["expand_grad"], "r": f["reduce_grad"],
        }
        sums = {
            key: lax.psum_scatter(g.astype(F32), "dp", scatter_dimension=0, tiled=True)
            for key, g in grads.items()
        }
        small = lax.psum(b["small_out"], "dp")
        sums["i"] = sums["i"].reshape(inward_master.shape)
        sums["g"] = small[:2]
        sums["t"] = lax.dot_general(
            onehot, small[8 : 8 + heads, : 2 * ROWS], (((0,), (1,)), ((), ())),
            precision=lax.Precision.HIGHEST,
        )
        states["i"] = (inward_master, inward_first, inward_second)
        rates = {
            "i": rate_inward, "o": rate_outward, "e": rate_expand,
            "r": rate_reduce, "g": rate_gains, "t": rate_table,
        }
        for key in "ioergt":
            new[key] = list(adamw(*states[key], sums[key], rates[key]))
            if key not in "gt":
                new[key].append(new[key][0].astype(BF))
    outputs = [layer_out, input_grad]
    for key in "ioergt":
        outputs += new[key]
    return tuple(outputs)


def solution(mesh):
    rows = P("dp", None)
    inward = P("dp", None, "mp")
    tall = P(("mp", "dp"), None)
    wide = P("dp", "mp")
    table = P(None, "mp")
    return jax.shard_map(
        partial(shards, mesh.shape["dp"]),
        mesh=mesh,
        in_specs=(rows, rows, P("dp", None, None))
        + (inward,) * 3
        + (tall,) * 3
        + (wide,) * 3
        + (tall,) * 3
        + (P(),) * 3
        + (table,) * 3,
        out_specs=(rows, rows)
        + (inward,) * 4
        + (tall,) * 4
        + (wide,) * 4
        + (tall,) * 4
        + (P(),) * 3
        + (table,) * 3,
        check_vma=False,
    )
```

time: 1070 us -> 261 us (0.24)
  waiting for transfers between devices: 549 us -> 0 us
  Pallas kernels: 0 us -> 229 us
  matrix products: 201 us -> 1.28 us
  blocking collectives: 127 us -> 0 us
  local copies, waits for them, and re-layouts: 114 us -> 28.6 us
  other arithmetic: 58.4 us -> 0.7 us
  between operations: 14.5 us -> 0.86 us
    reduce_scatter x4 -> x0, waiting for transfers between devices: 311 us -> none  [the longest x1 136 us: shards(): lax.psum_scatter(reduce_grad, 'dp', scatter_dimension=0, tiled=True)]
    pallas_call x0 -> x2, Pallas kernels: none -> 229 us  [run(): pl.pallas_call(body, grid=grid, in_specs=[i[2] for i in ins], out_specs=[...]
    dot_general x52 -> x1, matrix products: 201 us -> 1.28 us  [shards(): lax.dot_general(table_master, onehot, (((0,), (1,)), ((), ())), precision...]
    all_gather x3 -> x0, waiting for transfers between devices: 136 us -> none  [the longest x1 62.2 us: shards(): lax.all_gather(reduce_master.astype(jnp.bfloat16), 'dp', axis=0, tiled=True)]
    psum x4 -> x0, waiting for transfers between devices: 103 us -> none  [the longest x1 31.6 us: shards(): normed_grad = lax.psum(normed_terms, 'mp')]
    psum x1 -> x0, blocking collectives: 77.5 us -> none  [shards(): lax.psum((jnp.stack([gain_one_grad, gain_two_grad]), table_grad), 'dp')]
    all_gather x1 -> x0, blocking collectives: 49.1 us -> none  [shards(): lax.all_gather(outward_master.astype(jnp.bfloat16), 'dp', axis=0, tiled=T...]
    another operation x10 -> x0, local copies, waits for them, and re-layouts: 21.8 us -> none  [the longest x6 13.9 us: shards(): jnp.stack([query_grad, key_grad, value_grad], axis=3)]
  transfers between devices with their start and end apart: 11 -> 0, of which waited for: 10 -> 0; matrix products, arithmetic and copies ran while one was open for 17% -> 0% of each run, Pallas kernels for 0% -> 0%
where the time goes in v2:
time: 261 us
  Pallas kernels  229 us (88%)
  local copies, waits for them, and re-layouts  28.6 us (11%)
    pallas_call x2, Pallas kernels, run(): pl.pallas_call(body, grid=grid, in_specs=[i[2] for i in ins], out_specs=[...  229 us
    unnamed x69, local copies, waits for them, and re-layouts  18.8 us

profile of v2, /device:TPU:0, one launch (start us, length us, event | category | flops | bytes accessed | tf_op | source)
XLA Modules:
  0.0 260.6 jit_solution(3215507614361886622)
XLA Ops:
  0.7 0.7 select_bitcast_fusion
  1.4 0.6 pad.8.refs_2_
  2.0 1.4 copy.53.refs_30_
  3.3 1.4 copy.54.refs_31_
  4.7 1.3 convolution_bitcast_fusion
  6.0 0.6 pad.9.refs_4_
  6.6 1.4 copy.52.refs_29_
  8.0 131.9 %forward.1 = (bf16[8,256,1152]{2,1,0:T(8,128)(2,1)}, bf16[8,6,256,256]{3,2,1,0:T(8,128)(2,1)}, bf16[8,256,768]{2,1,0:T(8,128)(2,1)}, bf16[8,256,768]{2,1,0:T(8,1...) custom-call(bf16[2000,768]{1,0:T(8,128)(2,1)} %refs_0_.1, ...), custom_call_target="tpu_custom_call" | custom-call | tf_op jit(solution)/shard_map/forward/pallas_call | solution.py:80
  139.9 3.5 %reshape.59 = bf16[2000,768]{1,0:T(8,128)(2,1)} reshape(bf16[8,250,768]{2,1,0:T(8,128)(2,1)} %bitcast.16) | data formatting | bytes 6144000 | tf_op jit(solution)/shard_map/reshape | solution.py:900
  143.4 97.3 %backward.1 = (f32[8,256,768]{2,1,0:T(8,128)}, f32[3,48,384]{2,1,0:T(8,128)}, f32[3,48,384]{2,1,0:T(8,128)}, f32[3,48,384]{2,1,0:T(8,128)}, bf16[3,48,384]{2,1,0...) custom-call(f32[8,256,768]{2,1,0:T(8,128)} %get-tuple-element.60.ref, ...), custom_call_target="tpu_custom_call" | custom-call | tf_op jit(solution)/shard_map/backward/pallas_call | solution.py:80
  240.8 5.1 %reshape.60 = f32[2000,768]{1,0:T(8,128)} reshape(f32[8,250,768]{2,1,0:T(8,128)} %bitcast.15) | data formatting | bytes 12288000 | tf_op jit(solution)/shard_map/reshape | solution.py:901
  245.9 0.7 copy.55
  246.6 0.7 copy.56
  247.2 0.7 copy.57
  247.9 0.7 copy.77
  248.6 0.7 copy.78
  249.3 0.7 copy.79
  250.0 0.6 copy.80
  250.6 0.6 copy.81
  251.2 0.6 copy.82
  251.9 0.6 copy.83
  252.5 0.6 copy.84
  253.1 0.7 copy.85
  253.9 0.7 copy.86
  254.6 0.7 copy.87
  255.3 0.7 copy.88
  255.9 0.7 copy.89
  256.7 0.7 copy.90
  257.4 0.7 copy.91
  258.1 0.7 copy.92
  259.4 0.6 copy.94
  260.0 0.6 copy.95
  (45 shorter events, 0.7 us)
Async XLA Ops:
  240.6 5.3 %copy-start.18 = (f32[32,6]{1,0:T(8,128)S(1)}, f32[32,6]{1,0:T(8,128)}, u32[]{:S(2)}) copy-start(f32[32,6]{1,0:T(8,128)} %get-tuple-element.139) | copy-start | bytes 2308
  240.6 5.9 %copy-start.17 = (f32[32,6]{1,0:T(8,128)S(1)}, f32[32,6]{1,0:T(8,128)}, u32[]{:S(2)}) copy-start(f32[32,6]{1,0:T(8,128)} %get-tuple-element.140) | copy-start | bytes 2308
  240.6 6.6 %copy-start.16 = (f32[32,6]{1,0:T(8,128)S(1)}, f32[32,6]{1,0:T(8,128)}, u32[]{:S(2)}) copy-start(f32[32,6]{1,0:T(8,128)} %get-tuple-element.141) | copy-start | bytes 2308
  240.7 7.2 %copy-start.8 = (f32[3,48,384]{2,1,0:T(8,128)S(1)}, f32[3,48,384]{2,1,0:T(8,128)}, u32[]{:S(2)}) copy-start(f32[3,48,384]{2,1,0:T(8,128)} %get-tuple-element.72) | copy-start | bytes 663556
  240.7 7.9 %copy-start.7 = (f32[3,48,384]{2,1,0:T(8,128)S(1)}, f32[3,48,384]{2,1,0:T(8,128)}, u32[]{:S(2)}) copy-start(f32[3,48,384]{2,1,0:T(8,128)} %get-tuple-element.73) | copy-start | bytes 663556
  240.7 8.6 %copy-start.6 = (f32[3,48,384]{2,1,0:T(8,128)S(1)}, f32[3,48,384]{2,1,0:T(8,128)}, u32[]{:S(2)}) copy-start(f32[3,48,384]{2,1,0:T(8,128)} %get-tuple-element.74) | copy-start | bytes 663556
  240.7 9.3 %copy-start.11 = (bf16[3,48,384]{2,1,0:T(8,128)(2,1)S(1)}, bf16[3,48,384]{2,1,0:T(8,128)(2,1)}, u32[]{:S(2)}) copy-start(bf16[3,48,384]{2,1,0:T(8,128)(2,1)} %get-tuple-element.75) | copy-start | bytes 331780
  240.7 9.9 %copy-start.14 = (f32[24,768]{1,0:T(8,128)S(1)}, f32[24,768]{1,0:T(8,128)}, u32[]{:S(2)}) copy-start(f32[24,768]{1,0:T(8,128)} %get-tuple-element.172) | copy-start | bytes 221188
  240.7 10.5 %copy-start.13 = (f32[24,768]{1,0:T(8,128)S(1)}, f32[24,768]{1,0:T(8,128)}, u32[]{:S(2)}) copy-start(f32[24,768]{1,0:T(8,128)} %get-tuple-element.173) | copy-start | bytes 221188
  240.7 11.2 %copy-start.12 = (f32[24,768]{1,0:T(8,128)S(1)}, f32[24,768]{1,0:T(8,128)}, u32[]{:S(2)}) copy-start(f32[24,768]{1,0:T(8,128)} %get-tuple-element.174) | copy-start | bytes 221188
  240.7 11.8 %copy-start.15 = (bf16[24,768]{1,0:T(8,128)(2,1)S(1)}, bf16[24,768]{1,0:T(8,128)(2,1)}, u32[]{:S(2)}) copy-start(bf16[24,768]{1,0:T(8,128)(2,1)} %get-tuple-element.175) | copy-start | bytes 110596
  240.7 12.4 %copy-start.5 = (f32[48,1536]{1,0:T(8,128)S(1)}, f32[48,1536]{1,0:T(8,128)}, u32[]{:S(2)}) copy-start(f32[48,1536]{1,0:T(8,128)} %get-tuple-element.176) | copy-start | bytes 884740
  240.7 13.1 %copy-start.4 = (f32[48,1536]{1,0:T(8,128)S(1)}, f32[48,1536]{1,0:T(8,128)}, u32[]{:S(2)}) copy-start(f32[48,1536]{1,0:T(8,128)} %get-tuple-element.177) | copy-start | bytes 884740
  245.8 8.8 %copy-start.3 = (f32[48,1536]{1,0:T(8,128)S(1)}, f32[48,1536]{1,0:T(8,128)}, u32[]{:S(2)}) copy-start(f32[48,1536]{1,0:T(8,128)} %get-tuple-element.178) | copy-start | bytes 884740
  245.8 9.5 %copy-start.10 = (bf16[48,1536]{1,0:T(8,128)(2,1)S(1)}, bf16[48,1536]{1,0:T(8,128)(2,1)}, u32[]{:S(2)}) copy-start(bf16[48,1536]{1,0:T(8,128)(2,1)} %get-tuple-element.179) | copy-start | bytes 442372
  245.8 10.1 %copy-start.2 = (f32[96,768]{1,0:T(8,128)S(1)}, f32[96,768]{1,0:T(8,128)}, u32[]{:S(2)}) copy-start(f32[96,768]{1,0:T(8,128)} %get-tuple-element.180) | copy-start | bytes 884740
  245.8 10.8 %copy-start.1 = (f32[96,768]{1,0:T(8,128)S(1)}, f32[96,768]{1,0:T(8,128)}, u32[]{:S(2)}) copy-start(f32[96,768]{1,0:T(8,128)} %get-tuple-element.181) | copy-start | bytes 884740
  245.8 11.6 %copy-start = (f32[96,768]{1,0:T(8,128)S(1)}, f32[96,768]{1,0:T(8,128)}, u32[]{:S(2)}) copy-start(f32[96,768]{1,0:T(8,128)} %get-tuple-element.182) | copy-start | bytes 884740
  245.8 12.3 %copy-start.9 = (bf16[96,768]{1,0:T(8,128)(2,1)S(1)}, bf16[96,768]{1,0:T(8,128)(2,1)}, u32[]{:S(2)}) copy-start(bf16[96,768]{1,0:T(8,128)(2,1)} %get-tuple-element.183) | copy-start | bytes 442372
  245.8 12.9 %copy-start.21 = (f32[2,768]{1,0:T(2,128)S(1)}, f32[2,768]{1,0:T(2,128)}, u32[]{:S(2)}) copy-start(f32[2,768]{1,0:T(2,128)} %get-tuple-element.184) | copy-start | bytes 18436
  245.9 13.5 %copy-start.20 = (f32[2,768]{1,0:T(2,128)S(1)}, f32[2,768]{1,0:T(2,128)}, u32[]{:S(2)}) copy-start(f32[2,768]{1,0:T(2,128)} %get-tuple-element.185) | copy-start | bytes 18436
  245.9 14.1 %copy-start.19 = (f32[2,768]{1,0:T(2,128)S(1)}, f32[2,768]{1,0:T(2,128)}, u32[]{:S(2)}) copy-start(f32[2,768]{1,0:T(2,128)} %get-tuple-element.186) | copy-start | bytes 18436

commit v3 on v2

v3 whole, which is shorter than its diff:
```python
from functools import partial
import math

import jax
import jax.numpy as jnp
import numpy as np
from jax import lax
from jax.experimental import pallas as pl
from jax.experimental.pallas import tpu as pltpu
from jax.sharding import PartitionSpec as P

DH = 64
PLEN = 250
STEP = 5
ROWS = 256
BUCKETS = 32
SPAN = 128

MESH = pl.DeviceIdType.MESH
BF = jnp.bfloat16
F32 = jnp.float32
MIB = 2**20

norm_eps = 1e-06
masked_score = -1000000000.0
beta_first = 0.5
beta_second = 0.5
adam_eps = 1e-08
decay_rate = 0.01
rate_inward = 0.015
rate_outward = 0.3
rate_expand = 0.04
rate_reduce = 0.02
rate_gains = 0.5
rate_table = 0.5


def adamw(weight, first_moment, second, gradient, step_rate):
    new_first = beta_first * first_moment + (1.0 - beta_first) * gradient
    new_second = beta_second * second + (1.0 - beta_second) * gradient * gradient
    first_hat = new_first / (1.0 - beta_first**STEP)
    second_hat = new_second / (1.0 - beta_second**STEP)
    new_weight = weight - step_rate * (
        first_hat / (jnp.sqrt(second_hat) + adam_eps) + decay_rate * weight
    )
    return (new_weight, new_first, new_second)


def distance_onehot():
    span = 2 * ROWS
    relative = np.arange(span)
    relative = np.where(relative < ROWS, relative, relative - span)
    half = BUCKETS // 2
    exact = half // 2
    distance = np.abs(relative)
    far = np.full_like(distance, exact)
    for level in range(1, half - exact):
        far += distance >= math.ceil(exact * (SPAN / exact) ** (level / (half - exact)))
    bucket = np.where(relative > 0, half, 0) + np.where(distance < exact, distance, far)
    return (bucket[:, None] == np.arange(BUCKETS)[None]).astype(np.float32)


def dot(a, b, ca=1, cb=0):
    return lax.dot_general(a, b, (((ca,), (cb,)), ((), ())), preferred_element_type=F32)


class Refs:
    pass


def run(kernel, grid, ins, outs, scratch, collective, limit, name):
    names = [i[0] for i in ins] + [o[0] for o in outs] + [s[0] for s in scratch]

    def body(*refs):
        space = Refs()
        for key, ref in zip(names, refs, strict=True):
            setattr(space, key, ref)
        kernel(space)

    results = pl.pallas_call(
        body,
        grid=grid,
        in_specs=[i[2] for i in ins],
        out_specs=[o[3] for o in outs],
        out_shape=[jax.ShapeDtypeStruct(o[1], o[2]) for o in outs],
        scratch_shapes=[s[1] for s in scratch],
        compiler_params=pltpu.CompilerParams(
            collective_id=collective, has_side_effects=True, vmem_limit_bytes=limit * MIB
        ),
        name=name,
    )(*[i[1] for i in ins])
    return dict(zip([o[0] for o in outs], results))


def whole(shape):
    return pl.BlockSpec(shape, lambda p: (0,) * len(shape), pipeline_mode=pl.Buffered(1))


def steps(first, count, shape):
    rest = (0,) * (len(shape) - 1)
    return pl.BlockSpec(shape, lambda p: (jnp.clip(p - first, 0, count - 1),) + rest)


ANY = pl.BlockSpec(memory_space=pl.ANY)


class Links:
    def __init__(self, n):
        me = lax.axis_index("dp")
        self.n, self.nz, self.me = n, n // 4, me
        x, y = lax.rem(me, 2), lax.rem(me // 2, 2)
        self.z, self.column = me // 4, lax.rem(me, 4)
        self.x_peer, self.y_peer = me + 1 - 2 * x, me + 2 - 4 * y
        self.far_peer = self.x_peer + 2 - 4 * y
        self.z_pair = self.z + 1 - 2 * lax.rem(self.z, 2)
        self.pair_peer = self.z_pair * 4 + self.column

    def z_peer(self, k):
        return lax.rem(self.z + k + self.nz, self.nz) * 4 + self.column

    def block(self, k, column_of, z=None):
        return lax.rem((self.z if z is None else z) + k, self.nz) * 4 + lax.rem(column_of, 4)

    def peers(self):
        ids = [self.x_peer, self.y_peer] + [self.z_peer(k) for k in range(1, self.nz)]
        return [{"dp": i} for i in ids]

    def column_peer(self, k):
        return self.z * 4 + lax.rem(self.column + k + 4, 4)


def greet(peers):
    barrier = pltpu.get_barrier_semaphore()
    for peer in peers:
        pl.semaphore_signal(barrier, inc=1, device_id=peer, device_id_type=MESH)
    pl.semaphore_wait(barrier, len(peers))


def partner():
    return {"mp": 1 - lax.axis_index("mp")}


def cut(ref, blk, rows):
    return ref.at[pl.ds(pl.multiple_of(blk * rows, 16), rows)]


def remote(src, dst, send, recv, peer):
    return pltpu.make_async_remote_copy(
        src_ref=src,
        dst_ref=dst,
        send_sem=send,
        recv_sem=recv,
        device_id=peer,
        device_id_type=MESH,
    )


class Gather:
    def __init__(self, links, full, ss, rs):
        self.l, self.full, self.ss, self.rs = links, full, ss, rs

    def at(self, a, blk):
        ref, rows, lanes = self.full[a]
        rows = pl.ds(pl.multiple_of(blk * rows, 16), rows)
        return ref.at[rows] if lanes is None else ref.at[rows, pl.ds(*lanes)]

    def copy(self, a, role, k, blk, peer):
        at = self.at(a, blk)
        return remote(at, at, self.ss.at[a, role, k], self.rs.at[a, role, k], {"dp": peer})

    def put(self, a, value):
        self.at(a, self.l.me)[...] = value

    def own(self, a):
        l = self.l
        for k in range(1, l.nz):
            self.copy(a, 0, k, l.me, l.z_peer(-k)).start()
        self.copy(a, 1, 0, l.me, l.x_peer).start()
        self.copy(a, 2, 0, l.me, l.y_peer).start()

    def along(self, a):
        l = self.l
        for k in range(1, l.nz):
            blk = l.block(k, l.me)
            self.copy(a, 0, k, blk, l.x_peer).wait_recv()
            self.copy(a, 1, k, blk, l.x_peer).start()
            self.copy(a, 2, k, blk, l.y_peer).start()

    def across(self, a):
        l = self.l
        for k in range(0, l.nz, 2):
            role, source, target = (1, l.x_peer, l.y_peer) if k % 4 == 0 else (2, l.y_peer, l.x_peer)
            blk = l.block(k, source)
            self.copy(a, role, k, blk, source).wait_recv()
            self.copy(a, 3, k, blk, target).start()

    def share(self, a):
        l = self.l
        for k in range(0, l.nz, 2):
            blk = l.block(k, l.far_peer)
            self.copy(a, 3, k, blk, l.x_peer).wait_recv()
            self.copy(a, 4, k, blk, l.pair_peer).start()

    def arrived(self, a):
        l = self.l
        for k in range(l.nz):
            if k % 4 != 0:
                self.copy(a, 1, k, l.block(k, l.x_peer), l.x_peer).wait_recv()
            if k % 4 != 2:
                self.copy(a, 2, k, l.block(k, l.y_peer), l.y_peer).wait_recv()
            if k % 2 == 0:
                self.copy(a, 4, k, l.block(k, l.far_peer, l.z_pair), l.pair_peer).wait_recv()

    def sent(self, a):
        l = self.l
        for k in range(l.nz):
            roles = (0,) * (k > 0) + (1, 2) + (3, 4) * (k % 2 == 0)
            for role in roles:
                self.copy(a, role, k, l.me, l.x_peer).wait_send()


class Scatter:
    def __init__(self, links, grads, bufs, ss, rs):
        self.l, self.grads, self.bufs, self.ss, self.rs = links, grads, bufs, ss, rs

    def part(self, a, blk):
        ref, rows = self.grads[a]
        return cut(ref, blk, rows)

    def read(self, a, blk):
        ref, rows = self.grads[a]
        return ref[pl.ds(pl.multiple_of(blk * rows, 16), rows), :].astype(F32)

    def copy(self, a, role, k, src, slot, peer):
        dst = self.bufs[a].at[slot, k]
        return remote(src, dst, self.ss.at[a, role, k], self.rs.at[a, role, k], {"dp": peer})

    def arrive(self, a, role, k, slot):
        self.copy(a, role, k, self.part(a, 0), slot, self.l.x_peer).wait_recv()

    def far(self, a):
        l = self.l
        for k in range(l.nz):
            peer = l.y_peer if k % 2 == 0 else l.x_peer
            self.copy(a, 0, k, self.part(a, l.block(k, l.far_peer)), 0, peer).start()

    def plain(self, a):
        l = self.l
        for k in range(l.nz):
            if k % 2 == 1:
                self.copy(a, 1, k, self.part(a, l.block(k, l.x_peer)), 2, l.x_peer).start()
            else:
                self.copy(a, 2, k, self.part(a, l.block(k, l.y_peer)), 4, l.y_peer).start()

    def near(self, a):
        l = self.l
        for k in range(l.nz):
            self.arrive(a, 0, k, 0)
            role, peer, slot = (1, l.x_peer, 1) if k % 2 == 0 else (2, l.y_peer, 3)
            mine = self.read(a, l.block(k, peer)) + self.bufs[a][0, k].astype(F32)
            self.bufs[a][slot, k] = mine.astype(BF)
            self.copy(a, role, k, self.bufs[a].at[slot, k], slot + 1, peer).start()

    def along(self, a, kept):
        l = self.l
        for k in list(range(1, l.nz)) + [0]:
            self.arrive(a, 1, k, 2)
            self.arrive(a, 2, k, 4)
            mine = (
                self.read(a, l.block(k, l.me))
                + self.bufs[a][2, k].astype(F32)
                + self.bufs[a][4, k].astype(F32)
            )
            if k == 0:
                kept[...] = mine
            else:
                self.bufs[a][5, k] = mine.astype(BF)
                self.copy(a, 3, k, self.bufs[a].at[5, k], 6, l.z_peer(k)).start()

    def total(self, a, kept):
        total = kept[...]
        for k in range(1, self.l.nz):
            self.arrive(a, 3, k, 6)
            total += self.bufs[a][6, k].astype(F32)
        return total

    def sent(self, a):
        for k in range(self.l.nz):
            for role in (0, 1, 2) + (3,) * (k > 0):
                self.copy(a, role, k, self.part(a, 0), 0, self.l.x_peer).wait_send()


class Swap:
    def __init__(self, mine, theirs, ss, rs):
        self.mine, self.theirs, self.ss, self.rs = mine, theirs, ss, rs

    def copy(self, slot):
        return remote(
            self.mine.at[slot], self.theirs.at[slot], self.ss.at[slot], self.rs.at[slot], partner()
        )

    def put(self, p, value):
        self.mine[lax.rem(p, 2)] = value.astype(BF)

    def send(self, p):
        self.copy(lax.rem(p, 2)).start()

    def take(self, p):
        slot = lax.rem(p, 2)
        self.copy(slot).wait()
        return self.mine[slot].astype(F32) + self.theirs[slot].astype(F32)


def swap_scratch(name, d):
    return [
        (name + "_mine", pltpu.VMEM((2, ROWS, d), BF)),
        (name + "_theirs", pltpu.VMEM((2, ROWS, d), BF)),
        (name + "_ss", pltpu.SemaphoreType.DMA((2,))),
        (name + "_rs", pltpu.SemaphoreType.DMA((2,))),
    ]


def swap_of(r, name):
    return Swap(*(getattr(r, name + part) for part in ("_mine", "_theirs", "_ss", "_rs")))


class Spread:
    def __init__(self, links, own, z_slots, xy_slots, ss, rs):
        self.l, self.own, self.z_slots, self.xy_slots = links, own, z_slots, xy_slots
        self.ss, self.rs = ss, rs

    def copy(self, stage, k, src, dst, peer):
        return remote(src, dst, self.ss.at[stage, k], self.rs.at[stage, k], {"dp": peer})

    def along(self):
        l = self.l
        self.z_slots[l.z] = self.own[...]
        for k in range(1, l.nz):
            self.copy(0, k, self.own, self.z_slots.at[l.z], l.z_peer(k)).start()

    def across(self):
        l = self.l
        for k in range(1, l.nz):
            self.copy(0, k, self.own, self.z_slots.at[lax.rem(l.z - k + l.nz, l.nz)], l.z_peer(k)).wait()
        total = self.z_slots[0]
        for k in range(1, l.nz):
            total += self.z_slots[k]
        self.own[...] = total
        self.xy_slots[l.column] = total
        for k in range(1, 4):
            self.copy(1, k, self.own, self.xy_slots.at[l.column], l.column_peer(k)).start()

    def total(self):
        l = self.l
        for k in range(1, 4):
            self.copy(1, k, self.own, self.xy_slots.at[lax.rem(l.column - k + 4, 4)], l.column_peer(k)).wait()
        total = self.xy_slots[0]
        for k in range(1, 4):
            total += self.xy_slots[k]
        return total


def every(step, actions):
    for at, what, argument in actions:
        pl.when(step == at)(partial(what, argument))


gelu_root = math.sqrt(2.0 / math.pi)
gelu_cube = 0.044715
WINDOW = 272


def inverse_rms(v):
    return lax.rsqrt(jnp.mean(v * v, axis=-1, keepdims=True) + norm_eps)


def window_start(p, total):
    return min(p * PLEN // 16 * 16, total - WINDOW)


def align(source, target, windows, sems, passages):
    total = source.shape[0]

    def fetch(p):
        return pltpu.make_async_copy(
            source.at[pl.ds(window_start(p, total), WINDOW)], windows.at[p % 2], sems.at[p % 2]
        )

    def start():
        fetch(0).start()
        fetch(1).start()

    def move(first, last):
        for p in range(first, last):
            fetch(p).wait()
            off = p * PLEN - window_start(p, total)
            rows = windows[p % 2].astype(F32)[off : off + PLEN]
            pad = jnp.zeros((ROWS - PLEN, rows.shape[1]), F32)
            target[p] = jnp.concatenate([rows, pad], axis=0).astype(BF)
            if p + 2 < passages:
                fetch(p + 2).start()

    return start, move


PAIR = 2 * DH


def attend_kernel(n, passages, heads, direct, r):
    s = pl.program_id(0)
    pairs = heads // 2
    att = swap_of(r, "att")
    if direct:
        links = Links(n)
        rows_i, rows_o = r.wi.shape[0] // n, r.wo_wide.shape[0] // n
        full = [(r.wi, rows_i, (3 * PAIR * j, 3 * PAIR)) for j in range(pairs)]
        full += [(r.wo_wide, rows_o, None)]
        full += [(r.we, r.we.shape[0] // n, None), (r.wr, r.wr.shape[0] // n, None)]
        o, e, red = pairs, pairs + 1, pairs + 2
        gather = Gather(links, full, r.g_ss, r.g_rs)
    tok_start, tok_move = align(r.tokens, r.tok, r.tok_window, r.tok_sem, passages)
    cot_start, cot_move = align(r.cotangent, r.cot, r.cot_window, r.cot_sem, passages)

    def local(src, dst, i):
        return pltpu.make_async_copy(src, dst, r.out_sem.at[i])

    @pl.when(s == 0)
    def _():
        tok_start()
        cot_start()
        if direct:
            for j in range(pairs):
                lanes = slice(j * PAIR, (j + 1) * PAIR)
                gather.put(j, jnp.concatenate([r.own_i[c][:, lanes] for c in range(3)], axis=1).astype(BF))
            pad = jnp.zeros((rows_o - r.own_o.shape[0], r.own_o.shape[1]), F32)
            gather.put(o, jnp.concatenate([r.own_o[...], pad], axis=0).astype(BF))
            gather.put(e, r.own_e[0])
            gather.put(red, r.own_r[: full[red][1]].astype(BF))
            greet(links.peers() + [partner()])
            for a in range(pairs + 1):
                gather.own(a)
        else:
            greet([partner()])
        tok_move(0, passages // 2)
        if direct:
            gather.along(0)
            gather.along(1)
        tok_move(passages // 2, passages)
        local(r.tok, r.tok_out, 0).start()
        if direct:
            gather.across(0)
            gather.along(2)
            gather.across(1)
            gather.share(0)
        cot_move(0, passages // 2)
        if direct:
            gather.along(o)
            gather.across(2)
            gather.share(1)
            gather.own(e)
        cot_move(passages // 2, passages)
        local(r.cot, r.cot_out, 1).start()
        for h in range(heads):
            line = dot_exact(r.table[h : h + 1, :], r.onehot[...])
            rows = jnp.broadcast_to(line, (ROWS, 2 * ROWS))
            r.bias[h] = pltpu.roll(rows, 0, 1, stride=1, stride_axis=0)[:, :ROWS]
        if direct:
            gather.across(o)
            gather.share(2)
            gather.own(red)
            gather.share(o)
            for j in range(pairs):
                gather.arrived(j)

    @pl.when(s < passages)
    def _():
        x = r.tok[s].astype(F32)
        normed = (x * inverse_rms(x) * r.gains[0:1, :]).astype(BF)
        r.normed[0] = normed
        r.proj[0] = dot(normed, r.wi[...]).astype(BF)
        valid = r.buckets[0, pl.ds(s, 1), :] < BUCKETS
        masked = jnp.concatenate(
            [jnp.where(valid, 0.0, masked_score), jnp.full((1, ROWS - PLEN), masked_score, F32)], axis=1
        )
        for h in range(heads):
            first = h // 2 * 3 * PAIR + h % 2 * DH
            q, k, v = (r.proj[0, :, first + c * PAIR : first + c * PAIR + DH] for c in range(3))
            sc = dot(q, k, 1, 1) + r.bias[h] + masked
            e_ = jnp.exp(sc - jnp.max(sc, axis=-1, keepdims=True))
            a = (e_ * (1.0 / jnp.sum(e_, axis=-1, keepdims=True))).astype(BF)
            r.probs[0, h] = a
            r.ctx[0, :, h * DH : (h + 1) * DH] = dot(a, v).astype(BF)

    if direct:

        @pl.when(s == 0)
        def _():
            gather.arrived(o)
            rows = r.own_o.shape[0]
            for d in range(n):
                block = r.wo_wide[d * rows_o : (d + 1) * rows_o, :].astype(F32)
                r.wo_f32[d * rows : (d + 1) * rows, :] = block[:rows]
            r.wo[...] = r.wo_f32[...].astype(BF)

        every(s, (
            (1, gather.along, e), (2, gather.along, red), (2, gather.across, e), (4, gather.across, red),
            (4, gather.share, e), (5, gather.share, red),
        ))

        @pl.when(s == passages - 1)
        def _():
            local(r.wi, r.wi_out, 2).start()
            local(r.wo, r.wo_out, 3).start()

    @pl.when(s < passages)
    def _():
        att.put(s, dot(r.ctx[0], r.wo[...]))

    if direct:

        @pl.when(s == passages)
        def _():
            gather.arrived(e)
            gather.arrived(red)
            local(r.we, r.we_out, 4).start()
            local(r.wr, r.wr_out, 5).start()

    @pl.when(s > 0)
    def _():
        last = s - 1
        r.hidden[0] = r.tok[last].astype(F32) + att.take(last)

    @pl.when(s < passages)
    def _():
        att.send(s)

    @pl.when(s == passages)
    def _():
        local(r.tok, r.tok_out, 0).wait()
        local(r.cot, r.cot_out, 1).wait()
        if direct:
            for a in range(pairs + 3):
                gather.sent(a)
            local(r.wi, r.wi_out, 2).wait()
            local(r.wo, r.wo_out, 3).wait()
            local(r.we, r.we_out, 4).wait()
            local(r.wr, r.wr_out, 5).wait()


def dot_exact(a, b):
    return lax.dot_general(
        a, b, (((1,), (1,)), ((), ())), precision=lax.Precision.HIGHEST, preferred_element_type=F32
    )


def attend(n, passages, heads, direct, tokens, cotangent, buckets, gains, table, onehot, weights):
    d = tokens.shape[1]
    width = heads * DH
    one = (1, ROWS, d)
    ins = [("tokens", tokens, ANY), ("cotangent", cotangent, ANY)]
    first_rows = pl.BlockSpec((1,) + buckets.shape[1:], lambda p: (0, 0, 0), pipeline_mode=pl.Buffered(1))
    ins += [("buckets", buckets, first_rows)]
    ins += [(k, v, whole(v.shape)) for k, v in (("gains", gains), ("table", table), ("onehot", onehot))]
    ins += [(k, v, whole(v.shape)) for k, v in weights.items()]
    outs = [
        ("proj", (passages, ROWS, 3 * width), BF, steps(0, passages, (1, ROWS, 3 * width))),
        ("probs", (passages, heads, ROWS, ROWS), BF, steps(0, passages, (1, heads, ROWS, ROWS))),
        ("normed", (passages, ROWS, d), BF, steps(0, passages, one)),
        ("ctx", (passages, ROWS, width), BF, steps(0, passages, (1, ROWS, width))),
        ("hidden", (passages, ROWS, d), F32, steps(1, passages, one)),
        ("tok_out", (passages, ROWS, d), BF, ANY),
        ("cot_out", (passages, ROWS, d), BF, ANY),
    ]
    scratch = [
        ("tok", pltpu.VMEM((passages, ROWS, d), BF)),
        ("cot", pltpu.VMEM((passages, ROWS, d), BF)),
        ("tok_window", pltpu.VMEM((2, WINDOW, d), BF)),
        ("cot_window", pltpu.VMEM((2, WINDOW, d), BF)),
        ("tok_sem", pltpu.SemaphoreType.DMA((2,))),
        ("cot_sem", pltpu.SemaphoreType.DMA((2,))),
        ("out_sem", pltpu.SemaphoreType.DMA((6,))),
        ("bias", pltpu.VMEM((heads, ROWS, ROWS), F32)),
    ] + swap_scratch("att", d)
    if direct:
        part = weights["own_r"].shape[0] // 2 * n
        padded = weights["own_o"].shape[0]
        padded += -padded % 16
        shapes = {"wi": (d, 3 * width), "wo": (width, d), "we": (d, part), "wr": (part, d)}
        for key, shape in shapes.items():
            outs.append((key + "_out", shape, BF, ANY))
            scratch.append((key, pltpu.VMEM(shape, BF)))
        arrays = heads // 2 + 3
        scratch += [
            ("wo_f32", pltpu.VMEM((width, d), F32)),
            ("wo_wide", pltpu.VMEM((n * padded, d), BF)),
            ("g_ss", pltpu.SemaphoreType.DMA((arrays, 5, n // 4))),
            ("g_rs", pltpu.SemaphoreType.DMA((arrays, 5, n // 4))),
        ]
    kernel = partial(attend_kernel, n, passages, heads, direct)
    return run(kernel, (passages + 1,), ins, outs, scratch, 1, 60, "attend")


def feed_kernel(n, passages, direct, r):
    s = pl.program_id(0)
    count = passages
    out, back_in = (swap_of(r, name) for name in ("out", "in"))
    if direct:
        links = Links(n)
        full = [(r.we_b, r.we_b.shape[0] // n, None), (r.wr_b, r.wr_b.shape[0] // n, None)]
        gather = Gather(links, full, r.g_ss, r.g_rs)
        grads = [(g, g.shape[0] // n) for g in (r.stage_r, r.stage_e)]
        kept = [r.sum_r, r.sum_e]
        sums = Scatter(links, grads, [r.buf_r, r.buf_e], r.s_ss, r.s_rs)

    @pl.when(s == 0)
    def _():
        if direct:
            gather.put(0, r.own_e[1])
            gather.put(1, r.own_r[full[1][1] :].astype(BF))
            greet(links.peers() + [partner()])
            gather.own(0)
            gather.own(1)
        else:
            greet([partner()])
        r.gain_grad[...] = jnp.zeros_like(r.gain_grad)

    @pl.when((s == 0) | (s == count))
    def _():
        r.acc_r[...] = jnp.zeros_like(r.acc_r)
        r.acc_e[...] = jnp.zeros_like(r.acc_e)

    if direct:
        every(s, (
            (1, gather.along, 0), (2, gather.along, 1), (2, gather.across, 0), (4, gather.across, 1),
            (4, gather.share, 0), (6, gather.share, 1), (count, gather.arrived, 0), (count, gather.arrived, 1),
            (count, sums.far, 0), (count, sums.far, 1), (count, sums.plain, 0), (count, sums.plain, 1),
            (count + 2, sums.near, 0), (count + 3, sums.near, 1),
        ))
        for a in range(2):
            pl.when(s == count + 6 + a)(partial(sums.along, a, kept[a]))

    def part(normed, c, we, wr):
        u = dot(normed, we[...])
        square = u * u
        t = jnp.tanh(u * (gelu_root + (gelu_root * gelu_cube) * square))
        half = 0.5 * (1.0 + t)
        act = (u * half).astype(BF)
        slope = half + (0.5 * u) * (1.0 - t * t) * (
            gelu_root + (3.0 * gelu_root * gelu_cube) * square
        )
        back = (dot(c, wr[...], 1, 1) * slope).astype(BF)
        r.acc_r[...] += dot(act, c, 0, 0)
        r.acc_e[...] += dot(normed, back, 0, 0)
        return dot(act, wr[...]), dot(back, we[...], 1, 1)

    @pl.when(s < count)
    def _():
        h = r.hidden_now[0]
        normed = (h * inverse_rms(h) * r.gains[1:2, :]).astype(BF)
        r.normed_two[s] = normed
        r.out_sum[s], r.in_sum[s] = part(normed, r.cot_now[0], r.we_a, r.wr_a)

    @pl.when(s == count - 1)
    def _():
        r.stage_r[...] = r.acc_r[...].astype(BF)
        r.stage_e[...] = r.acc_e[...].astype(BF)

    p = s - count

    @pl.when((s >= count) & (s < 2 * count))
    def _():
        r_part, n_part = part(r.normed_two[p], r.cot_now[0], r.we_b, r.wr_b)
        out.put(p, r.out_sum[p] + r_part)
        back_in.put(p, r.in_sum[p] + n_part)

    @pl.when(s == 2 * count - 1)
    def _():
        r.grad_r[...] = r.acc_r[...].astype(BF)
        r.grad_e[...] = r.acc_e[...].astype(BF)

    @pl.when(s > count)
    def _():
        last = p - 1
        h = r.hidden[0]
        r.layer[0] = (h + out.take(last)).astype(BF)
        grad = back_in.take(last)
        inv = inverse_rms(h)
        zed = r.gains[1:2, :] * grad
        hr = h * inv
        r.gain_grad[0:1, :] += jnp.sum(grad * hr, axis=0, keepdims=True)
        inner = jnp.mean(zed * hr, axis=-1, keepdims=True)
        hidden_grad = r.cot[0].astype(F32) + inv * (zed - hr * inner)
        r.hidden_grad[0] = hidden_grad
        r.above[0] = hidden_grad.astype(BF)

    @pl.when((s >= count) & (s < 2 * count))
    def _():
        out.send(p)
        back_in.send(p)

    if direct:

        @pl.when(s == 2 * count)
        def _():
            for a in range(2):
                kept[a][...] = sums.total(a, kept[a])
            for a in range(2):
                gather.sent(a)
                sums.sent(a)


def feed(n, passages, direct, f, gains, weights):
    d = gains.shape[1]
    one = (1, ROWS, d)
    late = steps(passages + 1, passages, one)
    again = pl.BlockSpec(one, lambda p: (lax.rem(jnp.minimum(p, 2 * passages - 1), passages), 0, 0))
    ins = [
        ("hidden_now", f["hidden"], steps(0, passages, one)),
        ("hidden", f["hidden"], late),
        ("cot_now", f["cot_out"], again),
        ("cot", f["cot_out"], late),
    ]
    fixed = dict(weights, gains=gains)
    part = weights["wr_a"].shape[0]
    outs = [
        ("layer", (passages, ROWS, d), BF, late),
        ("hidden_grad", (passages, ROWS, d), F32, late),
        ("above", (passages, ROWS, d), BF, late),
        ("grad_r", (part, d), BF, whole((part, d))),
        ("grad_e", (d, part), BF, whole((d, part))),
        ("gain_grad", (8, d), F32, whole((8, d))),
    ]
    scratch = [
        ("normed_two", pltpu.VMEM((passages, ROWS, d), BF)),
        ("out_sum", pltpu.VMEM((passages, ROWS, d), F32)),
        ("in_sum", pltpu.VMEM((passages, ROWS, d), F32)),
        ("acc_r", pltpu.VMEM((part, d), F32)),
        ("acc_e", pltpu.VMEM((d, part), F32)),
    ]
    stage = [("stage_r", (part, d)), ("stage_e", (d, part))]
    if direct:
        scratch += [(k, pltpu.VMEM(shape, BF)) for k, shape in stage]
        nz = n // 4
        scratch += [
            ("we_b", pltpu.VMEM((d, part), BF)),
            ("wr_b", pltpu.VMEM((part, d), BF)),
            ("buf_r", pltpu.VMEM((7, nz, part // n, d), BF)),
            ("buf_e", pltpu.VMEM((7, nz, d // n, part), BF)),
            ("g_ss", pltpu.SemaphoreType.DMA((2, 5, nz))),
            ("g_rs", pltpu.SemaphoreType.DMA((2, 5, nz))),
            ("s_ss", pltpu.SemaphoreType.DMA((2, 4, nz))),
            ("s_rs", pltpu.SemaphoreType.DMA((2, 4, nz))),
        ]
        for key, shape in (("sum_r", (part // n, d)), ("sum_e", (d // n, part))):
            outs.append((key, shape, F32, whole(shape)))
    else:
        outs += [(k, shape, BF, whole(shape)) for k, shape in stage]
    for name in ("out", "in"):
        scratch += swap_scratch(name, d)
    ins += [(k, v, whole(v.shape)) for k, v in fixed.items()]
    kernel = partial(feed_kernel, n, passages, direct)
    return run(kernel, (2 * passages + 1,), ins, outs, scratch, 2, 60, "feed")


def back_kernel(n, passages, heads, direct, r):
    s = pl.program_id(0)
    pairs = heads // 2
    count = passages
    rounds = pairs * count
    swap = swap_of(r, "in")
    stage = [getattr(r, f"stage_i{j}") for j in range(pairs)]
    if direct:
        links = Links(n)
        refs = [r.grad_r, r.grad_e, r.stage_o] + stage
        grads = [(g, g.shape[0] // n) for g in refs]
        names = ["r", "e", "o"] + [f"i{j}" for j in range(pairs)]
        bufs = [getattr(r, "buf_" + k) for k in names]
        kept = [getattr(r, "sum_" + k) for k in names]
        sums = Scatter(links, grads, bufs, r.s_ss, r.s_rs)
        wide = Spread(links, r.wide, r.wide_z, r.wide_xy, r.w_ss, r.w_rs)
        last_small = Spread(links, r.slim, r.slim_z, r.slim_xy, r.l_ss, r.l_rs)

    @pl.when(s == 0)
    def _():
        if direct:
            greet(links.peers() + [{"dp": links.far_peer}, partner()])
            for a in range(2):
                sums.far(a)
            for a in range(2):
                sums.plain(a)
        else:
            greet([partner()])
        r.acc_o[...] = jnp.zeros_like(r.acc_o)
        r.acc_s[...] = jnp.zeros_like(r.acc_s)
        r.gain_one[...] = jnp.zeros_like(r.gain_one)

    if direct:
        near = [(0, 3), (1, 4), (2, count + 3)] + [(3 + j, (j + 1) * count + 5 - j) for j in range(pairs)]
        far = [(2, count)] + [(3 + j, (j + 1) * count) for j in range(pairs)]
        along = [(0, 8), (1, 10), (2, count + 6)] + [(3 + j, (j + 1) * count + 8 - j) for j in range(pairs)]
        for a, at in far:
            every(s, ((at, sums.far, a), (at, sums.plain, a)))
        for a, at in near:
            every(s, ((at, sums.near, a),))
        for a, at in along:
            pl.when(s == at)(partial(sums.along, a, kept[a]))

    j, p = s // count, lax.rem(s, count)

    @pl.when(s < count)
    def _():
        above = r.above[0]
        r.acc_o[...] += dot(r.ctx[0], above, 0, 0)
        dctx = dot(above, r.wo[...], 1, 1).astype(BF)
        for i in range(pairs):
            r.dctx[i, p] = dctx[:, i * PAIR : (i + 1) * PAIR]

    @pl.when((s < rounds) & (p == 0))
    def _():
        r.acc_i[...] = jnp.zeros_like(r.acc_i)

    @pl.when(s < rounds)
    def _():
        grads_of = [[], [], []]
        dc_pair = r.dctx[j, p]
        for h in range(2):
            q, k, v = (r.proj[0, :, c * PAIR + h * DH : c * PAIR + (h + 1) * DH] for c in range(3))
            dc = dc_pair[:, h * DH : (h + 1) * DH]
            a = r.probs[0, h]
            grads_of[2].append(dot(a, dc, 0, 0))
            dp = dot(dc, v, 1, 1)
            a = a.astype(F32)
            centre = jnp.sum(a * dp, axis=-1, keepdims=True)
            ds = (a * (dp - centre)).astype(BF)
            r.acc_s[2 * j + h] += ds.astype(F32)
            grads_of[0].append(dot(ds, k))
            grads_of[1].append(dot(ds, q, 0, 0))
        dproj = jnp.concatenate([g for c in range(3) for g in grads_of[c]], axis=1).astype(BF)
        r.dproj[p, :, pl.ds(pl.multiple_of(j * 3 * PAIR, 3 * PAIR), 3 * PAIR)] = dproj
        r.acc_i[...] += dot(r.normed[0], dproj, 0, 0)

    @pl.when(s == count - 1)
    def _():
        blocks = n if direct else 1
        rows = r.acc_o.shape[0] // blocks
        padded = r.stage_o.shape[0] // blocks
        for b in range(blocks):
            part = r.acc_o[b * rows : (b + 1) * rows, :]
            if padded > rows:
                part = jnp.concatenate([part, jnp.zeros((padded - rows, part.shape[1]), F32)], axis=0)
            r.stage_o[b * padded : (b + 1) * padded, :] = part.astype(BF)

    for i in range(pairs):

        @pl.when(s == (i + 1) * count - 1)
        def _():
            stage[i][...] = r.acc_i[...].astype(BF)

    @pl.when(s == rounds)
    def _():
        r.wide[...] = jnp.zeros_like(r.wide)
        r.wide[heads : heads + 1, :] = r.gain_two[0:1, :]
        for h in range(heads):
            rows = jnp.concatenate([r.acc_s[h], jnp.zeros((ROWS, ROWS), F32)], axis=1)
            while rows.shape[0] > 1:
                half = rows.shape[0] // 2
                rows = rows[:half] + pltpu.roll(rows[half:], 2 * ROWS - half, 1)
            r.wide[h : h + 1, : 2 * ROWS] = rows
        if direct:
            wide.along()

    if direct:
        pl.when(s == rounds + 2)(wide.across)

    t = s - rounds

    @pl.when((s >= rounds) & (s < rounds + count))
    def _():
        swap.put(t, dot(r.dproj[t], r.wi[...], 1, 1))

    @pl.when(s > rounds)
    def _():
        x = r.tok[0].astype(F32)
        grad = swap.take(t - 1)
        inv = inverse_rms(x)
        zed = r.gains[0:1, :] * grad
        xr = x * inv
        r.gain_one[0:1, :] += jnp.sum(grad * xr, axis=0, keepdims=True)
        inner = jnp.mean(zed * xr, axis=-1, keepdims=True)
        r.input_grad[0] = r.hidden_grad[0] + inv * (zed - xr * inner)

    @pl.when((s >= rounds) & (s < rounds + count))
    def _():
        swap.send(t)

    @pl.when(s == rounds + count)
    def _():
        if not direct:
            r.wide_sum[...] = r.wide[...]
            r.slim_sum[...] = r.gain_one[...]
            return
        d = r.gain_one.shape[1]
        for c in range(d // 128):
            r.slim[c : c + 1, :] = r.gain_one[0:1, c * 128 : (c + 1) * 128]
        for c in range(d // 128, 8):
            r.slim[c : c + 1, :] = jnp.zeros((1, 128), F32)
        last_small.along()
        r.wide_sum[...] = wide.total()
        for a in range(3):
            kept[a][...] = sums.total(a, kept[a])
        last_small.across()
        for a in range(3, 3 + pairs):
            kept[a][...] = sums.total(a, kept[a])
        r.slim_sum[...] = last_small.total()
        for a in range(3 + pairs):
            sums.sent(a)


def back(n, passages, heads, direct, f, m, gains, wi, wo):
    d = gains.shape[1]
    width = heads * DH
    pairs = heads // 2
    rounds = pairs * passages
    one = (1, ROWS, d)
    first = lambda shape: steps(0, passages, shape)
    late = steps(rounds + 1, passages, one)

    def turn(s):
        s = jnp.minimum(s, rounds - 1)
        return s // passages, lax.rem(s, passages)

    ins = [
        ("above", m["above"], first(one)),
        ("ctx", f["ctx"], first((1, ROWS, width))),
        ("normed", f["normed"], pl.BlockSpec(one, lambda s: (turn(s)[1], 0, 0))),
        ("proj", f["proj"], pl.BlockSpec((1, ROWS, 3 * PAIR), lambda s: (turn(s)[1], 0, turn(s)[0]))),
        ("probs", f["probs"], pl.BlockSpec((1, 2, ROWS, ROWS), lambda s: (turn(s)[1], turn(s)[0], 0, 0))),
        ("tok", f["tok_out"], late),
        ("hidden_grad", m["hidden_grad"], late),
    ]
    fixed = [("gains", gains), ("wi", wi), ("wo", wo), ("gain_two", m["gain_grad"])]
    outs = [
        ("input_grad", (passages, ROWS, d), F32, late),
        ("wide_sum", (8, d), F32, whole((8, d))),
    ]
    scratch = [
        ("acc_i", pltpu.VMEM((d, 3 * PAIR), F32)),
        ("acc_o", pltpu.VMEM((width, d), F32)),
        ("acc_s", pltpu.VMEM((heads, ROWS, ROWS), F32)),
        ("dctx", pltpu.VMEM((pairs, passages, ROWS, PAIR), BF)),
        ("dproj", pltpu.VMEM((passages, ROWS, 3 * width), BF)),
        ("gain_one", pltpu.VMEM((8, d), F32)),
        ("wide", pltpu.VMEM((8, d), F32)),
    ] + swap_scratch("in", d)
    rows_o = width
    if direct:
        rows_o = width // n
        rows_o = (rows_o + -rows_o % 16) * n
    stage = [("stage_o", (rows_o, d))] + [(f"stage_i{j}", (d, 3 * PAIR)) for j in range(pairs)]
    if direct:
        nz = n // 4
        fixed += [(k, m[k]) for k in ("grad_r", "grad_e")]
        scratch += [(k, pltpu.VMEM(shape, BF)) for k, shape in stage]
        blocks = {"r": m["grad_r"].shape, "e": m["grad_e"].shape, "o": (rows_o, d)}
        blocks.update({f"i{j}": (d, 3 * PAIR) for j in range(pairs)})
        for key, shape in blocks.items():
            shape = (shape[0] // n, shape[1])
            scratch.append(("buf_" + key, pltpu.VMEM((7, nz) + shape, BF)))
            outs.append(("sum_" + key, shape, F32, whole(shape)))
        outs.append(("slim_sum", (8, 128), F32, whole((8, 128))))
        scratch += [
            ("wide_z", pltpu.VMEM((nz, 8, d), F32)),
            ("wide_xy", pltpu.VMEM((4, 8, d), F32)),
            ("slim", pltpu.VMEM((8, 128), F32)),
            ("slim_z", pltpu.VMEM((nz, 8, 128), F32)),
            ("slim_xy", pltpu.VMEM((4, 8, 128), F32)),
            ("s_ss", pltpu.SemaphoreType.DMA((len(blocks), 4, nz))),
            ("s_rs", pltpu.SemaphoreType.DMA((len(blocks), 4, nz))),
        ]
        for key in ("w_ss", "w_rs", "l_ss", "l_rs"):
            scratch.append((key, pltpu.SemaphoreType.DMA((2, max(nz, 4)))))
    else:
        outs += [(k, shape, BF, whole(shape)) for k, shape in stage]
        outs.append(("slim_sum", (8, d), F32, whole((8, d))))
    ins += [(k, v, whole(v.shape)) for k, v in fixed]
    kernel = partial(back_kernel, n, passages, heads, direct)
    return run(kernel, (rounds + passages + 1,), ins, outs, scratch, 3, 60, "back")


def shards(
    n,
    tokens,
    cotangent,
    buckets,
    inward_master,
    inward_first,
    inward_second,
    outward_master,
    outward_first,
    outward_second,
    expand_master,
    expand_first,
    expand_second,
    reduce_master,
    reduce_first,
    reduce_second,
    gains_master,
    gains_first,
    gains_second,
    table_master,
    table_first,
    table_second,
):
    d = tokens.shape[1]
    passages = tokens.shape[0] // PLEN
    heads = inward_master.shape[2] // DH
    pairs = heads // 2
    rows_i, rows_e, rows_r = inward_master.shape[0], expand_master.shape[0], reduce_master.shape[0]
    units = expand_master.shape[1]
    direct = n % 8 == 0 and rows_i % 16 == 0 and rows_r % 32 == 0 and outward_master.shape[0] % 8 == 0

    def by_pairs(a):
        return a.reshape(-1, 3, pairs, PAIR).transpose(0, 2, 1, 3).reshape(-1, 3 * pairs * PAIR)

    def unit_halves(a):
        return a.reshape(rows_e, n, 2, units // (2 * n)).transpose(2, 0, 1, 3).reshape(2, rows_e, -1)

    def unit_order(a):
        return a.reshape(2, rows_e, n, units // (2 * n)).transpose(1, 2, 0, 3).reshape(rows_e, units)

    onehot = jnp.asarray(distance_onehot())
    bucket_rows = buckets.transpose(1, 0, 2)
    table_rows = jnp.pad(table_master.T, ((0, -heads % 8), (0, 0)))
    if direct:
        own_e = unit_halves(expand_master.astype(BF))
        first = {
            "own_i": inward_master.transpose(1, 0, 2),
            "own_o": outward_master,
            "own_e": own_e,
            "own_r": reduce_master,
        }
    else:
        masters = (by_pairs(inward_master), outward_master, expand_master, reduce_master)
        wi, wo, we, wr = (
            lax.all_gather(w.astype(BF), "dp", axis=0, tiled=True) for w in masters
        )
        first = {"wi": wi, "wo": wo}
    f = attend(
        n, passages, heads, direct, tokens, cotangent, bucket_rows, gains_master, table_rows, onehot, first
    )
    if direct:
        wi, wo = f["wi_out"], f["wo_out"]
        second = {"we_a": f["we_out"], "wr_a": f["wr_out"], "own_e": own_e, "own_r": reduce_master}
    else:
        half = units // 2
        second = {"we_a": we[:, :half], "wr_a": wr[:half], "we_b": we[:, half:], "wr_b": wr[half:]}
    m = feed(n, passages, direct, f, gains_master, second)
    b = back(n, passages, heads, direct, f, m, gains_master, wi, wo)

    def scatter(g):
        return lax.psum_scatter(g.astype(F32), "dp", scatter_dimension=0, tiled=True)

    if direct:
        inward_parts = [b[f"sum_i{j}"] for j in range(pairs)]
        outward_sum = b["sum_o"][: outward_master.shape[0]]
        expand_sum = unit_order(jnp.stack([m["sum_e"], b["sum_e"]]))
        reduce_sum = jnp.concatenate([m["sum_r"], b["sum_r"]], axis=0)
        wide_sum = b["wide_sum"]
        gain_one = b["slim_sum"][: d // 128].reshape(1, d)
    else:
        inward_parts = [scatter(b[f"stage_i{j}"]) for j in range(pairs)]
        outward_sum = scatter(b["stage_o"])
        expand_sum = scatter(jnp.concatenate([m["stage_e"], m["grad_e"]], axis=1))
        reduce_sum = scatter(jnp.concatenate([m["stage_r"], m["grad_r"]], axis=0))
        wide_sum, gain_one = lax.psum((b["wide_sum"], b["slim_sum"][:1]), "dp")
    inward_sum = jnp.stack([g.reshape(-1, 3, PAIR) for g in inward_parts], axis=2)
    inward_sum = inward_sum.reshape(inward_master.shape)
    gains_sum = jnp.concatenate([gain_one, wide_sum[heads : heads + 1]], axis=0)
    table_sum = lax.dot_general(
        onehot.T, wide_sum[:heads, : 2 * ROWS], (((1,), (1,)), ((), ())), precision=lax.Precision.HIGHEST
    )

    layer_out = m["layer"][:, :PLEN].reshape(tokens.shape)
    input_grad = b["input_grad"][:, :PLEN].reshape(tokens.shape)
    outputs = [layer_out, input_grad]
    for w, first_moment, second_moment, gradient, rate, copied in (
        (inward_master, inward_first, inward_second, inward_sum, rate_inward, True),
        (outward_master, outward_first, outward_second, outward_sum, rate_outward, True),
        (expand_master, expand_first, expand_second, expand_sum, rate_expand, True),
        (reduce_master, reduce_first, reduce_second, reduce_sum, rate_reduce, True),
        (gains_master, gains_first, gains_second, gains_sum, rate_gains, False),
        (table_master, table_first, table_second, table_sum, rate_table, False),
    ):
        new = adamw(w, first_moment, second_moment, gradient, rate)
        outputs += list(new)
        if copied:
            outputs.append(new[0].astype(BF))
    return tuple(outputs)


def solution(mesh):
    rows = P("dp", None)
    inward = P("dp", None, "mp")
    tall = P(("mp", "dp"), None)
    wide = P("dp", "mp")
    table = P(None, "mp")
    return jax.shard_map(
        partial(shards, mesh.shape["dp"]),
        mesh=mesh,
        in_specs=(rows, rows, P("dp", None, None))
        + (inward,) * 3
        + (tall,) * 3
        + (wide,) * 3
        + (tall,) * 3
        + (P(),) * 3
        + (table,) * 3,
        out_specs=(rows, rows)
        + (inward,) * 4
        + (tall,) * 4
        + (wide,) * 4
        + (tall,) * 4
        + (P(),) * 3
        + (table,) * 3,
        check_vma=False,
    )
```

time: 261 us -> 244 us (0.935)
  local copies, waits for them, and re-layouts: 28.6 us -> 12.6 us
  Pallas kernels: 229 us -> 222 us
  other arithmetic: 0.7 us -> 6.63 us
    unnamed x69 -> x61, local copies, waits for them, and re-layouts: 18.8 us -> 0.17 us
    pallas_call x2 -> x3, Pallas kernels: 229 us -> 222 us  [run(): pl.pallas_call(body, grid=grid, in_specs=[i[2] for i in ins], out_specs=[...]
    convert_element_type x0 -> x5, other arithmetic: none -> 5.87 us  [the longest x4 4.9 us: shards(): outputs.append(new[0].astype(BF))]
where the time goes in v3:
time: 244 us; the launch traced here: 243 us
  Pallas kernels  222 us (91%)
  local copies, waits for them, and re-layouts  12.6 us (5%)
  other arithmetic  6.63 us (3%)
    pallas_call x3, Pallas kernels, run(): pl.pallas_call(body, grid=grid, in_specs=[i[2] for i in ins], out_specs=[...  222 us
    reshape x1, local copies, waits for them, and re-layouts, shards(): input_grad = b['input_grad'][:, :PLEN].reshape(tokens.shape)  5.1 us
    convert_element_type x4, other arithmetic, shards(): outputs.append(new[0].astype(BF))  4.9 us

profile of v3, /device:TPU:0, one launch (start us, length us, event | category | flops | bytes accessed | tf_op | source)
XLA Modules:
  0.0 243.3 jit_solution(4392023713408631802)
XLA Ops:
  0.7 1.3 pad.4.refs_4_
  1.9 1.0 convert_element_type.17
  2.9 0.4 reshape.74
  3.3 0.1 copy.55
  3.4 1.0 reshape.75.refs_8_.refs_6_
  4.4 68.0 %attend.1 = (bf16[8,256,1152]{2,1,0:T(8,128)(2,1)}, bf16[8,6,256,256]{3,2,1,0:T(8,128)(2,1)}, bf16[8,256,768]{2,1,0:T(8,128)(2,1)}, bf16[8,256,384]{2,1,0:T(8,12...) custom-call(bf16[2000,768]{1,0:T(8,128)(2,1)} %refs_0_.1, ...), custom_call_target="tpu_custom_call" | custom-call | tf_op jit(solution)/shard_map/attend/pallas_call | solution.py:80
  72.4 71.4 %feed.1 = (bf16[8,256,768]{2,1,0:T(8,128)(2,1)}, f32[8,256,768]{2,1,0:T(8,128)}, bf16[8,256,768]{2,1,0:T(8,128)(2,1)}, bf16[768,768]{1,0:T(8,128)(2,1)}, bf16[76...) custom-call(f32[8,256,768]{2,1,0:T(8,128)} %get-tuple-element.52.refs_0_.refs_1_, ...), custom_call_target="tpu_custom_call" | custom-call | tf_op jit(solution)/shard_map/feed/pallas_call | solution.py:80
  143.8 82.7 %back.1 = (f32[8,256,768]{2,1,0:T(8,128)}, f32[8,768]{1,0:T(8,128)}, f32[48,768]{1,0:T(8,128)}, f32[48,768]{1,0:T(8,128)}, f32[32,768]{1,0:T(8,128)}, /*index=5*...) custom-call(bf16[8,256,768]{2,1,0:T(8,128)(2,1)} %get-tuple-element.57.refs_0_, ...), custom_call_target="tpu_custom_call" | custom-call | tf_op jit(solution)/shard_map/back/pallas_call | solution.py:80
  226.5 2.1 reshape.76
  228.6 0.0 copy-start.27
  228.6 0.0 copy-start.15
  228.6 0.0 copy-start.24
  228.6 0.0 copy-start.25
  228.7 0.0 copy-start.17
  228.7 5.1 %reshape.77 = f32[2000,768]{1,0:T(8,128)} reshape(f32[8,250,768]{2,1,0:T(8,128)} %bitcast.21) | data formatting | bytes 12288000 | tf_op jit(solution)/shard_map/reshape | solution.py:1084
  233.9 0.9 multiply_subtract_fusion.5
  234.8 0.6 multiply_subtract_fusion.4
  235.6 0.1 pad_maximum_fusion
  235.7 0.2 copy.50
  235.8 0.1 reshape.78
  236.0 0.7 fusion.14
  236.8 0.2 stack.14
  237.0 0.0 copy-start.2
  237.0 0.0 copy-start.5
  237.0 0.2 stack.13
  237.2 0.1 maximum_bitcast_fusion
  237.3 0.0 copy-start.1
  237.3 0.6 copy.51
  237.9 1.1 reshape.79
  239.1 2.0 fusion.16
  241.0 1.1 fusion.12
  242.2 1.1 fusion.10
  (58 shorter events, 0.2 us)
Async XLA Ops:
  143.8 82.7 %copy-start = (bf16[8,256,768]{2,1,0:T(8,128)(2,1)S(1)}, bf16[8,256,768]{2,1,0:T(8,128)(2,1)}, u32[]{:S(2)}) copy-start(bf16[8,256,768]{2,1,0:T(8,128)(2,1)} %get-tuple-element.56) | copy-start | bytes 9437188
  228.6 5.2 %copy-start.23 = (f32[8,768]{1,0:T(8,128)S(1)}, f32[8,768]{1,0:T(8,128)}, u32[]{:S(2)}) copy-start(f32[8,768]{1,0:T(8,128)} %get-tuple-element.79) | copy-start | bytes 73732
  228.6 5.3 %copy-start.3 = (f32[512,32]{1,0:T(8,128)S(1)}, f32[512,32]{1,0:T(8,128)}, u32[]{:S(2)}) copy-start(f32[512,32]{1,0:T(8,128)} %constant.23.clone.refs_5_) | copy-start | bytes 196612
  228.6 5.3 %copy-start.22 = (f32[32,6]{0,1:T(8,128)S(1)}, f32[32,6]{0,1:T(8,128)}, u32[]{:S(2)}) copy-start(f32[32,6]{0,1:T(8,128)} %param.40) | copy-start | bytes 2308
  228.6 5.3 %copy-start.26 = (f32[32,6]{0,1:T(8,128)S(1)}, f32[32,6]{0,1:T(8,128)}, u32[]{:S(2)}) copy-start(f32[32,6]{0,1:T(8,128)} %param.41) | copy-start | bytes 2308
  228.6 5.3 %copy-start.27 = (f32[32,6]{0,1:T(8,128)S(1)}, f32[32,6]{0,1:T(8,128)}, u32[]{:S(2)}) copy-start(f32[32,6]{0,1:T(8,128)} %param.42) | copy-start | bytes 2308
  228.6 6.2 %copy-start.28 = (f32[8,128]{1,0:T(8,128)S(1)}, f32[8,128]{1,0:T(8,128)}, u32[]{:S(2)}) copy-start(f32[8,128]{1,0:T(8,128)} %get-tuple-element.78) | copy-start | bytes 12292
  228.6 6.2 %copy-start.15 = (f32[2,768]{1,0:T(2,128)S(1)}, f32[2,768]{1,0:T(2,128)}, u32[]{:S(2)}) copy-start(f32[2,768]{1,0:T(2,128)} %refs_7_.5) | copy-start | bytes 18436
  228.6 6.2 %copy-start.24 = (f32[2,768]{1,0:T(2,128)S(1)}, f32[2,768]{1,0:T(2,128)}, u32[]{:S(2)}) copy-start(f32[2,768]{1,0:T(2,128)} %param.38) | copy-start | bytes 18436
  228.6 6.2 %copy-start.25 = (f32[2,768]{1,0:T(2,128)S(1)}, f32[2,768]{1,0:T(2,128)}, u32[]{:S(2)}) copy-start(f32[2,768]{1,0:T(2,128)} %param.39) | copy-start | bytes 18436
  228.7 6.8 %copy-start.20 = (f32[48,384]{1,0:T(8,128)S(1)}, f32[48,384]{1,0:T(8,128)}, u32[]{:S(2)}) copy-start(f32[48,384]{1,0:T(8,128)} %get-tuple-element.70) | copy-start | bytes 221188
  228.7 6.8 %copy-start.19 = (f32[48,384]{1,0:T(8,128)S(1)}, f32[48,384]{1,0:T(8,128)}, u32[]{:S(2)}) copy-start(f32[48,384]{1,0:T(8,128)} %get-tuple-element.71) | copy-start | bytes 221188
  228.7 6.9 %copy-start.18 = (f32[48,384]{1,0:T(8,128)S(1)}, f32[48,384]{1,0:T(8,128)}, u32[]{:S(2)}) copy-start(f32[48,384]{1,0:T(8,128)} %get-tuple-element.72) | copy-start | bytes 221188
  228.7 7.3 %copy-start.9 = (f32[24,768]{1,0:T(8,128)S(1)}, f32[24,768]{1,0:T(8,128)}, u32[]{:S(2)}) copy-start(f32[24,768]{1,0:T(8,128)} %refs_7_.3) | copy-start | bytes 221188
  228.7 7.3 %copy-start.16 = (f32[24,768]{1,0:T(8,128)S(1)}, f32[24,768]{1,0:T(8,128)}, u32[]{:S(2)}) copy-start(f32[24,768]{1,0:T(8,128)} %param.29) | copy-start | bytes 221188
  228.7 7.3 %copy-start.17 = (f32[24,768]{1,0:T(8,128)S(1)}, f32[24,768]{1,0:T(8,128)}, u32[]{:S(2)}) copy-start(f32[24,768]{1,0:T(8,128)} %param.30) | copy-start | bytes 221188
  228.7 7.3 %copy-start.21 = (f32[32,768]{1,0:T(8,128)S(1)}, f32[32,768]{1,0:T(8,128)}, u32[]{:S(2)}) copy-start(f32[32,768]{1,0:T(8,128)} %get-tuple-element.73) | copy-start | bytes 294916
  233.8 2.9 %copy-start.11 = (f32[48,768]{1,0:T(8,128)S(1)}, f32[48,768]{1,0:T(8,128)}, u32[]{:S(2)}) copy-start(f32[48,768]{1,0:T(8,128)} %get-tuple-element.76) | copy-start | bytes 442372
  233.8 2.9 %copy-start.12 = (f32[48,768]{1,0:T(8,128)S(1)}, f32[48,768]{1,0:T(8,128)}, u32[]{:S(2)}) copy-start(f32[48,768]{1,0:T(8,128)} %get-tuple-element.77) | copy-start | bytes 442372
  233.8 3.0 %copy-start.14 = (f32[48,768]{1,0:T(8,128)S(1)}, f32[48,768]{1,0:T(8,128)}, u32[]{:S(2)}) copy-start(f32[48,768]{1,0:T(8,128)} %get-tuple-element.75) | copy-start | bytes 442372
  233.9 3.2 %copy-start.13 = (f32[48,768]{1,0:T(8,128)S(1)}, f32[48,768]{1,0:T(8,128)}, u32[]{:S(2)}) copy-start(f32[48,768]{1,0:T(8,128)} %get-tuple-element.74) | copy-start | bytes 442372
  236.0 3.0 %copy-start.4 = (f32[48,3,384]{2,0,1:T(8,128)S(1)}, f32[48,3,384]{2,0,1:T(8,128)}, u32[]{:S(2)}) copy-start(f32[48,3,384]{2,0,1:T(8,128)} %param.25) | copy-start | bytes 663556
  236.0 3.0 %copy-start.10 = (f32[48,3,384]{2,0,1:T(8,128)S(1)}, f32[48,3,384]{2,0,1:T(8,128)}, u32[]{:S(2)}) copy-start(f32[48,3,384]{2,0,1:T(8,128)} %param.26) | copy-start | bytes 663556
  237.0 4.0 %copy-start.2 = (f32[48,1536]{1,0:T(8,128)S(1)}, f32[48,1536]{1,0:T(8,128)}, u32[]{:S(2)}) copy-start(f32[48,1536]{1,0:T(8,128)} %param.31) | copy-start | bytes 884740
  237.0 4.0 %copy-start.5 = (f32[48,1536]{1,0:T(8,128)S(1)}, f32[48,1536]{1,0:T(8,128)}, u32[]{:S(2)}) copy-start(f32[48,1536]{1,0:T(8,128)} %param.32) | copy-start | bytes 884740
  237.0 4.0 %copy-start.6 = (f32[48,1536]{1,0:T(8,128)S(1)}, f32[48,1536]{1,0:T(8,128)}, u32[]{:S(2)}) copy-start(f32[48,1536]{1,0:T(8,128)} %param.33) | copy-start | bytes 884740
  237.3 4.9 %copy-start.1 = (f32[96,768]{1,0:T(8,128)S(1)}, f32[96,768]{1,0:T(8,128)}, u32[]{:S(2)}) copy-start(f32[96,768]{1,0:T(8,128)} %refs_7_.4) | copy-start | bytes 884740
  237.3 4.8 %copy-start.7 = (f32[96,768]{1,0:T(8,128)S(1)}, f32[96,768]{1,0:T(8,128)}, u32[]{:S(2)}) copy-start(f32[96,768]{1,0:T(8,128)} %param.35) | copy-start | bytes 884740
  239.1 3.1 %copy-start.8 = (f32[96,768]{1,0:T(8,128)S(1)}, f32[96,768]{1,0:T(8,128)}, u32[]{:S(2)}) copy-start(f32[96,768]{1,0:T(8,128)} %param.36) | copy-start | bytes 884740

commit v4 on v3

v4 whole, which is shorter than its diff:
```python
from functools import partial
import math

import jax
import jax.numpy as jnp
import numpy as np
from jax import lax
from jax.experimental import pallas as pl
from jax.experimental.pallas import tpu as pltpu
from jax.sharding import PartitionSpec as P

DH = 64
PLEN = 250
STEP = 5
ROWS = 256
BUCKETS = 32
SPAN = 128

MESH = pl.DeviceIdType.MESH
BF = jnp.bfloat16
F32 = jnp.float32
MIB = 2**20

norm_eps = 1e-06
masked_score = -1000000000.0
beta_first = 0.5
beta_second = 0.5
adam_eps = 1e-08
decay_rate = 0.01
rate_inward = 0.015
rate_outward = 0.3
rate_expand = 0.04
rate_reduce = 0.02
rate_gains = 0.5
rate_table = 0.5


def adamw(weight, first_moment, second, gradient, step_rate):
    new_first = beta_first * first_moment + (1.0 - beta_first) * gradient
    new_second = beta_second * second + (1.0 - beta_second) * gradient * gradient
    first_hat = new_first / (1.0 - beta_first**STEP)
    second_hat = new_second / (1.0 - beta_second**STEP)
    new_weight = weight - step_rate * (
        first_hat / (jnp.sqrt(second_hat) + adam_eps) + decay_rate * weight
    )
    return (new_weight, new_first, new_second)


def distance_onehot():
    span = 2 * ROWS
    relative = np.arange(span)
    relative = np.where(relative < ROWS, relative, relative - span)
    half = BUCKETS // 2
    exact = half // 2
    distance = np.abs(relative)
    far = np.full_like(distance, exact)
    for level in range(1, half - exact):
        far += distance >= math.ceil(exact * (SPAN / exact) ** (level / (half - exact)))
    bucket = np.where(relative > 0, half, 0) + np.where(distance < exact, distance, far)
    return (bucket[:, None] == np.arange(BUCKETS)[None]).astype(np.float32)


def dot(a, b, ca=1, cb=0):
    return lax.dot_general(a, b, (((ca,), (cb,)), ((), ())), preferred_element_type=F32)


class Refs:
    pass


def run(kernel, ins, outs, scratch, collective, limit, name):
    names = [i[0] for i in ins] + [o[0] for o in outs] + [s[0] for s in scratch]

    def body(*refs):
        space = Refs()
        for key, ref in zip(names, refs, strict=True):
            setattr(space, key, ref)
        kernel(space)

    results = pl.pallas_call(
        body,
        in_specs=[i[2] for i in ins],
        out_specs=[o[3] for o in outs],
        out_shape=[jax.ShapeDtypeStruct(o[1], o[2]) for o in outs],
        scratch_shapes=[s[1] for s in scratch],
        compiler_params=pltpu.CompilerParams(
            collective_id=collective, has_side_effects=True, vmem_limit_bytes=limit * MIB
        ),
        name=name,
    )(*[i[1] for i in ins])
    return dict(zip([o[0] for o in outs], results))


ANY = pl.BlockSpec(memory_space=pl.ANY)
VMEM = pl.BlockSpec(memory_space=pltpu.VMEM)


class Load:
    def __init__(self, r, name):
        self.hbm, self.buf, self.sem = (getattr(r, name + part) for part in ("", "_buf", "_sem"))

    def copy(self, p):
        return pltpu.make_async_copy(self.hbm.at[p], self.buf.at[p], self.sem.at[p])

    def start(self):
        for p in range(self.hbm.shape[0]):
            self.copy(p).start()

    def wait(self, p):
        self.copy(p).wait()


class Drain:
    def __init__(self, r, name):
        self.hbm, self.buf, self.sem = (getattr(r, name + part) for part in ("", "_buf", "_sem"))

    def copy(self, p):
        slot = lax.rem(p, 2)
        return pltpu.make_async_copy(self.buf.at[slot], self.hbm.at[p], self.sem.at[slot])

    def slot(self, p):
        pl.when(p >= 2)(lambda: self.copy(p - 2).wait())
        return self.buf.at[lax.rem(p, 2)]

    def start(self, p):
        self.copy(p).start()

    def last(self):
        for p in range(max(self.hbm.shape[0] - 2, 0), self.hbm.shape[0]):
            self.copy(p).wait()


def stream_scratch(name, shape, dtype):
    return [
        (name + "_buf", pltpu.VMEM((2,) + tuple(shape), dtype)),
        (name + "_sem", pltpu.SemaphoreType.DMA((2,))),
    ]


class Links:
    def __init__(self, n):
        me = lax.axis_index("dp")
        self.n, self.nz, self.me = n, n // 4, me
        x, y = lax.rem(me, 2), lax.rem(me // 2, 2)
        self.z, self.column = me // 4, lax.rem(me, 4)
        self.x_peer, self.y_peer = me + 1 - 2 * x, me + 2 - 4 * y
        self.far_peer = self.x_peer + 2 - 4 * y
        self.z_pair = self.z + 1 - 2 * lax.rem(self.z, 2)
        self.pair_peer = self.z_pair * 4 + self.column

    def z_peer(self, k):
        return lax.rem(self.z + k + self.nz, self.nz) * 4 + self.column

    def block(self, k, column_of, z=None):
        return lax.rem((self.z if z is None else z) + k, self.nz) * 4 + lax.rem(column_of, 4)

    def peers(self):
        ids = [self.x_peer, self.y_peer] + [self.z_peer(k) for k in range(1, self.nz)]
        return [{"dp": i} for i in ids]

    def column_peer(self, k):
        return self.z * 4 + lax.rem(self.column + k + 4, 4)


def greet(peers):
    barrier = pltpu.get_barrier_semaphore()
    for peer in peers:
        pl.semaphore_signal(barrier, inc=1, device_id=peer, device_id_type=MESH)
    pl.semaphore_wait(barrier, len(peers))


def partner():
    return {"mp": 1 - lax.axis_index("mp")}


def cut(ref, blk, rows):
    return ref.at[pl.ds(pl.multiple_of(blk * rows, 16), rows)]


def remote(src, dst, send, recv, peer):
    return pltpu.make_async_remote_copy(
        src_ref=src,
        dst_ref=dst,
        send_sem=send,
        recv_sem=recv,
        device_id=peer,
        device_id_type=MESH,
    )


class Gather:
    def __init__(self, links, full, ss, rs):
        self.l, self.full, self.ss, self.rs = links, full, ss, rs

    def at(self, a, blk):
        ref, rows, lanes = self.full[a]
        rows = pl.ds(pl.multiple_of(blk * rows, 16), rows)
        return ref.at[rows] if lanes is None else ref.at[rows, pl.ds(*lanes)]

    def copy(self, a, role, k, blk, peer):
        at = self.at(a, blk)
        return remote(at, at, self.ss.at[a, role, k], self.rs.at[a, role, k], {"dp": peer})

    def put(self, a, value):
        self.at(a, self.l.me)[...] = value

    def own(self, a):
        l = self.l
        for k in range(1, l.nz):
            self.copy(a, 0, k, l.me, l.z_peer(-k)).start()
        self.copy(a, 1, 0, l.me, l.x_peer).start()
        self.copy(a, 2, 0, l.me, l.y_peer).start()

    def along(self, a):
        l = self.l
        for k in range(1, l.nz):
            blk = l.block(k, l.me)
            self.copy(a, 0, k, blk, l.x_peer).wait_recv()
            self.copy(a, 1, k, blk, l.x_peer).start()
            self.copy(a, 2, k, blk, l.y_peer).start()

    def across(self, a):
        l = self.l
        for k in range(0, l.nz, 2):
            role, source, target = (1, l.x_peer, l.y_peer) if k % 4 == 0 else (2, l.y_peer, l.x_peer)
            blk = l.block(k, source)
            self.copy(a, role, k, blk, source).wait_recv()
            self.copy(a, 3, k, blk, target).start()

    def share(self, a):
        l = self.l
        for k in range(0, l.nz, 2):
            blk = l.block(k, l.far_peer)
            self.copy(a, 3, k, blk, l.x_peer).wait_recv()
            self.copy(a, 4, k, blk, l.pair_peer).start()

    def arrived(self, a):
        l = self.l
        for k in range(l.nz):
            if k % 4 != 0:
                self.copy(a, 1, k, l.block(k, l.x_peer), l.x_peer).wait_recv()
            if k % 4 != 2:
                self.copy(a, 2, k, l.block(k, l.y_peer), l.y_peer).wait_recv()
            if k % 2 == 0:
                self.copy(a, 4, k, l.block(k, l.far_peer, l.z_pair), l.pair_peer).wait_recv()

    def sent(self, a):
        l = self.l
        for k in range(l.nz):
            roles = (0,) * (k > 0) + (1, 2) + (3, 4) * (k % 2 == 0)
            for role in roles:
                self.copy(a, role, k, l.me, l.x_peer).wait_send()


class Scatter:
    def __init__(self, links, grads, bufs, ss, rs):
        self.l, self.grads, self.bufs, self.ss, self.rs = links, grads, bufs, ss, rs

    def part(self, a, blk):
        ref, rows = self.grads[a]
        return cut(ref, blk, rows)

    def read(self, a, blk):
        ref, rows = self.grads[a]
        return ref[pl.ds(pl.multiple_of(blk * rows, 16), rows), :].astype(F32)

    def copy(self, a, role, k, src, slot, peer):
        dst = self.bufs[a].at[slot, k]
        return remote(src, dst, self.ss.at[a, role, k], self.rs.at[a, role, k], {"dp": peer})

    def arrive(self, a, role, k, slot):
        self.copy(a, role, k, self.part(a, 0), slot, self.l.x_peer).wait_recv()

    def far(self, a):
        l = self.l
        for k in range(l.nz):
            peer = l.y_peer if k % 2 == 0 else l.x_peer
            self.copy(a, 0, k, self.part(a, l.block(k, l.far_peer)), 0, peer).start()

    def plain(self, a):
        l = self.l
        for k in range(l.nz):
            if k % 2 == 1:
                self.copy(a, 1, k, self.part(a, l.block(k, l.x_peer)), 1, l.x_peer).start()
            else:
                self.copy(a, 2, k, self.part(a, l.block(k, l.y_peer)), 2, l.y_peer).start()

    def near(self, a):
        l = self.l
        for k in range(l.nz):
            self.arrive(a, 0, k, 0)
            role, peer = (1, l.x_peer) if k % 2 == 0 else (2, l.y_peer)
            mine = self.read(a, l.block(k, peer)) + self.bufs[a][0, k].astype(F32)
            self.bufs[a][0, k] = mine.astype(BF)
            self.copy(a, role, k, self.bufs[a].at[0, k], role, peer).start()

    def along(self, a, kept):
        l = self.l
        for k in list(range(1, l.nz)) + [0]:
            self.arrive(a, 1, k, 1)
            self.arrive(a, 2, k, 2)
            mine = (
                self.read(a, l.block(k, l.me))
                + self.bufs[a][1, k].astype(F32)
                + self.bufs[a][2, k].astype(F32)
            )
            if k == 0:
                kept[...] = mine
            else:
                self.bufs[a][1, k] = mine.astype(BF)
                self.copy(a, 3, k, self.bufs[a].at[1, k], 3, l.z_peer(k)).start()

    def total(self, a, kept):
        total = kept[...]
        for k in range(1, self.l.nz):
            self.arrive(a, 3, k, 3)
            total += self.bufs[a][3, k].astype(F32)
        kept[...] = total

    def sent(self, a):
        for k in range(self.l.nz):
            for role in (0, 1, 2) + (3,) * (k > 0):
                self.copy(a, role, k, self.part(a, 0), 0, self.l.x_peer).wait_send()


LAG = 2
SLOTS = 4


class Swap:
    def __init__(self, mine, theirs, ss, rs):
        self.mine, self.theirs, self.ss, self.rs = mine, theirs, ss, rs

    def copy(self, slot):
        return remote(
            self.mine.at[slot], self.theirs.at[slot], self.ss.at[slot], self.rs.at[slot], partner()
        )

    def put(self, p, value):
        self.mine[lax.rem(p, SLOTS)] = value.astype(BF)

    def send(self, p):
        self.copy(lax.rem(p, SLOTS)).start()

    def wait(self, p):
        self.copy(lax.rem(p, SLOTS)).wait()

    def rows(self, p, at):
        slot = lax.rem(p, SLOTS)
        return self.mine[slot, at].astype(F32) + self.theirs[slot, at].astype(F32)


def swap_scratch(name, d):
    return [
        (name + "_mine", pltpu.VMEM((SLOTS, ROWS, d), BF)),
        (name + "_theirs", pltpu.VMEM((SLOTS, ROWS, d), BF)),
        (name + "_ss", pltpu.SemaphoreType.DMA((SLOTS,))),
        (name + "_rs", pltpu.SemaphoreType.DMA((SLOTS,))),
    ]


def swap_of(r, name):
    return Swap(*(getattr(r, name + part) for part in ("_mine", "_theirs", "_ss", "_rs")))


class Spread:
    def __init__(self, links, own, z_slots, xy_slots, mp_slot, ss, rs):
        self.l, self.own, self.z_slots, self.xy_slots = links, own, z_slots, xy_slots
        self.mp_slot = mp_slot
        self.ss, self.rs = ss, rs

    def copy(self, stage, k, src, dst, peer):
        return remote(src, dst, self.ss.at[stage, k], self.rs.at[stage, k], {"dp": peer})

    def along(self):
        l = self.l
        self.z_slots[l.z] = self.own[...]
        for k in range(1, l.nz):
            self.copy(0, k, self.own, self.z_slots.at[l.z], l.z_peer(k)).start()

    def across(self):
        l = self.l
        for k in range(1, l.nz):
            self.copy(0, k, self.own, self.z_slots.at[lax.rem(l.z - k + l.nz, l.nz)], l.z_peer(k)).wait()
        total = self.z_slots[0]
        for k in range(1, l.nz):
            total += self.z_slots[k]
        self.own[...] = total
        self.xy_slots[l.column] = total
        for k in range(1, 4):
            self.copy(1, k, self.own, self.xy_slots.at[l.column], l.column_peer(k)).start()

    def over(self):
        l = self.l
        for k in range(1, 4):
            self.copy(1, k, self.own, self.xy_slots.at[lax.rem(l.column - k + 4, 4)], l.column_peer(k)).wait()
        total = self.xy_slots[0]
        for k in range(1, 4):
            total += self.xy_slots[k]
        self.own[...] = total
        self.pair().start()

    def pair(self):
        return remote(self.own, self.mp_slot, self.ss.at[1, 0], self.rs.at[1, 0], partner())

    def total(self, split):
        self.pair().wait()
        own, other = self.own[...], self.mp_slot[...]
        row = lax.broadcasted_iota(jnp.int32, own.shape, 0)
        return jnp.where(row >= split, own + other, own)


def every(step, actions):
    for at, what, argument in actions:
        pl.when(step == at)(partial(what, argument))


gelu_root = math.sqrt(2.0 / math.pi)
gelu_cube = 0.044715
WINDOW = 272


STRIP = 32


def strips(step=STRIP):
    return [slice(i, i + step) for i in range(0, ROWS, step)]


def inverse_rms(v):
    return lax.rsqrt(jnp.mean(v * v, axis=-1, keepdims=True) + norm_eps)


def window_start(p, total):
    return min(p * PLEN // 16 * 16, total - WINDOW)


def align(source, target, windows, sems, passages):
    total = source.shape[0]

    def fetch(p):
        return pltpu.make_async_copy(
            source.at[pl.ds(window_start(p, total), WINDOW)], windows.at[p % 2], sems.at[p % 2]
        )

    def start():
        fetch(0).start()
        fetch(1).start()

    def move(first, last):
        for p in range(first, last):
            fetch(p).wait()
            off = p * PLEN - window_start(p, total)
            rows = windows[p % 2].astype(F32)[off : off + PLEN]
            pad = jnp.zeros((ROWS - PLEN, rows.shape[1]), F32)
            target[p] = jnp.concatenate([rows, pad], axis=0).astype(BF)
            if p + 2 < passages:
                fetch(p + 2).start()

    return start, move


def loop(first, last, body):
    lax.fori_loop(first, last, lambda p, carry: (body(p), carry)[1], 0)


PAIR = 2 * DH


def low_lanes(shape):
    return lax.broadcasted_iota(jnp.int32, shape, 1) < DH


def of_head(h, pair):
    low = low_lanes(pair.shape)
    zero = jnp.zeros_like(pair)
    return jnp.where(low, pair, zero) if h % 2 == 0 else jnp.where(low, zero, pair)


def either(first, second):
    return jnp.where(low_lanes(first.shape), first, second)


def forward_kernel(n, passages, heads, direct, r):
    width = heads * DH
    count = passages
    pair, back_in = (swap_of(r, name) for name in ("pair", "in"))
    if direct:
        links = Links(n)
        rows_o = r.wo_wide.shape[0] // n
        full = [(r.wi, r.wi.shape[0] // n, None), (r.wo_wide, rows_o, None)]
        full += [(w, w.shape[0] // n, None) for w in (r.we_a, r.wr_a, r.we_b, r.wr_b)]
        gather = Gather(links, full, r.g_ss, r.g_rs)
        grads = [(g, g.shape[0] // n) for g in (r.stage_r, r.stage_e)]
        kept = [r.sum_r, r.sum_e]
        sums = Scatter(links, grads, [r.buf_r, r.buf_e], r.s_ss, r.s_rs)
    tok_start, tok_move = align(r.tokens, r.tok, r.window, r.window_sem, passages)
    cot_start, cot_move = align(r.cotangent, r.cot, r.window, r.window_sem, passages)
    half = passages // 2
    proj, probs, normed_out, ctx = (Drain(r, name) for name in ("proj", "probs", "normed", "ctx"))
    layer, hidden_grad = (Drain(r, name) for name in ("layer", "hidden_grad"))

    def local(src, dst, i):
        return pltpu.make_async_copy(src, dst, r.out_sem.at[i])

    local(r.buckets.at[0], r.bucket_rows, 5).start()
    tok_start()
    if direct:
        gather.put(0, jnp.concatenate([r.own_i[c] for c in range(3)], axis=1).astype(BF))
        pad = jnp.zeros((rows_o - r.own_o.shape[0], r.own_o.shape[1]), F32)
        gather.put(1, jnp.concatenate([r.own_o[...], pad], axis=0).astype(BF))
        greet(links.peers() + [partner()])
        gather.own(0)
        gather.own(1)
        gather.put(2, r.own_e[0])
        gather.put(3, r.own_r[: full[3][1]].astype(BF))
        gather.put(4, r.own_e[1])
        gather.put(5, r.own_r[full[3][1] :].astype(BF))
    else:
        greet([partner()])
    tok_move(0, half)
    if direct:
        gather.along(0)
        gather.own(2)
    tok_move(half, passages)
    local(r.tok, r.tok_out, 0).start()
    cot_start()
    if direct:
        gather.across(0)
        gather.along(1)
    cot_move(0, half)
    if direct:
        gather.share(0)
        gather.own(3)
        gather.across(1)
    cot_move(half, passages)
    for h in range(heads):
        line = dot_exact(r.table[h : h + 1, :], r.onehot[...])
        rows = jnp.broadcast_to(line, (ROWS, 2 * ROWS))
        r.bias[h] = pltpu.roll(rows, 0, 1, stride=1, stride_axis=0)[:, :ROWS]
    r.gain_grad[...] = jnp.zeros_like(r.gain_grad)

    def normalise(p):
        for at in strips():
            x = r.tok[p, at].astype(F32)
            r.out_sum[p, at] = x * inverse_rms(x) * r.gains[0:1, :]

    loop(0, count, normalise)
    local(r.buckets.at[0], r.bucket_rows, 5).wait()
    if direct:
        gather.share(1)
        gather.own(4)
        gather.arrived(0)

    def lanes(c, j):
        return slice(c * width + j * PAIR, c * width + (j + 1) * PAIR)

    def settle(p):
        pair.wait(p)
        for at in strips():
            r.hidden[p, at] = r.tok[p, at].astype(F32) + pair.rows(p, at)

    def attend(p):
        normed = r.out_sum[p].astype(BF)
        normed_slot, proj_slot, probs_slot, ctx_slot = (
            stream.slot(p) for stream in (normed_out, proj, probs, ctx)
        )
        normed_slot[...] = normed
        proj_slot[...] = dot(normed, r.wi[...]).astype(BF)
        valid = r.bucket_rows[pl.ds(p, 1), :] < BUCKETS
        masked = jnp.concatenate(
            [jnp.where(valid, 0.0, masked_score), jnp.full((1, ROWS - PLEN), masked_score, F32)], axis=1
        )
        pairs = [[proj_slot[:, lanes(c, j)] for c in range(3)] for j in range(heads // 2)]
        products = [dot(of_head(h, pairs[h // 2][0]), pairs[h // 2][1], 1, 1) for h in range(heads)]
        weighted = []
        for h in range(heads):
            parts = []
            for at in strips(64):
                sc = products[h][at] + r.bias[h, at] + masked
                e_ = jnp.exp(sc - jnp.max(sc, axis=-1, keepdims=True))
                parts.append((e_ * (1.0 / jnp.sum(e_, axis=-1, keepdims=True))).astype(BF))
                probs_slot[h, at] = parts[-1]
            weighted.append(jnp.concatenate(parts, axis=0))
        results = [dot(weighted[h], pairs[h // 2][2]) for h in range(heads)]
        for j in range(heads // 2):
            ctx_slot[:, lanes(0, j)] = either(results[2 * j], results[2 * j + 1]).astype(BF)
        if direct:

            @pl.when(p == 0)
            def _():
                gather.arrived(1)
                rows = r.own_o.shape[0]
                wide = r.acc_r
                for d in range(n):
                    block = r.wo_wide[d * rows_o : (d + 1) * rows_o, :].astype(F32)
                    wide[d * rows : (d + 1) * rows, :] = block[:rows]
                r.wo[...] = wide[: n * rows, :].astype(BF)

            every(p, (
                (1, gather.along, 2), (1, gather.own, 5), (2, gather.across, 2), (2, gather.along, 3),
                (3, gather.share, 2), (4, gather.across, 3), (4, gather.along, 4), (5, gather.share, 3),
                (6, gather.across, 4), (6, gather.along, 5), (7, gather.share, 4),
            ))
        pair.put(p, dot(ctx_slot[...], r.wo[...]))
        pl.when(p >= LAG)(lambda: settle(p - LAG))
        pair.send(p)
        for stream in (normed_out, proj, probs, ctx):
            stream.start(p)

    loop(0, count, attend)

    if direct:
        gather.across(5)
        gather.arrived(2)
        gather.arrived(3)
        local(r.wi, r.wi_out, 1).start()
        local(r.wo, r.wo_out, 2).start()

    def clear():
        r.acc_r[...] = jnp.zeros_like(r.acc_r)
        r.acc_e[...] = jnp.zeros_like(r.acc_e)

    def normed_two(p):
        parts = []
        for at in strips():
            h = r.hidden[p, at]
            parts.append((h * inverse_rms(h) * r.gains[1:2, :]).astype(BF))
        return jnp.concatenate(parts, axis=0)

    def inner_part(normed, c, we, wr):
        u_all, in_all = dot(normed, we[...]), dot(c, wr[...], 1, 1)
        acts, backs = [], []
        for at in strips():
            u = u_all[at]
            square = u * u
            t = jnp.tanh(u * (gelu_root + (gelu_root * gelu_cube) * square))
            half = 0.5 * (1.0 + t)
            acts.append((u * half).astype(BF))
            slope = half + (0.5 * u) * (1.0 - t * t) * (
                gelu_root + (3.0 * gelu_root * gelu_cube) * square
            )
            backs.append((in_all[at] * slope).astype(BF))
        return jnp.concatenate(acts, axis=0), jnp.concatenate(backs, axis=0)

    def outer_part(normed, c, act, back, we, wr):
        r.acc_r[...] += dot(act, c, 0, 0)
        r.acc_e[...] += dot(normed, back, 0, 0)
        return dot(act, wr[...]), dot(back, we[...], 1, 1)

    def first(p):
        normed, c = normed_two(p), r.cot[p]
        act, back = inner_part(normed, c, r.we_a, r.wr_a)
        r.out_sum[p], r.in_sum[p] = outer_part(normed, c, act, back, r.we_a, r.wr_a)

        @pl.when(p == 0)
        def _():
            for last in range(count - LAG, count):
                settle(last)

        if direct:
            every(p, ((1, gather.share, 5),))

    clear()
    loop(0, count, first)
    r.stage_r[...] = r.acc_r[...].astype(BF)
    r.stage_e[...] = r.acc_e[...].astype(BF)
    if direct:
        sums.far(0)
        sums.far(1)
        gather.arrived(4)
        gather.arrived(5)
    clear()

    def finish(last):
        layer_slot, grad_slot = layer.slot(last), hidden_grad.slot(last)
        pair.wait(count + last)
        back_in.wait(last)
        gain_rows = jnp.zeros((1, r.gains.shape[1]), F32)
        for at in strips():
            h = r.hidden[last, at]
            layer_slot[at] = (h + pair.rows(count + last, at)).astype(BF)
            grad = back_in.rows(last, at)
            inv = inverse_rms(h)
            hr = h * inv
            gain_rows += jnp.sum(grad * hr, axis=0, keepdims=True)
            zed = r.gains[1:2, :] * grad
            inner = jnp.mean(zed * hr, axis=-1, keepdims=True)
            grad_slot[at] = r.cot[last, at].astype(F32) + inv * (zed - hr * inner)
        r.gain_grad[0:1, :] += gain_rows

    def second(p, with_finish=True):
        normed, c = normed_two(p), r.cot[p]
        act, back = inner_part(normed, c, r.we_b, r.wr_b)
        if with_finish:
            finish(p - LAG)
        r_part, n_part = outer_part(normed, c, act, back, r.we_b, r.wr_b)
        pair.put(count + p, r.out_sum[p] + r_part)
        back_in.put(p, r.in_sum[p] + n_part)
        pair.send(count + p)
        back_in.send(p)
        if with_finish:
            for stream in (layer, hidden_grad):
                stream.start(p - LAG)
            if direct:
                every(p, ((2, sums.near, 0), (3, sums.near, 1)))
                for a in range(2):
                    pl.when(p == 6 + a)(partial(sums.along, a, kept[a]))

    loop(0, LAG, lambda p: second(p, False))
    if direct:
        sums.plain(0)
        sums.plain(1)
    loop(LAG, count, second)
    stage_rb, stage_eb = (r.wr_a, r.we_a) if direct else (r.stage_rb, r.stage_eb)
    if direct:
        gather.sent(2)
        gather.sent(3)
    stage_rb[...] = r.acc_r[...].astype(BF)
    stage_eb[...] = r.acc_e[...].astype(BF)
    local(stage_rb, r.grad_r, 3).start()
    local(stage_eb, r.grad_e, 4).start()
    for p in range(count - LAG, count):
        finish(p)
        for stream in (layer, hidden_grad):
            stream.start(p)
    if direct:
        for a in range(2):
            sums.total(a, kept[a])
        for a in (0, 1, 4, 5):
            gather.sent(a)
        for a in range(2):
            sums.sent(a)
        local(r.wi, r.wi_out, 1).wait()
        local(r.wo, r.wo_out, 2).wait()
    local(r.tok, r.tok_out, 0).wait()
    local(stage_rb, r.grad_r, 3).wait()
    local(stage_eb, r.grad_e, 4).wait()
    for stream in (normed_out, proj, probs, ctx, layer, hidden_grad):
        stream.last()


def dot_exact(a, b):
    return lax.dot_general(
        a, b, (((1,), (1,)), ((), ())), precision=lax.Precision.HIGHEST, preferred_element_type=F32
    )


def forward(n, passages, heads, direct, tokens, cotangent, buckets, gains, table, onehot, weights):
    d = tokens.shape[1]
    width = heads * DH
    ins = [("tokens", tokens, ANY), ("cotangent", cotangent, ANY)]
    ins += [("buckets", buckets, ANY)]
    ins += [(k, v, VMEM) for k, v in (("gains", gains), ("table", table), ("onehot", onehot))]
    ins += [(k, v, VMEM) for k, v in weights.items()]
    if direct:
        part = weights["own_r"].shape[0] // 2 * n
    else:
        part = weights["wr_a"].shape[0]
    streams = {
        "proj": ((ROWS, 3 * width), BF),
        "probs": ((heads, ROWS, ROWS), BF),
        "normed": ((ROWS, d), BF),
        "ctx": ((ROWS, width), BF),
        "layer": ((ROWS, d), BF),
        "hidden_grad": ((ROWS, d), F32),
    }
    outs = [(k, (passages,) + shape, dtype, ANY) for k, (shape, dtype) in streams.items()]
    outs += [
        ("tok_out", (passages, ROWS, d), BF, ANY),
        ("grad_r", (part, d), BF, ANY),
        ("grad_e", (d, part), BF, ANY),
        ("gain_grad", (8, d), F32, VMEM),
    ]
    scratch = [
        ("tok", pltpu.VMEM((passages, ROWS, d), BF)),
        ("cot", pltpu.VMEM((passages, ROWS, d), BF)),
        ("window", pltpu.VMEM((2, WINDOW, d), BF)),
        ("window_sem", pltpu.SemaphoreType.DMA((2,))),
        ("bucket_rows", pltpu.VMEM(buckets.shape[1:], buckets.dtype)),
        ("out_sem", pltpu.SemaphoreType.DMA((6,))),
        ("bias", pltpu.VMEM((heads, ROWS, ROWS), F32)),
        ("hidden", pltpu.VMEM((passages, ROWS, d), F32)),
        ("out_sum", pltpu.VMEM((passages, ROWS, d), F32)),
        ("in_sum", pltpu.VMEM((passages, ROWS, d), F32)),
        ("acc_r", pltpu.VMEM((part, d), F32)),
        ("acc_e", pltpu.VMEM((d, part), F32)),
    ]
    for k, (shape, dtype) in streams.items():
        scratch += stream_scratch(k, shape, dtype)
    for name in ("pair", "in"):
        scratch += swap_scratch(name, d)
    stage = [("stage_r", (part, d)), ("stage_e", (d, part))]
    if direct:
        nz = n // 4
        padded = weights["own_o"].shape[0]
        padded += -padded % 16
        outs += [("wi_out", (d, 3 * width), BF, ANY), ("wo_out", (width, d), BF, ANY)]
        for key, shape in (("sum_r", (part // n, d)), ("sum_e", (d // n, part))):
            outs.append((key, shape, F32, VMEM))
        scratch += [(k, pltpu.VMEM(shape, BF)) for k, shape in stage]
        shapes = {"wi": (d, 3 * width), "wo": (width, d), "wo_wide": (n * padded, d)}
        for half in "ab":
            shapes["we_" + half], shapes["wr_" + half] = (d, part), (part, d)
        scratch += [(key, pltpu.VMEM(shape, BF)) for key, shape in shapes.items()]
        scratch += [
            ("buf_r", pltpu.VMEM((4, nz, part // n, d), BF)),
            ("buf_e", pltpu.VMEM((4, nz, d // n, part), BF)),
            ("g_ss", pltpu.SemaphoreType.DMA((6, 5, nz))),
            ("g_rs", pltpu.SemaphoreType.DMA((6, 5, nz))),
            ("s_ss", pltpu.SemaphoreType.DMA((2, 4, nz))),
            ("s_rs", pltpu.SemaphoreType.DMA((2, 4, nz))),
        ]
    else:
        outs += [(k, shape, BF, VMEM) for k, shape in stage]
        scratch += [("stage_rb", pltpu.VMEM((part, d), BF)), ("stage_eb", pltpu.VMEM((d, part), BF))]
    kernel = partial(forward_kernel, n, passages, heads, direct)
    return run(kernel, ins, outs, scratch, 1, 63, "forward")


def back_kernel(n, passages, heads, direct, r):
    width = heads * DH
    count = passages
    swap = swap_of(r, "in")
    if direct:
        links = Links(n)
        refs = [r.grad_r, r.grad_e, r.stage_o, r.stage_v, r.stage_qk]
        grads = [(g, g.shape[0] // n) for g in refs]
        names = ["r", "e", "o", "v", "qk"]
        bufs = [getattr(r, "buf_" + k) for k in names]
        kept = [getattr(r, "sum_" + k) for k in names]
        sums = Scatter(links, grads, bufs, r.s_ss, r.s_rs)
        wide = Spread(links, r.wide, r.wide_z, r.wide_xy, r.wide_mp, r.w_ss, r.w_rs)
    ctx, normed, probs, proj, tok, hidden_grad = (
        Load(r, name) for name in ("ctx", "normed", "probs", "proj", "tok", "hidden_grad")
    )
    input_grad = Drain(r, "input_grad")

    for p in range(count):
        for stream in (hidden_grad, ctx, probs, normed):
            stream.copy(p).start()
    for stream in (proj, tok):
        stream.start()
    if direct:
        greet(links.peers() + [{"dp": links.far_peer}, partner()])
        sums.far(0)
        sums.far(1)
    else:
        greet([partner()])
    r.acc_o[...] = jnp.zeros_like(r.acc_o)
    r.acc_s[...] = jnp.zeros_like(r.acc_s)
    r.acc_v[...] = jnp.zeros_like(r.acc_v)
    r.acc_qk[...] = jnp.zeros_like(r.acc_qk)

    def lanes(c, j):
        return slice(c * width + j * PAIR, c * width + (j + 1) * PAIR)

    def values(p):
        for stream in (hidden_grad, ctx, probs, normed):
            stream.wait(p)
        top = hidden_grad.buf[p].astype(BF)
        r.acc_o[...] += dot(ctx.buf[p], top, 0, 0)
        dctx = dot(top, r.wo[...], 1, 1).astype(BF)
        r.dctx[p] = dctx
        results = [dot(probs.buf[p, h], dctx[:, lanes(0, h // 2)], 0, 0) for h in range(heads)]
        dv = [either(results[2 * j], results[2 * j + 1]) for j in range(heads // 2)]
        dv = jnp.concatenate(dv, axis=1).astype(BF)
        r.dproj[p, :, 2 * width :] = dv
        r.acc_v[...] += dot(normed.buf[p], dv, 0, 0)
        if direct:
            every(p, (
                (2, sums.plain, 0), (3, sums.plain, 1), (5, sums.near, 0), (7, sums.near, 1),
            ))

    loop(0, count, values)
    blocks = n if direct else 1
    rows = r.acc_o.shape[0] // blocks
    padded = r.stage_o.shape[0] // blocks
    for b in range(blocks):
        part = r.acc_o[b * rows : (b + 1) * rows, :]
        if padded > rows:
            part = jnp.concatenate([part, jnp.zeros((padded - rows, part.shape[1]), F32)], axis=0)
        r.stage_o[b * padded : (b + 1) * padded, :] = part.astype(BF)
    r.stage_v[...] = r.acc_v[...].astype(BF)
    if direct:
        sums.far(2)
        sums.far(3)

    def scores(p):
        proj.wait(p)
        pairs = [[proj.buf[p, :, lanes(c, j)] for c in range(3)] for j in range(heads // 2)]
        products = [
            dot(of_head(h, r.dctx[p, :, lanes(0, h // 2)]), pairs[h // 2][2], 1, 1) for h in range(heads)
        ]
        ds = []
        for h in range(heads):
            parts = []
            for rows in strips(64):
                a = probs.buf[p, h, rows].astype(F32)
                dp = products[h][rows]
                centre = jnp.sum(a * dp, axis=-1, keepdims=True)
                parts.append((a * (dp - centre)).astype(BF))
                r.acc_s[h, rows] += parts[-1].astype(F32)
            ds.append(jnp.concatenate(parts, axis=0))
        dq = [dot(ds[h], pairs[h // 2][1]) for h in range(heads)]
        dk = [dot(ds[h], pairs[h // 2][0], 0, 0) for h in range(heads)]
        for j in range(heads // 2):
            r.dproj[p, :, lanes(0, j)] = either(dq[2 * j], dq[2 * j + 1]).astype(BF)
            r.dproj[p, :, lanes(1, j)] = either(dk[2 * j], dk[2 * j + 1]).astype(BF)
        r.acc_qk[...] += dot(normed.buf[p], r.dproj[p, :, : 2 * width], 0, 0)
        if direct:
            every(p, ((0, sums.plain, 2), (0, sums.plain, 3)))
            for a, at in ((0, 1), (1, 2), (2, 5), (3, 6)):
                pl.when(p == at)(partial(sums.along, a, kept[a]))
            every(p, ((3, sums.near, 2), (4, sums.near, 3)))

    loop(0, count, scores)
    r.stage_qk[...] = r.acc_qk[...].astype(BF)
    if direct:
        sums.far(4)
    terms = jnp.sum(r.acc_v[...] * r.wi[:, 2 * width :].astype(F32), axis=1, keepdims=True)
    terms += jnp.sum(r.acc_qk[...] * r.wi[:, : 2 * width].astype(F32), axis=1, keepdims=True)
    r.wide[...] = jnp.zeros_like(r.wide)
    r.wide[heads : heads + 1, :] = 0.5 * r.gain_two[0:1, :]
    r.wide[heads + 1 : heads + 2, :] = terms.T / r.gains[0:1, :]
    for h in range(heads):
        lines = jnp.concatenate([r.acc_s[h], jnp.zeros((ROWS, ROWS), F32)], axis=1)
        while lines.shape[0] > 1:
            half = lines.shape[0] // 2
            lines = lines[:half] + pltpu.roll(lines[half:], 2 * ROWS - half, 1)
        r.wide[h : h + 1, : 2 * ROWS] = lines
    if direct:
        wide.along()
        sums.plain(4)

    def finish(last):
        tok.wait(last)
        slot = input_grad.slot(last)
        swap.wait(last)
        for at in strips():
            x = tok.buf[last, at].astype(F32)
            inv = inverse_rms(x)
            xr = x * inv
            zed = r.gains[0:1, :] * swap.rows(last, at)
            inner = jnp.mean(zed * xr, axis=-1, keepdims=True)
            slot[at] = hidden_grad.buf[last, at] + inv * (zed - xr * inner)

    def inputs(t, with_finish=True):
        terms = dot(r.dproj[t, :, : 2 * width], r.wi[:, : 2 * width], 1, 1)
        if with_finish:
            finish(t - LAG)
        terms += dot(r.dproj[t, :, 2 * width :], r.wi[:, 2 * width :], 1, 1)
        swap.put(t, terms)
        swap.send(t)
        if with_finish:
            input_grad.start(t - LAG)
            if direct:
                every(t, ((4, sums.near, 4),))
                pl.when(t == 2)(wide.across)
                pl.when(t == 5)(wide.over)

    loop(0, LAG, lambda t: inputs(t, False))
    loop(LAG, count, inputs)
    if direct:
        for a in range(4):
            sums.total(a, kept[a])
        sums.along(4, kept[4])
    for p in range(count - LAG, count):
        finish(p)
        input_grad.start(p)
    if direct:
        r.wide_sum[...] = wide.total(heads)
        sums.total(4, kept[4])
        for a in range(5):
            sums.sent(a)
    else:
        r.wide_sum[...] = r.wide[...]
    input_grad.last()


def back(n, passages, heads, direct, f, gains, wi, wo):
    d = gains.shape[1]
    width = heads * DH
    streams = {
        "ctx": ((ROWS, width), BF),
        "normed": ((ROWS, d), BF),
        "probs": ((heads, ROWS, ROWS), BF),
        "proj": ((ROWS, 3 * width), BF),
        "tok": ((ROWS, d), BF),
        "hidden_grad": ((ROWS, d), F32),
    }
    ins = [(k, f["tok_out" if k == "tok" else k], ANY) for k in streams]
    fixed = [("gains", gains), ("wi", wi), ("wo", wo), ("gain_two", f["gain_grad"])]
    outs = [
        ("input_grad", (passages, ROWS, d), F32, ANY),
        ("wide_sum", (8, d), F32, VMEM),
    ]
    scratch = [
        ("acc_qk", pltpu.VMEM((d, 2 * width), F32)),
        ("acc_v", pltpu.VMEM((d, width), F32)),
        ("acc_o", pltpu.VMEM((width, d), F32)),
        ("acc_s", pltpu.VMEM((heads, ROWS, ROWS), F32)),
        ("dctx", pltpu.VMEM((passages, ROWS, width), BF)),
        ("dproj", pltpu.VMEM((passages, ROWS, 3 * width), BF)),
        ("wide", pltpu.VMEM((8, d), F32)),
    ] + swap_scratch("in", d)
    for k, (shape, dtype) in streams.items():
        scratch.append((k + "_buf", pltpu.VMEM((passages,) + shape, dtype)))
        scratch.append((k + "_sem", pltpu.SemaphoreType.DMA((passages,))))
    scratch += stream_scratch("input_grad", (ROWS, d), F32)
    rows_o = width
    if direct:
        rows_o = width // n
        rows_o = (rows_o + -rows_o % 16) * n
    stage = [("stage_o", (rows_o, d)), ("stage_v", (d, width)), ("stage_qk", (d, 2 * width))]
    if direct:
        nz = n // 4
        fixed += [(k, f[k]) for k in ("grad_r", "grad_e")]
        scratch += [(k, pltpu.VMEM(shape, BF)) for k, shape in stage]
        blocks = {"r": f["grad_r"].shape, "e": f["grad_e"].shape}
        blocks.update({k[6:]: shape for k, shape in stage})
        for key, shape in blocks.items():
            shape = (shape[0] // n, shape[1])
            scratch.append(("buf_" + key, pltpu.VMEM((4, nz) + shape, BF)))
            outs.append(("sum_" + key, shape, F32, VMEM))
        scratch += [
            ("wide_z", pltpu.VMEM((nz, 8, d), F32)),
            ("wide_xy", pltpu.VMEM((4, 8, d), F32)),
            ("wide_mp", pltpu.VMEM((8, d), F32)),
            ("s_ss", pltpu.SemaphoreType.DMA((len(blocks), 4, nz))),
            ("s_rs", pltpu.SemaphoreType.DMA((len(blocks), 4, nz))),
            ("w_ss", pltpu.SemaphoreType.DMA((2, max(nz, 4)))),
            ("w_rs", pltpu.SemaphoreType.DMA((2, max(nz, 4)))),
        ]
    else:
        outs += [(k, shape, BF, VMEM) for k, shape in stage]
    ins += [(k, v, VMEM) for k, v in fixed]
    kernel = partial(back_kernel, n, passages, heads, direct)
    return run(kernel, ins, outs, scratch, 2, 63, "back")


def shards(
    n,
    tokens,
    cotangent,
    buckets,
    inward_master,
    inward_first,
    inward_second,
    outward_master,
    outward_first,
    outward_second,
    expand_master,
    expand_first,
    expand_second,
    reduce_master,
    reduce_first,
    reduce_second,
    gains_master,
    gains_first,
    gains_second,
    table_master,
    table_first,
    table_second,
):
    d = tokens.shape[1]
    passages = tokens.shape[0] // PLEN
    heads = inward_master.shape[2] // DH
    width = heads * DH
    rows_i, rows_e, rows_r = inward_master.shape[0], expand_master.shape[0], reduce_master.shape[0]
    units = expand_master.shape[1]
    direct = n % 8 == 0 and rows_i % 16 == 0 and rows_r % 32 == 0 and outward_master.shape[0] % 8 == 0

    def unit_halves(a):
        return a.reshape(rows_e, n, 2, units // (2 * n)).transpose(2, 0, 1, 3).reshape(2, rows_e, -1)

    def unit_order(a):
        return a.reshape(2, rows_e, n, units // (2 * n)).transpose(1, 2, 0, 3).reshape(rows_e, units)

    onehot = jnp.asarray(distance_onehot())
    bucket_rows = buckets.transpose(1, 0, 2)
    table_rows = table_master.T
    if direct:
        weights = {
            "own_i": inward_master.transpose(1, 0, 2),
            "own_o": outward_master,
            "own_e": unit_halves(expand_master.astype(BF)),
            "own_r": reduce_master,
        }
    else:
        masters = (inward_master.reshape(-1, 3 * width), outward_master, expand_master, reduce_master)
        wi, wo, we, wr = (
            lax.all_gather(w.astype(BF), "dp", axis=0, tiled=True) for w in masters
        )
        half = units // 2
        weights = {"wi": wi, "wo": wo}
        weights.update({"we_a": we[:, :half], "wr_a": wr[:half], "we_b": we[:, half:], "wr_b": wr[half:]})
    f = forward(
        n, passages, heads, direct, tokens, cotangent, bucket_rows, gains_master, table_rows, onehot, weights
    )
    if direct:
        wi, wo = f["wi_out"], f["wo_out"]
    b = back(n, passages, heads, direct, f, gains_master, wi, wo)

    def scatter(g):
        return lax.psum_scatter(g.astype(F32), "dp", scatter_dimension=0, tiled=True)

    if direct:
        inward_sum = jnp.concatenate([b["sum_qk"], b["sum_v"]], axis=1)
        outward_sum = b["sum_o"][: outward_master.shape[0]]
        expand_sum = unit_order(jnp.stack([f["sum_e"], b["sum_e"]]))
        reduce_sum = jnp.concatenate([f["sum_r"], b["sum_r"]], axis=0)
        wide_sum = b["wide_sum"]
    else:
        inward_sum = scatter(jnp.concatenate([b["stage_qk"], b["stage_v"]], axis=1))
        outward_sum = scatter(b["stage_o"])
        expand_sum = scatter(jnp.concatenate([f["stage_e"], f["grad_e"]], axis=1))
        reduce_sum = scatter(jnp.concatenate([f["stage_r"], f["grad_r"]], axis=0))
        wide_sum = lax.psum(b["wide_sum"], "dp")
        gains = lax.psum(wide_sum[heads : heads + 2], "mp")
        wide_sum = jnp.concatenate([wide_sum[:heads], gains], axis=0)
    inward_sum = inward_sum.reshape(inward_master.shape)
    gains_sum = jnp.concatenate([wide_sum[heads + 1 : heads + 2], wide_sum[heads : heads + 1]], axis=0)
    table_sum = lax.dot_general(
        onehot.T, wide_sum[:heads, : 2 * ROWS], (((1,), (1,)), ((), ())), precision=lax.Precision.HIGHEST
    )

    layer_out = f["layer"][:, :PLEN].reshape(tokens.shape)
    input_grad = b["input_grad"][:, :PLEN].reshape(tokens.shape)
    outputs = [layer_out, input_grad]
    for w, first_moment, second_moment, gradient, rate, copied in (
        (inward_master, inward_first, inward_second, inward_sum, rate_inward, True),
        (outward_master, outward_first, outward_second, outward_sum, rate_outward, True),
        (expand_master, expand_first, expand_second, expand_sum, rate_expand, True),
        (reduce_master, reduce_first, reduce_second, reduce_sum, rate_reduce, True),
        (gains_master, gains_first, gains_second, gains_sum, rate_gains, False),
        (table_master, table_first, table_second, table_sum, rate_table, False),
    ):
        new = adamw(w, first_moment, second_moment, gradient, rate)
        outputs += list(new)
        if copied:
            outputs.append(new[0].astype(BF))
    return tuple(outputs)


def solution(mesh):
    rows = P("dp", None)
    inward = P("dp", None, "mp")
    tall = P(("mp", "dp"), None)
    wide = P("dp", "mp")
    table = P(None, "mp")
    return jax.shard_map(
        partial(shards, mesh.shape["dp"]),
        mesh=mesh,
        in_specs=(rows, rows, P("dp", None, None))
        + (inward,) * 3
        + (tall,) * 3
        + (wide,) * 3
        + (tall,) * 3
        + (P(),) * 3
        + (table,) * 3,
        out_specs=(rows, rows)
        + (inward,) * 4
        + (tall,) * 4
        + (wide,) * 4
        + (tall,) * 4
        + (P(),) * 3
        + (table,) * 3,
        check_vma=False,
    )
```

time: 244 us -> 204 us (0.84)
  Pallas kernels: 222 us -> 184 us
    pallas_call x3 -> x2, Pallas kernels: 222 us -> 184 us  [run(): pl.pallas_call(body, in_specs=[i[2] for i in ins], out_specs=[o[3] for o...]
where the time goes in v4:
time: 204 us
  Pallas kernels  184 us (90%)
  local copies, waits for them, and re-layouts  12.2 us (6%)
  other arithmetic  5.59 us (3%)
    pallas_call x2, Pallas kernels, run(): pl.pallas_call(body, in_specs=[i[2] for i in ins], out_specs=[o[3] for o...  184 us
    reshape x1, local copies, waits for them, and re-layouts, shards(): input_grad = b['input_grad'][:, :PLEN].reshape(tokens.shape)  5.06 us

profile of v4, /device:TPU:0, one launch (start us, length us, event | category | flops | bytes accessed | tf_op | source)
XLA Modules:
  0.0 203.6 jit_solution(17121318935365126362)
XLA Ops:
  0.7 1.0 convert_element_type.15
  1.6 0.4 reshape.71
  2.0 0.1 copy.70
  2.1 1.0 reshape.72.refs_8_
  3.1 120.5 %forward.1 = (bf16[8,256,1152]{2,1,0:T(8,128)(2,1)}, bf16[8,6,256,256]{3,2,1,0:T(8,128)(2,1)}, bf16[8,256,768]{2,1,0:T(8,128)(2,1)}, bf16[8,256,384]{2,1,0:T(8,1...) custom-call(bf16[2000,768]{1,0:T(8,128)(2,1)} %refs_0_.1, ...), custom_call_target="tpu_custom_call" | custom-call | tf_op jit(solution)/shard_map/forward/pallas_call | solution.py:80
  123.6 3.5 %reshape.73 = bf16[2000,768]{1,0:T(8,128)(2,1)} reshape(bf16[8,250,768]{2,1,0:T(8,128)(2,1)} %bitcast.20) | data formatting | bytes 6144000 | tf_op jit(solution)/shard_map/reshape | solution.py:1128
  127.0 63.4 %back.1 = (f32[8,256,768]{2,1,0:T(8,128)}, f32[8,768]{1,0:T(8,128)}, f32[48,768]{1,0:T(8,128)}, f32[48,768]{1,0:T(8,128)}, f32[32,768]{1,0:T(8,128)}, /*index=5*/f32[48,384]{1,0:T(8,128)}, f32[48,768]{1,0:T(8,128)}) custom-call(bf16[8,256,384]{2,1,0:T(8,128)(2,1)} %get-tuple-element.46.refs_0_, bf16[8,256,768]{2,1,0:T(8,128)(2,1)} %get-tuple-element.47.refs_1_, ...), custom_call_target="tpu_custom_call" | custom-call | tf_op jit(solution)/shard_map/back/pallas_call | solution.py:80
  190.4 0.0 copy-start.3
  190.4 0.0 copy-start.9
  190.5 0.0 copy-start.10
  190.5 0.0 copy-start.8
  190.5 0.0 copy-start.16
  190.5 0.0 copy-start.17
  190.5 5.1 %reshape.74 = f32[2000,768]{1,0:T(8,128)} reshape(f32[8,250,768]{2,1,0:T(8,128)} %bitcast.19) | data formatting | bytes 12288000 | tf_op jit(solution)/shard_map/reshape | solution.py:1129
  195.7 1.0 fusion.16
  196.7 0.7 fusion.14
  197.4 0.2 stack.10
  197.6 0.2 stack.9
  197.8 0.0 copy-start
  197.8 0.0 copy-start.6
  197.8 0.0 copy-start.7
  197.8 0.1 maximum_bitcast_fusion
  197.9 0.6 copy.63
  198.5 0.0 copy-start.19
  198.6 0.0 copy-start.2
  198.6 0.0 copy-start.25
  198.6 0.0 copy-start.26
  198.6 1.1 reshape.76
  199.7 1.1 fusion.12
  200.9 1.1 fusion.10
  202.1 0.6 multiply_subtract_fusion.4
  202.7 0.9 multiply_subtract_fusion.5
  (45 shorter events, 0.1 us)
Async XLA Ops:
  190.4 5.2 %copy-start.11 = (f32[48,768]{1,0:T(8,128)S(1)}, f32[48,768]{1,0:T(8,128)}, u32[]{:S(2)}) copy-start(f32[48,768]{1,0:T(8,128)} %get-tuple-element.58) | copy-start | bytes 442372
  190.4 5.2 %copy-start.18 = (f32[48,384]{1,0:T(8,128)S(1)}, f32[48,384]{1,0:T(8,128)}, u32[]{:S(2)}) copy-start(f32[48,384]{1,0:T(8,128)} %get-tuple-element.59) | copy-start | bytes 221188
  190.4 5.2 %copy-start.3 = (f32[48,3,384]{2,0,1:T(8,128)S(1)}, f32[48,3,384]{2,0,1:T(8,128)}, u32[]{:S(2)}) copy-start(f32[48,3,384]{2,0,1:T(8,128)} %param.25) | copy-start | bytes 663556
  190.4 5.2 %copy-start.9 = (f32[48,3,384]{2,0,1:T(8,128)S(1)}, f32[48,3,384]{2,0,1:T(8,128)}, u32[]{:S(2)}) copy-start(f32[48,3,384]{2,0,1:T(8,128)} %param.26) | copy-start | bytes 663556
  190.5 5.2 %copy-start.10 = (f32[48,3,384]{2,0,1:T(8,128)S(1)}, f32[48,3,384]{2,0,1:T(8,128)}, u32[]{:S(2)}) copy-start(f32[48,3,384]{2,0,1:T(8,128)} %param.27) | copy-start | bytes 663556
  190.5 6.2 %copy-start.8 = (f32[24,768]{1,0:T(8,128)S(1)}, f32[24,768]{1,0:T(8,128)}, u32[]{:S(2)}) copy-start(f32[24,768]{1,0:T(8,128)} %refs_7_.1) | copy-start | bytes 221188
  190.5 6.2 %copy-start.16 = (f32[24,768]{1,0:T(8,128)S(1)}, f32[24,768]{1,0:T(8,128)}, u32[]{:S(2)}) copy-start(f32[24,768]{1,0:T(8,128)} %param.29) | copy-start | bytes 221188
  190.5 6.2 %copy-start.17 = (f32[24,768]{1,0:T(8,128)S(1)}, f32[24,768]{1,0:T(8,128)}, u32[]{:S(2)}) copy-start(f32[24,768]{1,0:T(8,128)} %param.30) | copy-start | bytes 221188
  190.5 6.2 %copy-start.20 = (f32[32,768]{1,0:T(8,128)S(1)}, f32[32,768]{1,0:T(8,128)}, u32[]{:S(2)}) copy-start(f32[32,768]{1,0:T(8,128)} %get-tuple-element.60) | copy-start | bytes 294916
  190.5 6.9 %copy-start.15 = (f32[48,768]{1,0:T(8,128)S(1)}, f32[48,768]{1,0:T(8,128)}, u32[]{:S(2)}) copy-start(f32[48,768]{1,0:T(8,128)} %get-tuple-element.62) | copy-start | bytes 442372
  195.6 2.0 copy-start.14
  196.6 3.1 %copy-start.1 = (f32[48,1536]{1,0:T(8,128)S(1)}, f32[48,1536]{1,0:T(8,128)}, u32[]{:S(2)}) copy-start(f32[48,1536]{1,0:T(8,128)} %param.31) | copy-start | bytes 884740
  196.6 3.1 %copy-start.4 = (f32[48,1536]{1,0:T(8,128)S(1)}, f32[48,1536]{1,0:T(8,128)}, u32[]{:S(2)}) copy-start(f32[48,1536]{1,0:T(8,128)} %param.32) | copy-start | bytes 884740
  196.6 3.1 %copy-start.5 = (f32[48,1536]{1,0:T(8,128)S(1)}, f32[48,1536]{1,0:T(8,128)}, u32[]{:S(2)}) copy-start(f32[48,1536]{1,0:T(8,128)} %param.33) | copy-start | bytes 884740
  197.8 3.0 %copy-start.12 = (f32[48,768]{1,0:T(8,128)S(1)}, f32[48,768]{1,0:T(8,128)}, u32[]{:S(2)}) copy-start(f32[48,768]{1,0:T(8,128)} %get-tuple-element.63) | copy-start | bytes 442372
  197.8 3.1 %copy-start.13 = (f32[48,768]{1,0:T(8,128)S(1)}, f32[48,768]{1,0:T(8,128)}, u32[]{:S(2)}) copy-start(f32[48,768]{1,0:T(8,128)} %get-tuple-element.64) | copy-start | bytes 442372
  197.8 3.1 %copy-start = (f32[96,768]{1,0:T(8,128)S(1)}, f32[96,768]{1,0:T(8,128)}, u32[]{:S(2)}) copy-start(f32[96,768]{1,0:T(8,128)} %refs_9_.1) | copy-start | bytes 884740
  197.8 3.1 %copy-start.6 = (f32[96,768]{1,0:T(8,128)S(1)}, f32[96,768]{1,0:T(8,128)}, u32[]{:S(2)}) copy-start(f32[96,768]{1,0:T(8,128)} %param.35) | copy-start | bytes 884740
  197.8 3.1 %copy-start.7 = (f32[96,768]{1,0:T(8,128)S(1)}, f32[96,768]{1,0:T(8,128)}, u32[]{:S(2)}) copy-start(f32[96,768]{1,0:T(8,128)} %param.36) | copy-start | bytes 884740
  198.5 3.5 %copy-start.21 = (f32[8,768]{1,0:T(8,128)S(1)}, f32[8,768]{1,0:T(8,128)}, u32[]{:S(2)}) copy-start(f32[8,768]{1,0:T(8,128)} %get-tuple-element.65) | copy-start | bytes 73732
  198.5 3.5 %copy-start.19 = (f32[2,768]{1,0:T(2,128)S(1)}, f32[2,768]{1,0:T(2,128)}, u32[]{:S(2)}) copy-start(f32[2,768]{1,0:T(2,128)} %refs_6_.1) | copy-start | bytes 18436
  198.5 3.5 %copy-start.23 = (f32[2,768]{1,0:T(2,128)S(1)}, f32[2,768]{1,0:T(2,128)}, u32[]{:S(2)}) copy-start(f32[2,768]{1,0:T(2,128)} %param.38) | copy-start | bytes 18436
  198.6 3.5 %copy-start.24 = (f32[2,768]{1,0:T(2,128)S(1)}, f32[2,768]{1,0:T(2,128)}, u32[]{:S(2)}) copy-start(f32[2,768]{1,0:T(2,128)} %param.39) | copy-start | bytes 18436
  198.6 4.1 %copy-start.2 = (f32[512,32]{1,0:T(8,128)S(1)}, f32[512,32]{1,0:T(8,128)}, u32[]{:S(2)}) copy-start(f32[512,32]{1,0:T(8,128)} %constant.21.clone.refs_5_) | copy-start | bytes 196612
  198.6 4.1 %copy-start.22 = (f32[32,6]{0,1:T(8,128)S(1)}, f32[32,6]{0,1:T(8,128)}, u32[]{:S(2)}) copy-start(f32[32,6]{0,1:T(8,128)} %param.40) | copy-start | bytes 2308
  198.6 4.1 %copy-start.25 = (f32[32,6]{0,1:T(8,128)S(1)}, f32[32,6]{0,1:T(8,128)}, u32[]{:S(2)}) copy-start(f32[32,6]{0,1:T(8,128)} %param.41) | copy-start | bytes 2308
  198.6 4.1 %copy-start.26 = (f32[32,6]{0,1:T(8,128)S(1)}, f32[32,6]{0,1:T(8,128)}, u32[]{:S(2)}) copy-start(f32[32,6]{0,1:T(8,128)} %param.42) | copy-start | bytes 2308

commit v5 on v4

--- a/solution.py
+++ b/solution.py
@@ -84,11 +84,14 @@
         out_shape=[jax.ShapeDtypeStruct(o[1], o[2]) for o in outs],
         scratch_shapes=[s[1] for s in scratch],
         compiler_params=pltpu.CompilerParams(
-            collective_id=collective, has_side_effects=True, vmem_limit_bytes=limit * MIB
+            collective_id=collective, has_side_effects=collective is not None, vmem_limit_bytes=limit * MIB
         ),
         name=name,
     )(*[i[1] for i in ins])
-    return dict(zip([o[0] for o in outs], results))
+    space = Refs()
+    for out, result in zip(outs, results, strict=True):
+        setattr(space, out[0], result)
+    return space
 
 
 ANY = pl.BlockSpec(memory_space=pl.ANY)
@@ -512,10 +515,12 @@
         greet(links.peers() + [partner()])
         gather.own(0)
         gather.own(1)
-        gather.put(2, r.own_e[0])
-        gather.put(3, r.own_r[: full[3][1]].astype(BF))
-        gather.put(4, r.own_e[1])
-        gather.put(5, r.own_r[full[3][1] :].astype(BF))
+        split, rest = full[3][1], full[5][1]
+        columns = [r.own_e[:, d * (split + rest) : (d + 1) * (split + rest)].astype(BF) for d in range(n)]
+        gather.put(2, jnp.concatenate([c[:, :split] for c in columns], axis=1))
+        gather.put(3, r.own_r[:split].astype(BF))
+        gather.put(4, jnp.concatenate([c[:, split:] for c in columns], axis=1))
+        gather.put(5, r.own_r[split:].astype(BF))
     else:
         greet([partner()])
     tok_move(0, half)
@@ -531,9 +536,11 @@
     cot_move(0, half)
     if direct:
         gather.share(0)
+        gather.across(1)
         gather.own(3)
-        gather.across(1)
     cot_move(half, passages)
+    if direct:
+        gather.share(1)
     for h in range(heads):
         line = dot_exact(r.table[h : h + 1, :], r.onehot[...])
         rows = jnp.broadcast_to(line, (ROWS, 2 * ROWS))
@@ -548,8 +555,6 @@
     loop(0, count, normalise)
     local(r.buckets.at[0], r.bucket_rows, 5).wait()
     if direct:
-        gather.share(1)
-        gather.own(4)
         gather.arrived(0)
 
     def lanes(c, j):
@@ -598,9 +603,16 @@
                 r.wo[...] = wide[: n * rows, :].astype(BF)
 
             every(p, (
-                (1, gather.along, 2), (1, gather.own, 5), (2, gather.across, 2), (2, gather.along, 3),
-                (3, gather.share, 2), (4, gather.across, 3), (4, gather.along, 4), (5, gather.share, 3),
-                (6, gather.across, 4), (6, gather.along, 5), (7, gather.share, 4),
+                (0, gather.along, 2),
+                (0, gather.along, 3),
+                (1, gather.across, 2),
+                (2, gather.across, 3),
+                (2, gather.share, 2),
+                (3, gather.share, 3),
+                (3, gather.own, 4),
+                (4, gather.own, 5),
+                (6, gather.along, 4),
+                (7, gather.along, 5),
             ))
         pair.put(p, dot(ctx_slot[...], r.wo[...]))
         pl.when(p >= LAG)(lambda: settle(p - LAG))
@@ -611,7 +623,6 @@
     loop(0, count, attend)
 
     if direct:
-        gather.across(5)
         gather.arrived(2)
         gather.arrived(3)
         local(r.wi, r.wi_out, 1).start()
@@ -643,9 +654,12 @@
             backs.append((in_all[at] * slope).astype(BF))
         return jnp.concatenate(acts, axis=0), jnp.concatenate(backs, axis=0)
 
+    part_a = r.wr_a.shape[0]
+
     def outer_part(normed, c, act, back, we, wr):
-        r.acc_r[...] += dot(act, c, 0, 0)
-        r.acc_e[...] += dot(normed, back, 0, 0)
+        units = wr.shape[0]
+        r.acc_r[:units] += dot(act, c, 0, 0)
+        r.acc_e[:, :units] += dot(normed, back, 0, 0)
         return dot(act, wr[...]), dot(back, we[...], 1, 1)
 
     def first(p):
@@ -659,12 +673,12 @@
                 settle(last)
 
         if direct:
-            every(p, ((1, gather.share, 5),))
+            every(p, ((0, gather.across, 4), (1, gather.across, 5), (2, gather.share, 4), (3, gather.share, 5), ))
 
     clear()
     loop(0, count, first)
-    r.stage_r[...] = r.acc_r[...].astype(BF)
-    r.stage_e[...] = r.acc_e[...].astype(BF)
+    r.stage_r[...] = r.acc_r[:part_a].astype(BF)
+    r.stage_e[...] = r.acc_e[:, :part_a].astype(BF)
     if direct:
         sums.far(0)
         sums.far(1)
@@ -703,23 +717,24 @@
             for stream in (layer, hidden_grad):
                 stream.start(p - LAG)
             if direct:
-                every(p, ((2, sums.near, 0), (3, sums.near, 1)))
-                for a in range(2):
-                    pl.when(p == 6 + a)(partial(sums.along, a, kept[a]))
+                every(p, ((3, sums.near, 0), (4, sums.near, 1)))
 
     loop(0, LAG, lambda p: second(p, False))
     if direct:
         sums.plain(0)
         sums.plain(1)
     loop(LAG, count, second)
-    stage_rb, stage_eb = (r.wr_a, r.we_a) if direct else (r.stage_rb, r.stage_eb)
-    if direct:
-        gather.sent(2)
-        gather.sent(3)
+    stage_rb, stage_eb = (r.wr_b, r.we_b) if direct else (r.stage_rb, r.stage_eb)
+    if direct:
+        gather.sent(4)
+        gather.sent(5)
     stage_rb[...] = r.acc_r[...].astype(BF)
     stage_eb[...] = r.acc_e[...].astype(BF)
     local(stage_rb, r.grad_r, 3).start()
     local(stage_eb, r.grad_e, 4).start()
+    if direct:
+        for a in range(2):
+            sums.along(a, kept[a])
     for p in range(count - LAG, count):
         finish(p)
         for stream in (layer, hidden_grad):
@@ -727,7 +742,7 @@
     if direct:
         for a in range(2):
             sums.total(a, kept[a])
-        for a in (0, 1, 4, 5):
+        for a in range(4):
             gather.sent(a)
         for a in range(2):
             sums.sent(a)
@@ -755,37 +770,38 @@
     ins += [(k, v, VMEM) for k, v in weights.items()]
     if direct:
         part = weights["own_r"].shape[0] // 2 * n
+        rest = weights["own_r"].shape[0] * n - part
     else:
-        part = weights["wr_a"].shape[0]
-    streams = {
-        "proj": ((ROWS, 3 * width), BF),
-        "probs": ((heads, ROWS, ROWS), BF),
-        "normed": ((ROWS, d), BF),
-        "ctx": ((ROWS, width), BF),
-        "layer": ((ROWS, d), BF),
-        "hidden_grad": ((ROWS, d), F32),
-    }
+        part, rest = weights["wr_a"].shape[0], weights["wr_b"].shape[0]
+    streams = dict(
+        proj=((ROWS, 3 * width), BF),
+        probs=((heads, ROWS, ROWS), BF),
+        normed=((ROWS, d), BF),
+        ctx=((ROWS, width), BF),
+        layer=((ROWS, d), BF),
+        hidden_grad=((ROWS, d), F32),
+    )
     outs = [(k, (passages,) + shape, dtype, ANY) for k, (shape, dtype) in streams.items()]
     outs += [
         ("tok_out", (passages, ROWS, d), BF, ANY),
-        ("grad_r", (part, d), BF, ANY),
-        ("grad_e", (d, part), BF, ANY),
+        ("grad_r", (rest, d), BF, ANY),
+        ("grad_e", (d, rest), BF, ANY),
         ("gain_grad", (8, d), F32, VMEM),
     ]
-    scratch = [
-        ("tok", pltpu.VMEM((passages, ROWS, d), BF)),
-        ("cot", pltpu.VMEM((passages, ROWS, d), BF)),
-        ("window", pltpu.VMEM((2, WINDOW, d), BF)),
-        ("window_sem", pltpu.SemaphoreType.DMA((2,))),
-        ("bucket_rows", pltpu.VMEM(buckets.shape[1:], buckets.dtype)),
-        ("out_sem", pltpu.SemaphoreType.DMA((6,))),
-        ("bias", pltpu.VMEM((heads, ROWS, ROWS), F32)),
-        ("hidden", pltpu.VMEM((passages, ROWS, d), F32)),
-        ("out_sum", pltpu.VMEM((passages, ROWS, d), F32)),
-        ("in_sum", pltpu.VMEM((passages, ROWS, d), F32)),
-        ("acc_r", pltpu.VMEM((part, d), F32)),
-        ("acc_e", pltpu.VMEM((d, part), F32)),
-    ]
+    scratch = [*dict(
+        tok=pltpu.VMEM((passages, ROWS, d), BF),
+        cot=pltpu.VMEM((passages, ROWS, d), BF),
+        window=pltpu.VMEM((2, WINDOW, d), BF),
+        window_sem=pltpu.SemaphoreType.DMA((2,)),
+        bucket_rows=pltpu.VMEM(buckets.shape[1:], buckets.dtype),
+        out_sem=pltpu.SemaphoreType.DMA((6,)),
+        bias=pltpu.VMEM((heads, ROWS, ROWS), F32),
+        hidden=pltpu.VMEM((passages, ROWS, d), F32),
+        out_sum=pltpu.VMEM((passages, ROWS, d), F32),
+        in_sum=pltpu.VMEM((passages, ROWS, d), F32),
+        acc_r=pltpu.VMEM((rest, d), F32),
+        acc_e=pltpu.VMEM((d, rest), F32),
+    ).items()]
     for k, (shape, dtype) in streams.items():
         scratch += stream_scratch(k, shape, dtype)
     for name in ("pair", "in"):
@@ -800,20 +816,20 @@
             outs.append((key, shape, F32, VMEM))
         scratch += [(k, pltpu.VMEM(shape, BF)) for k, shape in stage]
         shapes = {"wi": (d, 3 * width), "wo": (width, d), "wo_wide": (n * padded, d)}
-        for half in "ab":
-            shapes["we_" + half], shapes["wr_" + half] = (d, part), (part, d)
+        for half, size in (("a", part), ("b", rest)):
+            shapes["we_" + half], shapes["wr_" + half] = (d, size), (size, d)
         scratch += [(key, pltpu.VMEM(shape, BF)) for key, shape in shapes.items()]
-        scratch += [
-            ("buf_r", pltpu.VMEM((4, nz, part // n, d), BF)),
-            ("buf_e", pltpu.VMEM((4, nz, d // n, part), BF)),
-            ("g_ss", pltpu.SemaphoreType.DMA((6, 5, nz))),
-            ("g_rs", pltpu.SemaphoreType.DMA((6, 5, nz))),
-            ("s_ss", pltpu.SemaphoreType.DMA((2, 4, nz))),
-            ("s_rs", pltpu.SemaphoreType.DMA((2, 4, nz))),
-        ]
+        scratch += [*dict(
+            buf_r=pltpu.VMEM((4, nz, part // n, d), BF),
+            buf_e=pltpu.VMEM((4, nz, d // n, part), BF),
+            g_ss=pltpu.SemaphoreType.DMA((6, 5, nz)),
+            g_rs=pltpu.SemaphoreType.DMA((6, 5, nz)),
+            s_ss=pltpu.SemaphoreType.DMA((2, 4, nz)),
+            s_rs=pltpu.SemaphoreType.DMA((2, 4, nz)),
+        ).items()]
     else:
         outs += [(k, shape, BF, VMEM) for k, shape in stage]
-        scratch += [("stage_rb", pltpu.VMEM((part, d), BF)), ("stage_eb", pltpu.VMEM((d, part), BF))]
+        scratch += [("stage_rb", pltpu.VMEM((rest, d), BF)), ("stage_eb", pltpu.VMEM((d, rest), BF))]
     kernel = partial(forward_kernel, n, passages, heads, direct)
     return run(kernel, ins, outs, scratch, 1, 63, "forward")
 
@@ -910,9 +926,9 @@
         r.acc_qk[...] += dot(normed.buf[p], r.dproj[p, :, : 2 * width], 0, 0)
         if direct:
             every(p, ((0, sums.plain, 2), (0, sums.plain, 3)))
-            for a, at in ((0, 1), (1, 2), (2, 5), (3, 6)):
+            for a, at in ((0, 4), (1, 6)):
                 pl.when(p == at)(partial(sums.along, a, kept[a]))
-            every(p, ((3, sums.near, 2), (4, sums.near, 3)))
+            every(p, ((5, sums.near, 2), (7, sums.near, 3)))
 
     loop(0, count, scores)
     r.stage_qk[...] = r.acc_qk[...].astype(BF)
@@ -955,7 +971,9 @@
         if with_finish:
             input_grad.start(t - LAG)
             if direct:
-                every(t, ((4, sums.near, 4),))
+                every(t, ((6, sums.near, 4),))
+                for a, at in ((2, 3), (3, 5)):
+                    pl.when(t == at)(partial(sums.along, a, kept[a]))
                 pl.when(t == 2)(wide.across)
                 pl.when(t == 5)(wide.over)
 
@@ -981,29 +999,29 @@
 def back(n, passages, heads, direct, f, gains, wi, wo):
     d = gains.shape[1]
     width = heads * DH
-    streams = {
-        "ctx": ((ROWS, width), BF),
-        "normed": ((ROWS, d), BF),
-        "probs": ((heads, ROWS, ROWS), BF),
-        "proj": ((ROWS, 3 * width), BF),
-        "tok": ((ROWS, d), BF),
-        "hidden_grad": ((ROWS, d), F32),
-    }
-    ins = [(k, f["tok_out" if k == "tok" else k], ANY) for k in streams]
-    fixed = [("gains", gains), ("wi", wi), ("wo", wo), ("gain_two", f["gain_grad"])]
+    streams = dict(
+        ctx=((ROWS, width), BF),
+        normed=((ROWS, d), BF),
+        probs=((heads, ROWS, ROWS), BF),
+        proj=((ROWS, 3 * width), BF),
+        tok=((ROWS, d), BF),
+        hidden_grad=((ROWS, d), F32),
+    )
+    ins = [(k, f.tok_out if k == "tok" else getattr(f, k), ANY) for k in streams]
+    fixed = [("gains", gains), ("wi", wi), ("wo", wo), ("gain_two", f.gain_grad)]
     outs = [
         ("input_grad", (passages, ROWS, d), F32, ANY),
         ("wide_sum", (8, d), F32, VMEM),
     ]
-    scratch = [
-        ("acc_qk", pltpu.VMEM((d, 2 * width), F32)),
-        ("acc_v", pltpu.VMEM((d, width), F32)),
-        ("acc_o", pltpu.VMEM((width, d), F32)),
-        ("acc_s", pltpu.VMEM((heads, ROWS, ROWS), F32)),
-        ("dctx", pltpu.VMEM((passages, ROWS, width), BF)),
-        ("dproj", pltpu.VMEM((passages, ROWS, 3 * width), BF)),
-        ("wide", pltpu.VMEM((8, d), F32)),
-    ] + swap_scratch("in", d)
+    scratch = [*dict(
+        acc_qk=pltpu.VMEM((d, 2 * width), F32),
+        acc_v=pltpu.VMEM((d, width), F32),
+        acc_o=pltpu.VMEM((width, d), F32),
+        acc_s=pltpu.VMEM((heads, ROWS, ROWS), F32),
+        dctx=pltpu.VMEM((passages, ROWS, width), BF),
+        dproj=pltpu.VMEM((passages, ROWS, 3 * width), BF),
+        wide=pltpu.VMEM((8, d), F32),
+    ).items()] + swap_scratch("in", d)
     for k, (shape, dtype) in streams.items():
         scratch.append((k + "_buf", pltpu.VMEM((passages,) + shape, dtype)))
         scratch.append((k + "_sem", pltpu.SemaphoreType.DMA((passages,))))
@@ -1015,28 +1033,167 @@
     stage = [("stage_o", (rows_o, d)), ("stage_v", (d, width)), ("stage_qk", (d, 2 * width))]
     if direct:
         nz = n // 4
-        fixed += [(k, f[k]) for k in ("grad_r", "grad_e")]
+        fixed += [(k, getattr(f, k)) for k in ("grad_r", "grad_e")]
         scratch += [(k, pltpu.VMEM(shape, BF)) for k, shape in stage]
-        blocks = {"r": f["grad_r"].shape, "e": f["grad_e"].shape}
+        blocks = {"r": f.grad_r.shape, "e": f.grad_e.shape}
         blocks.update({k[6:]: shape for k, shape in stage})
         for key, shape in blocks.items():
             shape = (shape[0] // n, shape[1])
             scratch.append(("buf_" + key, pltpu.VMEM((4, nz) + shape, BF)))
             outs.append(("sum_" + key, shape, F32, VMEM))
-        scratch += [
-            ("wide_z", pltpu.VMEM((nz, 8, d), F32)),
-            ("wide_xy", pltpu.VMEM((4, 8, d), F32)),
-            ("wide_mp", pltpu.VMEM((8, d), F32)),
-            ("s_ss", pltpu.SemaphoreType.DMA((len(blocks), 4, nz))),
-            ("s_rs", pltpu.SemaphoreType.DMA((len(blocks), 4, nz))),
-            ("w_ss", pltpu.SemaphoreType.DMA((2, max(nz, 4)))),
-            ("w_rs", pltpu.SemaphoreType.DMA((2, max(nz, 4)))),
-        ]
+        scratch += [*dict(
+            wide_z=pltpu.VMEM((nz, 8, d), F32),
+            wide_xy=pltpu.VMEM((4, 8, d), F32),
+            wide_mp=pltpu.VMEM((8, d), F32),
+            s_ss=pltpu.SemaphoreType.DMA((len(blocks), 4, nz)),
+            s_rs=pltpu.SemaphoreType.DMA((len(blocks), 4, nz)),
+            w_ss=pltpu.SemaphoreType.DMA((2, max(nz, 4))),
+            w_rs=pltpu.SemaphoreType.DMA((2, max(nz, 4))),
+        ).items()]
     else:
         outs += [(k, shape, BF, VMEM) for k, shape in stage]
     ins += [(k, v, VMEM) for k, v in fixed]
     kernel = partial(back_kernel, n, passages, heads, direct)
     return run(kernel, ins, outs, scratch, 2, 63, "back")
+
+
+rates = {
+    "i": rate_inward, "o": rate_outward, "e": rate_expand, "r": rate_reduce, "g": rate_gains, "t": rate_table,
+}
+
+
+def update_kernel(n, passages, heads, keys, r):
+    total = r.layer_out.shape[0]
+    ins = [(getattr(r, k), getattr(r, k + "_in")) for k in keys]
+    fetch = {k: pltpu.make_async_copy(a, b, r.in_sem.at[i]) for i, (k, (a, b)) in enumerate(zip(keys, ins))}
+    stores = []
+
+    def store(src, dst):
+        copy = pltpu.make_async_copy(src, dst, r.out_sem.at[len(stores)])
+        copy.start()
+        stores.append(copy)
+
+    def passage(name, p, sem):
+        return pltpu.make_async_copy(getattr(r, name).at[p], getattr(r, name + "_in").at[p], sem.at[p])
+
+    for k in keys:
+        fetch[k].start()
+    for p in range(passages):
+        passage("grad", p, r.grad_sem).start()
+        passage("layer", p, r.layer_sem).start()
+
+    def get(k):
+        fetch[k].wait()
+        return getattr(r, k + "_in")
+
+    def step(key, gradient, at=...):
+        out = adamw(*(getattr(r, key + part + "_in")[at] for part in "wmv"), gradient, rates[key])
+        for part, value in zip(("_nw", "_nm", "_nv"), out):
+            getattr(r, key + part + "_out")[at] = value
+        if key not in "gt":
+            getattr(r, key + "_nc_out")[at] = out[0].astype(BF)
+
+    def ready(key):
+        for part in "wmv":
+            fetch[key + part].wait()
+
+    def done(key):
+        for part in ("_nw", "_nm", "_nv") + ("_nc",) * (key not in "gt"):
+            store(getattr(r, key + part + "_out"), getattr(r, key + part))
+
+    first_r, first_e = get("first_r"), get("first_e")
+    second_r, second_e = get("second_r"), get("second_e")
+    ready("r")
+    split = first_r.shape[0]
+    step("r", first_r[...], slice(0, split))
+    step("r", second_r[...], slice(split, split + second_r.shape[0]))
+    done("r")
+    ready("e")
+    one, two = first_e.shape[1] // n, second_e.shape[1] // n
+    columns = []
+    for d in range(n):
+        columns += [first_e[:, d * one : (d + 1) * one], second_e[:, d * two : (d + 1) * two]]
+    step("e", jnp.concatenate(columns, axis=1))
+    done("e")
+    ready("o")
+    step("o", get("sum_o")[: r.ow_in.shape[0]])
+    done("o")
+    ready("i")
+    qk, v = get("sum_qk"), get("sum_v")
+    width = v.shape[1]
+    step("i", qk[:, :width], 0)
+    step("i", qk[:, width:], 1)
+    step("i", v[...], 2)
+    done("i")
+    ready("g")
+    small = get("small")
+    step("g", small[heads + 1 : heads + 2], slice(0, 1))
+    step("g", small[heads : heads + 1], slice(1, 2))
+    done("g")
+    ready("t")
+    onehot = get("onehot")
+    step("t", lax.dot_general(
+        small[:heads, : 2 * ROWS], onehot[...], (((1,), (0,)), ((), ())),
+        precision=lax.Precision.HIGHEST, preferred_element_type=F32,
+    ))
+    done("t")
+    sent = 0
+    for p in range(passages):
+        at = slice(p * PLEN, (p + 1) * PLEN)
+        passage("grad", p, r.grad_sem).wait()
+        r.grad_rows[at] = r.grad_in[p, :PLEN]
+        passage("layer", p, r.layer_sem).wait()
+        r.layer_wide[at] = r.layer_in[p, :PLEN].astype(F32)
+        end = total if p == passages - 1 else (p + 1) * PLEN // 16 * 16
+        rows = slice(sent, end)
+        store(r.grad_rows.at[rows], r.input_grad.at[rows])
+        r.layer_rows[rows] = r.layer_wide[rows].astype(BF)
+        store(r.layer_rows.at[rows], r.layer_out.at[rows])
+        sent = end
+    for copy in stores:
+        copy.wait()
+
+
+def update(n, passages, heads, shape, f, b, onehot, states):
+    total, d = shape
+    small = dict(first_r=f.sum_r, first_e=f.sum_e, second_r=b.sum_r, second_e=b.sum_e)
+    ins = [(k, v) for k, v in small.items()]
+    ins += [(key + part, a) for key in "reo" for part, a in zip("wmv", states[key])]
+    ins += [("sum_o", b.sum_o), ("sum_qk", b.sum_qk), ("sum_v", b.sum_v)]
+    ins += [("small", b.wide_sum), ("onehot", onehot)]
+    ins += [(key + part, a) for key in "igt" for part, a in zip("wmv", states[key])]
+    keys = [k for k, _ in ins]
+    scratch = [(k + "_in", pltpu.VMEM(a.shape, a.dtype)) for k, a in ins]
+    outs = []
+    for key in "ioergt":
+        for part in ("_nw", "_nm", "_nv") + ("_nc",) * (key not in "gt"):
+            outs.append((key + part, states[key][0].shape, BF if part == "_nc" else F32, ANY))
+    scratch += [(k + "_out", pltpu.VMEM(dims, dtype)) for k, dims, dtype, _ in outs]
+    padded = (passages, ROWS, d)
+    count = len(outs) + 2 * passages
+    scratch += [*dict(
+        grad_in=pltpu.VMEM(padded, F32),
+        layer_in=pltpu.VMEM(padded, BF),
+        grad_rows=pltpu.VMEM((total, d), F32),
+        layer_wide=pltpu.VMEM((total, d), F32),
+        layer_rows=pltpu.VMEM((total, d), BF),
+        in_sem=pltpu.SemaphoreType.DMA((len(keys),)),
+        out_sem=pltpu.SemaphoreType.DMA((count,)),
+        grad_sem=pltpu.SemaphoreType.DMA((passages,)),
+        layer_sem=pltpu.SemaphoreType.DMA((passages,)),
+    ).items()]
+    ins += [("layer", f.layer), ("grad", b.input_grad)]
+    outs += [("layer_out", shape, BF, ANY), ("input_grad", shape, F32, ANY)]
+    kernel = partial(update_kernel, n, passages, heads, keys)
+    o = run(kernel, [(k, a, ANY) for k, a in ins], outs, scratch, None, 60, "update")
+    new = [o.layer_out, o.input_grad]
+    for key in "ioergt":
+        for part in ("_nw", "_nm", "_nv") + ("_nc",) * (key not in "gt"):
+            value = getattr(o, key + part)
+            if key == "i":
+                value = value.transpose(1, 0, 2)
+            new.append(value.T if key == "t" else value)
+    return tuple(new)
 
 
 def shards(
@@ -1067,26 +1224,20 @@
     passages = tokens.shape[0] // PLEN
     heads = inward_master.shape[2] // DH
     width = heads * DH
-    rows_i, rows_e, rows_r = inward_master.shape[0], expand_master.shape[0], reduce_master.shape[0]
+    rows_i, rows_r = inward_master.shape[0], reduce_master.shape[0]
     units = expand_master.shape[1]
     direct = n % 8 == 0 and rows_i % 16 == 0 and rows_r % 32 == 0 and outward_master.shape[0] % 8 == 0
-
-    def unit_halves(a):
-        return a.reshape(rows_e, n, 2, units // (2 * n)).transpose(2, 0, 1, 3).reshape(2, rows_e, -1)
-
-    def unit_order(a):
-        return a.reshape(2, rows_e, n, units // (2 * n)).transpose(1, 2, 0, 3).reshape(rows_e, units)
 
     onehot = jnp.asarray(distance_onehot())
     bucket_rows = buckets.transpose(1, 0, 2)
     table_rows = table_master.T
     if direct:
-        weights = {
-            "own_i": inward_master.transpose(1, 0, 2),
-            "own_o": outward_master,
-            "own_e": unit_halves(expand_master.astype(BF)),
-            "own_r": reduce_master,
-        }
+        weights = dict(
+            own_i=inward_master.transpose(1, 0, 2),
+            own_o=outward_master,
+            own_e=expand_master,
+            own_r=reduce_master,
+        )
     else:
         masters = (inward_master.reshape(-1, 3 * width), outward_master, expand_master, reduce_master)
         wi, wo, we, wr = (
@@ -1099,24 +1250,28 @@
         n, passages, heads, direct, tokens, cotangent, bucket_rows, gains_master, table_rows, onehot, weights
     )
     if direct:
-        wi, wo = f["wi_out"], f["wo_out"]
+        wi, wo = f.wi_out, f.wo_out
     b = back(n, passages, heads, direct, f, gains_master, wi, wo)
 
     def scatter(g):
         return lax.psum_scatter(g.astype(F32), "dp", scatter_dimension=0, tiled=True)
 
     if direct:
-        inward_sum = jnp.concatenate([b["sum_qk"], b["sum_v"]], axis=1)
-        outward_sum = b["sum_o"][: outward_master.shape[0]]
-        expand_sum = unit_order(jnp.stack([f["sum_e"], b["sum_e"]]))
-        reduce_sum = jnp.concatenate([f["sum_r"], b["sum_r"]], axis=0)
-        wide_sum = b["wide_sum"]
+        states = dict(
+            i=tuple(a.transpose(1, 0, 2) for a in (inward_master, inward_first, inward_second)),
+            o=(outward_master, outward_first, outward_second),
+            e=(expand_master, expand_first, expand_second),
+            r=(reduce_master, reduce_first, reduce_second),
+            g=(gains_master, gains_first, gains_second),
+            t=(table_master.T, table_first.T, table_second.T),
+        )
+        return update(n, passages, heads, tokens.shape, f, b, onehot, states)
     else:
-        inward_sum = scatter(jnp.concatenate([b["stage_qk"], b["stage_v"]], axis=1))
-        outward_sum = scatter(b["stage_o"])
-        expand_sum = scatter(jnp.concatenate([f["stage_e"], f["grad_e"]], axis=1))
-        reduce_sum = scatter(jnp.concatenate([f["stage_r"], f["grad_r"]], axis=0))
-        wide_sum = lax.psum(b["wide_sum"], "dp")
+        inward_sum = scatter(jnp.concatenate([b.stage_qk, b.stage_v], axis=1))
+        outward_sum = scatter(b.stage_o)
+        expand_sum = scatter(jnp.concatenate([f.stage_e, f.grad_e], axis=1))
+        reduce_sum = scatter(jnp.concatenate([f.stage_r, f.grad_r], axis=0))
+        wide_sum = lax.psum(b.wide_sum, "dp")
         gains = lax.psum(wide_sum[heads : heads + 2], "mp")
         wide_sum = jnp.concatenate([wide_sum[:heads], gains], axis=0)
     inward_sum = inward_sum.reshape(inward_master.shape)
@@ -1125,8 +1280,8 @@
         onehot.T, wide_sum[:heads, : 2 * ROWS], (((1,), (1,)), ((), ())), precision=lax.Precision.HIGHEST
     )
 
-    layer_out = f["layer"][:, :PLEN].reshape(tokens.shape)
-    input_grad = b["input_grad"][:, :PLEN].reshape(tokens.shape)
+    layer_out = f.layer[:, :PLEN].reshape(tokens.shape)
+    input_grad = b.input_grad[:, :PLEN].reshape(tokens.shape)
     outputs = [layer_out, input_grad]
     for w, first_moment, second_moment, gradient, rate, copied in (
         (inward_master, inward_first, inward_second, inward_sum, rate_inward, True),

time: 204 us -> 193 us (0.946)
  local copies, waits for them, and re-layouts: 12.2 us -> 0 us
  Pallas kernels: 184 us -> 191 us
  other arithmetic: 5.59 us -> 0 us
    reshape x6 -> x0, local copies, waits for them, and re-layouts: 11.1 us -> none  [the longest x1 5.06 us: shards(): input_grad = b['input_grad'][:, :PLEN].reshape(tokens.shape)]
    pallas_call x2 -> x3, Pallas kernels: 184 us -> 191 us  [run(): pl.pallas_call(body, in_specs=[i[2] for i in ins], out_specs=[o[3] for o...]
    convert_element_type x5 -> x0, other arithmetic: 4.89 us -> none  [the longest x4 3.91 us: shards(): outputs.append(new[0].astype(BF))]
where the time goes in v5:
time: 193 us; the launch traced here: 192 us
  Pallas kernels  191 us (99%)
    pallas_call x3, Pallas kernels, run(): pl.pallas_call(body, in_specs=[i[2] for i in ins], out_specs=[o[3] for o...  191 us

profile of v5, /device:TPU:0, one launch (start us, length us, event | category | flops | bytes accessed | tf_op | source)
XLA Modules:
  0.0 192.3 jit_solution(3066983934350496925)
XLA Ops:
  0.7 121.5 %forward.1 = (bf16[8,256,1152]{2,1,0:T(8,128)(2,1)}, bf16[8,6,256,256]{3,2,1,0:T(8,128)(2,1)}, bf16[8,256,768]{2,1,0:T(8,128)(2,1)}, bf16[8,256,384]{2,1,0:T(8,1...) custom-call(bf16[2000,768]{1,0:T(8,128)(2,1)} %refs_0_.1, ...), custom_call_target="tpu_custom_call" | custom-call | tf_op jit(solution)/shard_map/forward/pallas_call | solution.py:80
  122.2 59.5 %back.1 = (f32[8,256,768]{2,1,0:T(8,128)}, f32[8,768]{1,0:T(8,128)}, f32[48,768]{1,0:T(8,128)}, f32[48,768]{1,0:T(8,128)}, f32[32,768]{1,0:T(8,128)}, /*index=5*/f32[48,384]{1,0:T(8,128)}, f32[48,768]{1,0:T(8,128)}) custom-call(bf16[8,256,384]{2,1,0:T(8,128)(2,1)} %get-tuple-element.71.refs_0_, bf16[8,256,768]{2,1,0:T(8,128)(2,1)} %get-tuple-element.72.refs_1_, ...), custom_call_target="tpu_custom_call" | custom-call | tf_op jit(solution)/shard_map/back/pallas_call | solution.py:80
  181.8 10.4 %update.1 = (f32[3,48,384]{2,1,0:T(8,128)}, f32[3,48,384]{2,1,0:T(8,128)}, f32[3,48,384]{2,1,0:T(8,128)}, bf16[3,48,384]{2,1,0:T(8,128)(2,1)}, f32[24,768]{1,0:T...) custom-call(f32[48,768]{1,0:T(8,128)} %get-tuple-element.69.refs_0_,, ...), custom_call_target="tpu_custom_call" | custom-call | tf_op jit(solution)/shard_map/update/pallas_call | solution.py:80

commit v6 on v5

--- a/solution.py
+++ b/solution.py
@@ -297,7 +297,7 @@
             self.bufs[a][0, k] = mine.astype(BF)
             self.copy(a, role, k, self.bufs[a].at[0, k], role, peer).start()
 
-    def along(self, a, kept):
+    def along(self, a, kept, held=None):
         l = self.l
         for k in list(range(1, l.nz)) + [0]:
             self.arrive(a, 1, k, 1)
@@ -309,6 +309,8 @@
             )
             if k == 0:
                 kept[...] = mine
+            elif held is not None:
+                held[k] = mine.astype(BF)
             else:
                 self.bufs[a][1, k] = mine.astype(BF)
                 self.copy(a, 3, k, self.bufs[a].at[1, k], 3, l.z_peer(k)).start()
@@ -320,9 +322,9 @@
             total += self.bufs[a][3, k].astype(F32)
         kept[...] = total
 
-    def sent(self, a):
+    def sent(self, a, held=False):
         for k in range(self.l.nz):
-            for role in (0, 1, 2) + (3,) * (k > 0):
+            for role in (0, 1, 2) + (3,) * (k > 0 and not held):
                 self.copy(a, role, k, self.part(a, 0), 0, self.l.x_peer).wait_send()
 
 
@@ -492,11 +494,11 @@
         links = Links(n)
         rows_o = r.wo_wide.shape[0] // n
         full = [(r.wi, r.wi.shape[0] // n, None), (r.wo_wide, rows_o, None)]
-        full += [(w, w.shape[0] // n, None) for w in (r.we_a, r.wr_a, r.we_b, r.wr_b)]
+        full += [(w, w.shape[0] // n, None) for w in (r.we_a, r.wr_a, r.we_b, r.wr_b, r.we_c, r.wr_c)]
         gather = Gather(links, full, r.g_ss, r.g_rs)
-        grads = [(g, g.shape[0] // n) for g in (r.stage_r, r.stage_e)]
-        kept = [r.sum_r, r.sum_e]
-        sums = Scatter(links, grads, [r.buf_r, r.buf_e], r.s_ss, r.s_rs)
+        grads = [(g, g.shape[0] // n) for g in (r.stage_ra, r.stage_ea, r.stage_rb, r.stage_eb)]
+        kept = [r.sum_ra, r.sum_ea, r.sum_rb, r.sum_eb]
+        sums = Scatter(links, grads, [r.buf_ra, r.buf_ea, r.buf_rb, r.buf_eb], r.s_ss, r.s_rs)
     tok_start, tok_move = align(r.tokens, r.tok, r.window, r.window_sem, passages)
     cot_start, cot_move = align(r.cotangent, r.cot, r.window, r.window_sem, passages)
     half = passages // 2
@@ -515,12 +517,12 @@
         greet(links.peers() + [partner()])
         gather.own(0)
         gather.own(1)
-        split, rest = full[3][1], full[5][1]
-        columns = [r.own_e[:, d * (split + rest) : (d + 1) * (split + rest)].astype(BF) for d in range(n)]
-        gather.put(2, jnp.concatenate([c[:, :split] for c in columns], axis=1))
-        gather.put(3, r.own_r[:split].astype(BF))
-        gather.put(4, jnp.concatenate([c[:, split:] for c in columns], axis=1))
-        gather.put(5, r.own_r[split:].astype(BF))
+        third = full[3][1]
+        columns = [r.own_e[:, d * 3 * third : (d + 1) * 3 * third].astype(BF) for d in range(n)]
+        for i in range(3):
+            at = slice(i * third, (i + 1) * third)
+            gather.put(2 + 2 * i, jnp.concatenate([c[:, at] for c in columns], axis=1))
+            gather.put(3 + 2 * i, r.own_r[at].astype(BF))
     else:
         greet([partner()])
     tok_move(0, half)
@@ -603,16 +605,10 @@
                 r.wo[...] = wide[: n * rows, :].astype(BF)
 
             every(p, (
-                (0, gather.along, 2),
-                (0, gather.along, 3),
-                (1, gather.across, 2),
-                (2, gather.across, 3),
-                (2, gather.share, 2),
-                (3, gather.share, 3),
-                (3, gather.own, 4),
-                (4, gather.own, 5),
-                (6, gather.along, 4),
-                (7, gather.along, 5),
+                (0, gather.along, 2), (0, gather.along, 3), (0, gather.own, 4), (1, gather.across, 2),
+                (1, gather.own, 5), (2, gather.across, 3), (2, gather.share, 2), (3, gather.share, 3),
+                (3, gather.along, 4), (4, gather.along, 5), (4, gather.own, 6), (5, gather.across, 4),
+                (5, gather.own, 7), (6, gather.across, 5), (6, gather.share, 4), (7, gather.share, 5),
             ))
         pair.put(p, dot(ctx_slot[...], r.wo[...]))
         pl.when(p >= LAG)(lambda: settle(p - LAG))
@@ -654,13 +650,14 @@
             backs.append((in_all[at] * slope).astype(BF))
         return jnp.concatenate(acts, axis=0), jnp.concatenate(backs, axis=0)
 
-    part_a = r.wr_a.shape[0]
-
     def outer_part(normed, c, act, back, we, wr):
-        units = wr.shape[0]
-        r.acc_r[:units] += dot(act, c, 0, 0)
-        r.acc_e[:, :units] += dot(normed, back, 0, 0)
+        r.acc_r[...] += dot(act, c, 0, 0)
+        r.acc_e[...] += dot(normed, back, 0, 0)
         return dot(act, wr[...]), dot(back, we[...], 1, 1)
+
+    def staged(stage_r, stage_e):
+        stage_r[...] = r.acc_r[...].astype(BF)
+        stage_e[...] = r.acc_e[...].astype(BF)
 
     def first(p):
         normed, c = normed_two(p), r.cot[p]
@@ -673,17 +670,39 @@
                 settle(last)
 
         if direct:
-            every(p, ((0, gather.across, 4), (1, gather.across, 5), (2, gather.share, 4), (3, gather.share, 5), ))
+            every(p, (
+                (0, gather.along, 6), (1, gather.along, 7), (2, gather.across, 6), (3, gather.across, 7),
+                (4, gather.share, 6), (5, gather.share, 7),
+            ))
 
     clear()
     loop(0, count, first)
-    r.stage_r[...] = r.acc_r[:part_a].astype(BF)
-    r.stage_e[...] = r.acc_e[:, :part_a].astype(BF)
+    staged(r.stage_ra, r.stage_ea)
     if direct:
         sums.far(0)
         sums.far(1)
         gather.arrived(4)
         gather.arrived(5)
+    clear()
+
+    def middle(p):
+        normed, c = normed_two(p), r.cot[p]
+        act, back = inner_part(normed, c, r.we_b, r.wr_b)
+        r_part, n_part = outer_part(normed, c, act, back, r.we_b, r.wr_b)
+        r.out_sum[p] += r_part
+        r.in_sum[p] += n_part
+        if direct:
+            every(p, ((1, sums.plain, 0), (1, sums.plain, 1), (4, sums.near, 0), (6, sums.near, 1)))
+
+    loop(0, count, middle)
+    staged(r.stage_rb, r.stage_eb)
+    if direct:
+        sums.far(2)
+        sums.far(3)
+        sums.plain(2)
+        sums.plain(3)
+        gather.arrived(6)
+        gather.arrived(7)
     clear()
 
     def finish(last):
@@ -703,12 +722,12 @@
             grad_slot[at] = r.cot[last, at].astype(F32) + inv * (zed - hr * inner)
         r.gain_grad[0:1, :] += gain_rows
 
-    def second(p, with_finish=True):
+    def last_part(p, with_finish=True):
         normed, c = normed_two(p), r.cot[p]
-        act, back = inner_part(normed, c, r.we_b, r.wr_b)
+        act, back = inner_part(normed, c, r.we_c, r.wr_c)
         if with_finish:
             finish(p - LAG)
-        r_part, n_part = outer_part(normed, c, act, back, r.we_b, r.wr_b)
+        r_part, n_part = outer_part(normed, c, act, back, r.we_c, r.wr_c)
         pair.put(count + p, r.out_sum[p] + r_part)
         back_in.put(p, r.in_sum[p] + n_part)
         pair.send(count + p)
@@ -717,24 +736,23 @@
             for stream in (layer, hidden_grad):
                 stream.start(p - LAG)
             if direct:
-                every(p, ((3, sums.near, 0), (4, sums.near, 1)))
-
-    loop(0, LAG, lambda p: second(p, False))
-    if direct:
-        sums.plain(0)
-        sums.plain(1)
-    loop(LAG, count, second)
-    stage_rb, stage_eb = (r.wr_b, r.we_b) if direct else (r.stage_rb, r.stage_eb)
-    if direct:
-        gather.sent(4)
-        gather.sent(5)
-    stage_rb[...] = r.acc_r[...].astype(BF)
-    stage_eb[...] = r.acc_e[...].astype(BF)
-    local(stage_rb, r.grad_r, 3).start()
-    local(stage_eb, r.grad_e, 4).start()
-    if direct:
-        for a in range(2):
-            sums.along(a, kept[a])
+                for a, at in ((0, 2), (1, 3)):
+                    pl.when(p == at)(partial(sums.along, a, kept[a]))
+                every(p, ((4, sums.near, 2), (5, sums.near, 3)))
+
+    loop(0, LAG, lambda p: last_part(p, False))
+    loop(LAG, count, last_part)
+    stage_rc, stage_ec = (r.wr_c, r.we_c) if direct else (r.stage_rc, r.stage_ec)
+    if direct:
+        gather.sent(6)
+        gather.sent(7)
+    staged(stage_rc, stage_ec)
+    local(stage_rc, r.grad_r, 3).start()
+    local(stage_ec, r.grad_e, 4).start()
+    if direct:
+        for a, held in ((2, r.held_rb), (3, r.held_eb)):
+            held[0] = jnp.zeros(held.shape[1:], BF)
+            sums.along(a, kept[a], held)
     for p in range(count - LAG, count):
         finish(p)
         for stream in (layer, hidden_grad):
@@ -742,15 +760,15 @@
     if direct:
         for a in range(2):
             sums.total(a, kept[a])
+        for a in range(6):
+            gather.sent(a)
         for a in range(4):
-            gather.sent(a)
-        for a in range(2):
-            sums.sent(a)
+            sums.sent(a, a >= 2)
         local(r.wi, r.wi_out, 1).wait()
         local(r.wo, r.wo_out, 2).wait()
     local(r.tok, r.tok_out, 0).wait()
-    local(stage_rb, r.grad_r, 3).wait()
-    local(stage_eb, r.grad_e, 4).wait()
+    local(stage_rc, r.grad_r, 3).wait()
+    local(stage_ec, r.grad_e, 4).wait()
     for stream in (normed_out, proj, probs, ctx, layer, hidden_grad):
         stream.last()
 
@@ -769,10 +787,9 @@
     ins += [(k, v, VMEM) for k, v in (("gains", gains), ("table", table), ("onehot", onehot))]
     ins += [(k, v, VMEM) for k, v in weights.items()]
     if direct:
-        part = weights["own_r"].shape[0] // 2 * n
-        rest = weights["own_r"].shape[0] * n - part
+        part = weights["own_r"].shape[0] // 3 * n
     else:
-        part, rest = weights["wr_a"].shape[0], weights["wr_b"].shape[0]
+        part = weights["wr_a"].shape[0]
     streams = dict(
         proj=((ROWS, 3 * width), BF),
         probs=((heads, ROWS, ROWS), BF),
@@ -784,8 +801,8 @@
     outs = [(k, (passages,) + shape, dtype, ANY) for k, (shape, dtype) in streams.items()]
     outs += [
         ("tok_out", (passages, ROWS, d), BF, ANY),
-        ("grad_r", (rest, d), BF, ANY),
-        ("grad_e", (d, rest), BF, ANY),
+        ("grad_r", (part, d), BF, ANY),
+        ("grad_e", (d, part), BF, ANY),
         ("gain_grad", (8, d), F32, VMEM),
     ]
     scratch = [*dict(
@@ -799,37 +816,39 @@
         hidden=pltpu.VMEM((passages, ROWS, d), F32),
         out_sum=pltpu.VMEM((passages, ROWS, d), F32),
         in_sum=pltpu.VMEM((passages, ROWS, d), F32),
-        acc_r=pltpu.VMEM((rest, d), F32),
-        acc_e=pltpu.VMEM((d, rest), F32),
+        acc_r=pltpu.VMEM((part, d), F32),
+        acc_e=pltpu.VMEM((d, part), F32),
     ).items()]
     for k, (shape, dtype) in streams.items():
         scratch += stream_scratch(k, shape, dtype)
     for name in ("pair", "in"):
         scratch += swap_scratch(name, d)
-    stage = [("stage_r", (part, d)), ("stage_e", (d, part))]
+    stage = [("r" + half, (part, d)) for half in "ab"] + [("e" + half, (d, part)) for half in "ab"]
     if direct:
         nz = n // 4
         padded = weights["own_o"].shape[0]
         padded += -padded % 16
         outs += [("wi_out", (d, 3 * width), BF, ANY), ("wo_out", (width, d), BF, ANY)]
-        for key, shape in (("sum_r", (part // n, d)), ("sum_e", (d // n, part))):
-            outs.append((key, shape, F32, VMEM))
-        scratch += [(k, pltpu.VMEM(shape, BF)) for k, shape in stage]
+        for key, shape in stage:
+            block = (shape[0] // n, shape[1])
+            outs.append(("sum_" + key, block, F32, VMEM))
+            if key[1] == "b":
+                outs.append(("held_" + key, (nz,) + block, BF, VMEM))
+            scratch.append(("stage_" + key, pltpu.VMEM(shape, BF)))
+            scratch.append(("buf_" + key, pltpu.VMEM((4, nz) + block, BF)))
         shapes = {"wi": (d, 3 * width), "wo": (width, d), "wo_wide": (n * padded, d)}
-        for half, size in (("a", part), ("b", rest)):
-            shapes["we_" + half], shapes["wr_" + half] = (d, size), (size, d)
+        for third in "abc":
+            shapes["we_" + third], shapes["wr_" + third] = (d, part), (part, d)
         scratch += [(key, pltpu.VMEM(shape, BF)) for key, shape in shapes.items()]
         scratch += [*dict(
-            buf_r=pltpu.VMEM((4, nz, part // n, d), BF),
-            buf_e=pltpu.VMEM((4, nz, d // n, part), BF),
-            g_ss=pltpu.SemaphoreType.DMA((6, 5, nz)),
-            g_rs=pltpu.SemaphoreType.DMA((6, 5, nz)),
-            s_ss=pltpu.SemaphoreType.DMA((2, 4, nz)),
-            s_rs=pltpu.SemaphoreType.DMA((2, 4, nz)),
+            g_ss=pltpu.SemaphoreType.DMA((8, 5, nz)),
+            g_rs=pltpu.SemaphoreType.DMA((8, 5, nz)),
+            s_ss=pltpu.SemaphoreType.DMA((4, 4, nz)),
+            s_rs=pltpu.SemaphoreType.DMA((4, 4, nz)),
         ).items()]
     else:
-        outs += [(k, shape, BF, VMEM) for k, shape in stage]
-        scratch += [("stage_rb", pltpu.VMEM((rest, d), BF)), ("stage_eb", pltpu.VMEM((d, rest), BF))]
+        outs += [("stage_" + k, shape, BF, VMEM) for k, shape in stage]
+        scratch += [("stage_rc", pltpu.VMEM((part, d), BF)), ("stage_ec", pltpu.VMEM((d, part), BF))]
     kernel = partial(forward_kernel, n, passages, heads, direct)
     return run(kernel, ins, outs, scratch, 1, 63, "forward")
 
@@ -846,6 +865,11 @@
         bufs = [getattr(r, "buf_" + k) for k in names]
         kept = [getattr(r, "sum_" + k) for k in names]
         sums = Scatter(links, grads, bufs, r.s_ss, r.s_rs)
+        late = [
+            remote(held.at[k], land.at[k], r.c_ss.at[i, k], r.c_rs.at[i, k], {"dp": links.z_peer(k)})
+            for i, (held, land) in enumerate(((r.held_rb, r.land_rb), (r.held_eb, r.land_eb)))
+            for k in range(1, links.nz)
+        ]
         wide = Spread(links, r.wide, r.wide_z, r.wide_xy, r.wide_mp, r.w_ss, r.w_rs)
     ctx, normed, probs, proj, tok, hidden_grad = (
         Load(r, name) for name in ("ctx", "normed", "probs", "proj", "tok", "hidden_grad")
@@ -859,6 +883,8 @@
         stream.start()
     if direct:
         greet(links.peers() + [{"dp": links.far_peer}, partner()])
+        for copy in late:
+            copy.start()
         sums.far(0)
         sums.far(1)
     else:
@@ -885,7 +911,7 @@
         r.acc_v[...] += dot(normed.buf[p], dv, 0, 0)
         if direct:
             every(p, (
-                (2, sums.plain, 0), (3, sums.plain, 1), (5, sums.near, 0), (7, sums.near, 1),
+                (1, sums.plain, 0), (1, sums.plain, 1), (4, sums.near, 0), (6, sums.near, 1),
             ))
 
     loop(0, count, values)
@@ -926,9 +952,9 @@
         r.acc_qk[...] += dot(normed.buf[p], r.dproj[p, :, : 2 * width], 0, 0)
         if direct:
             every(p, ((0, sums.plain, 2), (0, sums.plain, 3)))
-            for a, at in ((0, 4), (1, 6)):
+            for a, at in ((0, 2), (1, 4)):
                 pl.when(p == at)(partial(sums.along, a, kept[a]))
-            every(p, ((5, sums.near, 2), (7, sums.near, 3)))
+            every(p, ((3, sums.near, 2), (5, sums.near, 3)))
 
     loop(0, count, scores)
     r.stage_qk[...] = r.acc_qk[...].astype(BF)
@@ -971,8 +997,9 @@
         if with_finish:
             input_grad.start(t - LAG)
             if direct:
-                every(t, ((6, sums.near, 4),))
-                for a, at in ((2, 3), (3, 5)):
+                every(t, ((4, sums.near, 4),))
+                pl.when(t == 7)(partial(sums.along, 4, kept[4]))
+                for a, at in ((2, 2), (3, 3)):
                     pl.when(t == at)(partial(sums.along, a, kept[a]))
                 pl.when(t == 2)(wide.across)
                 pl.when(t == 5)(wide.over)
@@ -980,9 +1007,17 @@
     loop(0, LAG, lambda t: inputs(t, False))
     loop(LAG, count, inputs)
     if direct:
+        for copy in late:
+            copy.wait()
+        for part, land, target in (
+            (r.part_rb, r.land_rb, r.sum_rb), (r.part_eb, r.land_eb, r.sum_eb),
+        ):
+            total = part[...]
+            for k in range(1, links.nz):
+                total += land[k].astype(F32)
+            target[...] = total
         for a in range(4):
             sums.total(a, kept[a])
-        sums.along(4, kept[4])
     for p in range(count - LAG, count):
         finish(p)
         input_grad.start(p)
@@ -1033,7 +1068,11 @@
     stage = [("stage_o", (rows_o, d)), ("stage_v", (d, width)), ("stage_qk", (d, 2 * width))]
     if direct:
         nz = n // 4
-        fixed += [(k, getattr(f, k)) for k in ("grad_r", "grad_e")]
+        fixed += [(k, getattr(f, k)) for k in ("grad_r", "grad_e", "held_rb", "held_eb")]
+        fixed += [("part_rb", f.sum_rb), ("part_eb", f.sum_eb)]
+        for key, shape in (("rb", f.sum_rb.shape), ("eb", f.sum_eb.shape)):
+            outs.append(("sum_" + key, shape, F32, VMEM))
+            scratch.append(("land_" + key, pltpu.VMEM((nz,) + shape, BF)))
         scratch += [(k, pltpu.VMEM(shape, BF)) for k, shape in stage]
         blocks = {"r": f.grad_r.shape, "e": f.grad_e.shape}
         blocks.update({k[6:]: shape for k, shape in stage})
@@ -1045,6 +1084,8 @@
             wide_z=pltpu.VMEM((nz, 8, d), F32),
             wide_xy=pltpu.VMEM((4, 8, d), F32),
             wide_mp=pltpu.VMEM((8, d), F32),
+            c_ss=pltpu.SemaphoreType.DMA((2, nz)),
+            c_rs=pltpu.SemaphoreType.DMA((2, nz)),
             s_ss=pltpu.SemaphoreType.DMA((len(blocks), 4, nz)),
             s_rs=pltpu.SemaphoreType.DMA((len(blocks), 4, nz)),
             w_ss=pltpu.SemaphoreType.DMA((2, max(nz, 4))),
@@ -1101,18 +1142,14 @@
         for part in ("_nw", "_nm", "_nv") + ("_nc",) * (key not in "gt"):
             store(getattr(r, key + part + "_out"), getattr(r, key + part))
 
-    first_r, first_e = get("first_r"), get("first_e")
-    second_r, second_e = get("second_r"), get("second_e")
+    pieces_r, pieces_e = ([get(key + third) for third in "abc"] for key in "re")
     ready("r")
-    split = first_r.shape[0]
-    step("r", first_r[...], slice(0, split))
-    step("r", second_r[...], slice(split, split + second_r.shape[0]))
+    third = pieces_r[0].shape[0]
+    for i, piece in enumerate(pieces_r):
+        step("r", piece[...], slice(i * third, (i + 1) * third))
     done("r")
     ready("e")
-    one, two = first_e.shape[1] // n, second_e.shape[1] // n
-    columns = []
-    for d in range(n):
-        columns += [first_e[:, d * one : (d + 1) * one], second_e[:, d * two : (d + 1) * two]]
+    columns = [piece[:, d * third : (d + 1) * third] for d in range(n) for piece in pieces_e]
     step("e", jnp.concatenate(columns, axis=1))
     done("e")
     ready("o")
@@ -1156,7 +1193,7 @@
 
 def update(n, passages, heads, shape, f, b, onehot, states):
     total, d = shape
-    small = dict(first_r=f.sum_r, first_e=f.sum_e, second_r=b.sum_r, second_e=b.sum_e)
+    small = dict(ra=f.sum_ra, rb=b.sum_rb, rc=b.sum_r, ea=f.sum_ea, eb=b.sum_eb, ec=b.sum_e)
     ins = [(k, v) for k, v in small.items()]
     ins += [(key + part, a) for key in "reo" for part, a in zip("wmv", states[key])]
     ins += [("sum_o", b.sum_o), ("sum_qk", b.sum_qk), ("sum_v", b.sum_v)]
@@ -1226,7 +1263,7 @@
     width = heads * DH
     rows_i, rows_r = inward_master.shape[0], reduce_master.shape[0]
     units = expand_master.shape[1]
-    direct = n % 8 == 0 and rows_i % 16 == 0 and rows_r % 32 == 0 and outward_master.shape[0] % 8 == 0
+    direct = n % 8 == 0 and rows_i % 16 == 0 and rows_r % 48 == 0 and outward_master.shape[0] % 8 == 0
 
     onehot = jnp.asarray(distance_onehot())
     bucket_rows = buckets.transpose(1, 0, 2)
@@ -1243,9 +1280,10 @@
         wi, wo, we, wr = (
             lax.all_gather(w.astype(BF), "dp", axis=0, tiled=True) for w in masters
         )
-        half = units // 2
+        cuts = [slice(i * units // 3, (i + 1) * units // 3) for i in range(3)]
         weights = {"wi": wi, "wo": wo}
-        weights.update({"we_a": we[:, :half], "wr_a": wr[:half], "we_b": we[:, half:], "wr_b": wr[half:]})
+        for third, at in zip("abc", cuts):
+            weights["we_" + third], weights["wr_" + third] = we[:, at], wr[at]
     f = forward(
         n, passages, heads, direct, tokens, cotangent, bucket_rows, gains_master, table_rows, onehot, weights
     )
@@ -1269,8 +1307,8 @@
     else:
         inward_sum = scatter(jnp.concatenate([b.stage_qk, b.stage_v], axis=1))
         outward_sum = scatter(b.stage_o)
-        expand_sum = scatter(jnp.concatenate([f.stage_e, f.grad_e], axis=1))
-        reduce_sum = scatter(jnp.concatenate([f.stage_r, f.grad_r], axis=0))
+        expand_sum = scatter(jnp.concatenate([f.stage_ea, f.stage_eb, f.grad_e], axis=1))
+        reduce_sum = scatter(jnp.concatenate([f.stage_ra, f.stage_rb, f.grad_r], axis=0))
         wide_sum = lax.psum(b.wide_sum, "dp")
         gains = lax.psum(wide_sum[heads : heads + 2], "mp")
         wide_sum = jnp.concatenate([wide_sum[:heads], gains], axis=0)

time: 193 us -> 180 us (0.933)
  Pallas kernels: 191 us -> 179 us
    pallas_call x3, Pallas kernels: 191 us -> 179 us  [run(): pl.pallas_call(body, in_specs=[i[2] for i in ins], out_specs=[o[3] for o...]
where the time goes in v6:
time: 180 us; the launch traced here: 179 us
  Pallas kernels  179 us (99%)
    pallas_call x3, Pallas kernels, run(): pl.pallas_call(body, in_specs=[i[2] for i in ins], out_specs=[o[3] for o...  179 us

profile of v6, /device:TPU:0, one launch (start us, length us, event | category | flops | bytes accessed | tf_op | source)
XLA Modules:
  0.0 179.5 jit_solution(5273097397965597809)
XLA Ops:
  0.7 115.5 %forward.1 = (bf16[8,256,1152]{2,1,0:T(8,128)(2,1)}, bf16[8,6,256,256]{3,2,1,0:T(8,128)(2,1)}, bf16[8,256,768]{2,1,0:T(8,128)(2,1)}, bf16[8,256,384]{2,1,0:T(8,1...) custom-call(bf16[2000,768]{1,0:T(8,128)(2,1)} %refs_0_.1, ...), custom_call_target="tpu_custom_call" | custom-call | tf_op jit(solution)/shard_map/forward/pallas_call | solution.py:80
  116.1 52.7 %back.1 = (f32[8,256,768]{2,1,0:T(8,128)}, f32[8,768]{1,0:T(8,128)}, f32[32,768]{1,0:T(8,128)}, f32[48,512]{1,0:T(8,128)}, f32[32,768]{1,0:T(8,128)}, /*index=5*...) custom-call(bf16[8,256,384]{2,1,0:T(8,128)(2,1)} %get-tuple-element.76.refs_0_, ...), custom_call_target="tpu_custom_call" | custom-call | tf_op jit(solution)/shard_map/back/pallas_call | solution.py:80
  168.9 10.4 %update.1 = (f32[3,48,384]{2,1,0:T(8,128)}, f32[3,48,384]{2,1,0:T(8,128)}, f32[3,48,384]{2,1,0:T(8,128)}, bf16[3,48,384]{2,1,0:T(8,128)(2,1)}, f32[24,768]{1,0:T...) custom-call(f32[32,768]{1,0:T(8,128)} %get-tuple-element.75.refs_0_,, ...), custom_call_target="tpu_custom_call" | custom-call | tf_op jit(solution)/shard_map/update/pallas_call | solution.py:80

commit v7 on v6

--- a/solution.py
+++ b/solution.py
@@ -192,8 +192,8 @@
 
 
 class Gather:
-    def __init__(self, links, full, ss, rs):
-        self.l, self.full, self.ss, self.rs = links, full, ss, rs
+    def __init__(self, links, full, ss, rs, short=()):
+        self.l, self.full, self.ss, self.rs, self.short = links, full, ss, rs, short
 
     def at(self, a, blk):
         ref, rows, lanes = self.full[a]
@@ -224,14 +224,17 @@
 
     def across(self, a):
         l = self.l
-        for k in range(0, l.nz, 2):
-            role, source, target = (1, l.x_peer, l.y_peer) if k % 4 == 0 else (2, l.y_peer, l.x_peer)
+        for k in range(0, l.nz, 1 if a in self.short else 2):
+            over_x = k % 2 == 0 if a in self.short else k % 4 == 0
+            role, source, target = (1, l.x_peer, l.y_peer) if over_x else (2, l.y_peer, l.x_peer)
             blk = l.block(k, source)
             self.copy(a, role, k, blk, source).wait_recv()
             self.copy(a, 3, k, blk, target).start()
 
     def share(self, a):
         l = self.l
+        if a in self.short:
+            return
         for k in range(0, l.nz, 2):
             blk = l.block(k, l.far_peer)
             self.copy(a, 3, k, blk, l.x_peer).wait_recv()
@@ -240,6 +243,11 @@
     def arrived(self, a):
         l = self.l
         for k in range(l.nz):
+            if a in self.short:
+                role, source = (2, l.y_peer) if k % 2 == 0 else (1, l.x_peer)
+                self.copy(a, role, k, l.block(k, source), source).wait_recv()
+                self.copy(a, 3, k, l.block(k, l.far_peer), l.x_peer).wait_recv()
+                continue
             if k % 4 != 0:
                 self.copy(a, 1, k, l.block(k, l.x_peer), l.x_peer).wait_recv()
             if k % 4 != 2:
@@ -250,7 +258,7 @@
     def sent(self, a):
         l = self.l
         for k in range(l.nz):
-            roles = (0,) * (k > 0) + (1, 2) + (3, 4) * (k % 2 == 0)
+            roles = (0,) * (k > 0) + (1, 2) + ((3,) if a in self.short else (3, 4) * (k % 2 == 0))
             for role in roles:
                 self.copy(a, role, k, l.me, l.x_peer).wait_send()
 
@@ -495,7 +503,7 @@
         rows_o = r.wo_wide.shape[0] // n
         full = [(r.wi, r.wi.shape[0] // n, None), (r.wo_wide, rows_o, None)]
         full += [(w, w.shape[0] // n, None) for w in (r.we_a, r.wr_a, r.we_b, r.wr_b, r.we_c, r.wr_c)]
-        gather = Gather(links, full, r.g_ss, r.g_rs)
+        gather = Gather(links, full, r.g_ss, r.g_rs, (0, 1))
         grads = [(g, g.shape[0] // n) for g in (r.stage_ra, r.stage_ea, r.stage_rb, r.stage_eb)]
         kept = [r.sum_ra, r.sum_ea, r.sum_rb, r.sum_eb]
         sums = Scatter(links, grads, [r.buf_ra, r.buf_ea, r.buf_rb, r.buf_eb], r.s_ss, r.s_rs)
@@ -516,7 +524,6 @@
         gather.put(1, jnp.concatenate([r.own_o[...], pad], axis=0).astype(BF))
         greet(links.peers() + [partner()])
         gather.own(0)
-        gather.own(1)
         third = full[3][1]
         columns = [r.own_e[:, d * 3 * third : (d + 1) * 3 * third].astype(BF) for d in range(n)]
         for i in range(3):
@@ -528,21 +535,22 @@
     tok_move(0, half)
     if direct:
         gather.along(0)
-        gather.own(2)
+        gather.own(1)
     tok_move(half, passages)
     local(r.tok, r.tok_out, 0).start()
     cot_start()
     if direct:
         gather.across(0)
+        gather.share(0)
+    cot_move(0, half)
+    if direct:
         gather.along(1)
-    cot_move(0, half)
-    if direct:
-        gather.share(0)
         gather.across(1)
+        gather.own(2)
+    cot_move(half, passages)
+    if direct:
+        gather.share(1)
         gather.own(3)
-    cot_move(half, passages)
-    if direct:
-        gather.share(1)
     for h in range(heads):
         line = dot_exact(r.table[h : h + 1, :], r.onehot[...])
         rows = jnp.broadcast_to(line, (ROWS, 2 * ROWS))
@@ -749,15 +757,14 @@
     staged(stage_rc, stage_ec)
     local(stage_rc, r.grad_r, 3).start()
     local(stage_ec, r.grad_e, 4).start()
-    if direct:
-        for a, held in ((2, r.held_rb), (3, r.held_eb)):
-            held[0] = jnp.zeros(held.shape[1:], BF)
-            sums.along(a, kept[a], held)
     for p in range(count - LAG, count):
         finish(p)
         for stream in (layer, hidden_grad):
             stream.start(p)
     if direct:
+        for a, held in ((2, r.held_rb), (3, r.held_eb)):
+            held[0] = jnp.zeros(held.shape[1:], BF)
+            sums.along(a, kept[a], held)
         for a in range(2):
             sums.total(a, kept[a])
         for a in range(6):
@@ -1117,11 +1124,11 @@
     def passage(name, p, sem):
         return pltpu.make_async_copy(getattr(r, name).at[p], getattr(r, name + "_in").at[p], sem.at[p])
 
-    for k in keys:
-        fetch[k].start()
     for p in range(passages):
         passage("grad", p, r.grad_sem).start()
         passage("layer", p, r.layer_sem).start()
+    for k in keys:
+        fetch[k].start()
 
     def get(k):
         fetch[k].wait()
@@ -1142,6 +1149,19 @@
         for part in ("_nw", "_nm", "_nv") + ("_nc",) * (key not in "gt"):
             store(getattr(r, key + part + "_out"), getattr(r, key + part))
 
+    sent = 0
+    for p in range(passages):
+        at = slice(p * PLEN, (p + 1) * PLEN)
+        passage("grad", p, r.grad_sem).wait()
+        r.grad_rows[at] = r.grad_in[p, :PLEN]
+        passage("layer", p, r.layer_sem).wait()
+        r.layer_wide[at] = r.layer_in[p, :PLEN].astype(F32)
+        end = total if p == passages - 1 else (p + 1) * PLEN // 16 * 16
+        rows = slice(sent, end)
+        store(r.grad_rows.at[rows], r.input_grad.at[rows])
+        r.layer_rows[rows] = r.layer_wide[rows].astype(BF)
+        store(r.layer_rows.at[rows], r.layer_out.at[rows])
+        sent = end
     pieces_r, pieces_e = ([get(key + third) for third in "abc"] for key in "re")
     ready("r")
     third = pieces_r[0].shape[0]
@@ -1174,19 +1194,6 @@
         precision=lax.Precision.HIGHEST, preferred_element_type=F32,
     ))
     done("t")
-    sent = 0
-    for p in range(passages):
-        at = slice(p * PLEN, (p + 1) * PLEN)
-        passage("grad", p, r.grad_sem).wait()
-        r.grad_rows[at] = r.grad_in[p, :PLEN]
-        passage("layer", p, r.layer_sem).wait()
-        r.layer_wide[at] = r.layer_in[p, :PLEN].astype(F32)
-        end = total if p == passages - 1 else (p + 1) * PLEN // 16 * 16
-        rows = slice(sent, end)
-        store(r.grad_rows.at[rows], r.input_grad.at[rows])
-        r.layer_rows[rows] = r.layer_wide[rows].astype(BF)
-        store(r.layer_rows.at[rows], r.layer_out.at[rows])
-        sent = end
     for copy in stores:
         copy.wait()
 

time: 180 us -> 179 us (level)
  no operation moved by 1% of the time
where the time goes in v7:
time: 179 us
  Pallas kernels  178 us (99%)
    pallas_call x3, Pallas kernels, run(): pl.pallas_call(body, in_specs=[i[2] for i in ins], out_specs=[o[3] for o...  178 us

profile of v7, /device:TPU:0, one launch (start us, length us, event | category | flops | bytes accessed | tf_op | source)
XLA Modules:
  0.0 178.8 jit_solution(16240128740315360550)
XLA Ops:
  0.7 117.1 %forward.1 = (bf16[8,256,1152]{2,1,0:T(8,128)(2,1)}, bf16[8,6,256,256]{3,2,1,0:T(8,128)(2,1)}, bf16[8,256,768]{2,1,0:T(8,128)(2,1)}, bf16[8,256,384]{2,1,0:T(8,1...) custom-call(bf16[2000,768]{1,0:T(8,128)(2,1)} %refs_0_.1, ...), custom_call_target="tpu_custom_call" | custom-call | tf_op jit(solution)/shard_map/forward/pallas_call | solution.py:80
  117.8 50.8 %back.1 = (f32[8,256,768]{2,1,0:T(8,128)}, f32[8,768]{1,0:T(8,128)}, f32[32,768]{1,0:T(8,128)}, f32[48,512]{1,0:T(8,128)}, f32[32,768]{1,0:T(8,128)}, /*index=5*...) custom-call(bf16[8,256,384]{2,1,0:T(8,128)(2,1)} %get-tuple-element.76.refs_0_, ...), custom_call_target="tpu_custom_call" | custom-call | tf_op jit(solution)/shard_map/back/pallas_call | solution.py:80
  168.6 10.0 %update.1 = (f32[3,48,384]{2,1,0:T(8,128)}, f32[3,48,384]{2,1,0:T(8,128)}, f32[3,48,384]{2,1,0:T(8,128)}, bf16[3,48,384]{2,1,0:T(8,128)(2,1)}, f32[24,768]{1,0:T...) custom-call(f32[32,768]{1,0:T(8,128)} %get-tuple-element.75.refs_0_,, ...), custom_call_target="tpu_custom_call" | custom-call | tf_op jit(solution)/shard_map/update/pallas_call | solution.py:80
